TPU v7x, 128 devices: a whole 4x4x4 slice. The times are simulated.
128 devices in a mesh: row: 8 (over x, core), col: 8 (over y, z_lo), chan: 2 (over z_hi).
Axes of the slice: x: 4, y: 4, z: 4 (z_hi: 2, z_lo: 2; z = z_hi * 2 + z_lo), core: 2. Of those that a mesh axis runs over, the one named last changes fastest.
Arguments:
- visibility: bfloat16 [8, 2, 64, 8, 8, 4096], P(None, None, 'chan', 'row', 'col'), may hold values from -6 to 6
- flags: int32 [2, 64, 8, 8, 4096], P(None, 'chan', 'row', 'col'), may hold values 0 or 1
- coeffs: float32 [512, 512], P(('row', 'col')), may hold values from -4 to 4
- station_uv: float32 [2, 2, 512], replicated, may hold values from -100 to 100
- source_lm: float32 [2, 256], replicated, may hold values from -0.1 to 0.1
- source_flux: float32 [256, 64], replicated, may hold values from 0.05 to 0.5
- cluster_ids: int32 [256], replicated, may hold values from 0 to 7
Outputs:
- coef_grad: float32 [512, 512], P(('row', 'col'))
All inputs are finite; a program needn't handle non-finite values. No bound on the sum of `flags` on one device may be relied on, other than what follows from the above.
Results may differ from a plain program's by a relative error of at most 0.0003.
Values sent between devices are 32-bit elements; how exact they have to be, the bound alone decides.
No kernel may reach another device: no remote copies, remote signals or barrier semaphores. Data moves between devices by JAX's collectives and lax.ppermute only.
A program may use at most 128 MiB of HBM per device.

v0:
```python
import math

import jax
import jax.numpy as jnp
from jax import lax
from jax.sharding import PartitionSpec as P

S = 512
K = 8
F = 64
NB = 8
T_SMP = 2


two_pi = 2.0 * math.pi
dof_nu = 2.0


def bernstein(channel_index, nbasis):
    position = (channel_index.astype(jnp.float32) + 0.5) / F
    power = jnp.arange(nbasis).astype(jnp.float32)
    binomial = jnp.array([math.comb(nbasis - 1, degree) for degree in range(nbasis)], jnp.float32)
    return (
        binomial[None, :]
        * position[:, None] ** power[None, :]
        * (1.0 - position)[:, None] ** (nbasis - 1.0 - power)[None, :]
    )


def frequency(channel_index):
    return 1.0 + 0.5 * (channel_index.astype(jnp.float32) + 0.5) / F


def geometry(station_uv, source_lm):
    return (
        station_uv[0][:, :, None] * source_lm[0][None, None, :]
        + station_uv[1][:, :, None] * source_lm[1][None, None, :]
    )


def coherency(geom_row, geom_col, freq, weights):
    phase_row = two_pi * freq * geom_row
    phase_col = two_pi * freq * geom_col
    cos_row = jnp.cos(phase_row)
    sin_row = jnp.sin(phase_row)
    cos_col = jnp.cos(phase_col)
    sin_col = jnp.sin(phase_col)
    left_cos = weights[None, :, None, :] * cos_row[:, None, :, :]
    left_sin = weights[None, :, None, :] * sin_row[:, None, :, :]
    right_one = jnp.concatenate([cos_col, sin_col], axis=2)
    right_two = jnp.concatenate([sin_col, cos_col], axis=2)
    real_part = jnp.einsum(
        "tkps,tqs->tkpq",
        jnp.concatenate([left_cos, left_sin], axis=3),
        right_one,
        precision=lax.Precision.HIGHEST,
    )
    imag_part = jnp.einsum(
        "tkps,tqs->tkpq",
        jnp.concatenate([left_cos, -left_sin], axis=3),
        right_two,
        precision=lax.Precision.HIGHEST,
    )
    return (real_part, imag_part)


def jones_matrix(basis_row, coef_block):
    terms = jnp.einsum("b,pkbe->ekp", basis_row, coef_block, precision=lax.Precision.HIGHEST)
    identity = jnp.array([1.0, 0.0, 0.0, 0.0, 0.0, 0.0, 1.0, 0.0], jnp.float32)
    return terms + identity[:, None, None]


def channel_cost(jones_row, jones_col, real_part, imag_part, observed, weight_mask, scale):
    squared = None
    for row_pol in range(2):
        for col_pol in range(2):
            prod_re = 0.0
            prod_im = 0.0
            for shared in range(2):
                left_re = jones_row[2 * (2 * row_pol + shared)][:, :, None]
                left_im = jones_row[2 * (2 * row_pol + shared) + 1][:, :, None]
                right_re = jones_col[2 * (2 * col_pol + shared)][:, None, :]
                right_im = jones_col[2 * (2 * col_pol + shared) + 1][:, None, :]
                prod_re = prod_re + left_re * right_re + left_im * right_im
                prod_im = prod_im + left_im * right_re - left_re * right_im
            model_re = jnp.sum(real_part * prod_re[None] - imag_part * prod_im[None], axis=1)
            model_im = jnp.sum(real_part * prod_im[None] + imag_part * prod_re[None], axis=1)
            component = 2 * (2 * row_pol + col_pol)
            resid_re = observed[component] - model_re
            resid_im = observed[component + 1] - model_im
            part = resid_re * resid_re + resid_im * resid_im
            squared = part if squared is None else squared + part
    robust = weight_mask * ((dof_nu + 8.0) / 2.0) * jnp.log1p(squared / dof_nu)
    return jnp.sum(robust) * scale


def channel_gradient(jones_row, jones_col, real_part, imag_part, observed, weight_mask, scale):

    def cost_of(first, second):
        return channel_cost(first, second, real_part, imag_part, observed, weight_mask, scale)

    value, pullback = jax.vjp(cost_of, jones_row, jones_col)
    return pullback(jnp.ones_like(value))


def project_block(basis, grad_block):
    projected = jnp.einsum("fb,fekp->pkbe", basis, grad_block, precision=lax.Precision.HIGHEST)
    return projected.reshape(grad_block.shape[3], K * NB * 8)


def per_device(visibility, flags, coeffs, station_uv, source_lm, source_flux, cluster_ids):
    scale = 1.0 / math.sqrt(S * F * T_SMP)
    row_count = S // lax.axis_size("row")
    col_count = S // lax.axis_size("col")
    chan_count = visibility.shape[2]
    samples = visibility.shape[1]
    row_start = lax.axis_index("row") * row_count
    col_start = lax.axis_index("col") * col_count
    chan_start = lax.axis_index("chan") * chan_count
    coef_whole = lax.all_gather(coeffs, ("row", "col"), axis=0, tiled=True)
    coef_row = lax.dynamic_slice_in_dim(coef_whole, row_start, row_count, 0).reshape(
        row_count, K, NB, 8
    )
    coef_col = lax.dynamic_slice_in_dim(coef_whole, col_start, col_count, 0).reshape(
        col_count, K, NB, 8
    )
    basis = bernstein(chan_start + jnp.arange(chan_count), NB)
    geom_row = geometry(lax.dynamic_slice_in_dim(station_uv, row_start, row_count, 2), source_lm)
    geom_col = geometry(lax.dynamic_slice_in_dim(station_uv, col_start, col_count, 2), source_lm)
    onehot = (cluster_ids[None, :] == jnp.arange(K)[:, None]).astype(jnp.float32)

    def step(channel, carry):
        grad_row, grad_col = carry
        global_chan = chan_start + channel
        basis_row = lax.dynamic_index_in_dim(basis, channel, 0, False)
        freq = frequency(global_chan)
        flux_now = lax.dynamic_index_in_dim(source_flux, global_chan, 1, False)
        real_part, imag_part = coherency(geom_row, geom_col, freq, onehot * flux_now[None, :])
        observed = lax.dynamic_index_in_dim(visibility, channel, 2, False)
        observed = observed.reshape(8, samples, row_count, col_count).astype(jnp.float32)
        weight_mask = lax.dynamic_index_in_dim(flags, channel, 1, False)
        weight_mask = weight_mask.reshape(samples, row_count, col_count).astype(jnp.float32)
        jones_row = jones_matrix(basis_row, coef_row)
        jones_col = jones_matrix(basis_row, coef_col)
        part_row, part_col = channel_gradient(
            jones_row, jones_col, real_part, imag_part, observed, weight_mask, scale
        )
        grad_row = lax.dynamic_update_index_in_dim(grad_row, part_row, channel, 0)
        grad_col = lax.dynamic_update_index_in_dim(grad_col, part_col, channel, 0)
        return (grad_row, grad_col)

    start_row = jnp.zeros((chan_count, 8, K, row_count), jnp.float32)
    start_col = jnp.zeros((chan_count, 8, K, col_count), jnp.float32)
    grad_row, grad_col = lax.fori_loop(0, chan_count, step, (start_row, start_col))
    partial_value = jnp.zeros((chan_count, 8, K, S), jnp.float32)
    partial_value = lax.dynamic_update_slice_in_dim(partial_value, grad_row, row_start, 3)
    col_part = lax.dynamic_slice_in_dim(partial_value, col_start, col_count, 3) + grad_col
    partial_value = lax.dynamic_update_slice_in_dim(partial_value, col_part, col_start, 3)
    owned_jones = lax.psum_scatter(partial_value, ("row", "col"), scatter_dimension=3, tiled=True)
    owned = project_block(basis, owned_jones)
    return lax.psum(owned, "chan")


def solution(mesh):
    return jax.shard_map(
        per_device,
        mesh=mesh,
        in_specs=(
            P(None, None, "chan", "row", "col", None),
            P(None, "chan", "row", "col", None),
            P(("row", "col"), None),
            P(),
            P(),
            P(),
            P(),
        ),
        out_specs=P(("row", "col"), None),
        check_vma=False,
    )
```

profile of v0, /device:TPU:0, one launch (start us, length us, event | category | flops | bytes accessed | tf_op | source)
XLA Modules:
  0.0 1408.2 jit_solution(1437710409602909602)
XLA Ops:
  7.4 8.5 copy.26
  16.2 149.1 %all-gather.2.cloned.1.call-done = f32[512,512]{1,0:T(8,128)} async-done(((f32[8,512]{1,0:T(8,128)}), f32[512,512]{1,0:T(8,128)}) %all-gather.2.cloned.1.call-update) | async-done | bytes 1048592 | tf_op jit(solution)/shard_map/all_gather | solution.py:120
  166.5 834.5 %while.21 = (s32[]{:T(128)}, f32[32,8,8,64]{3,2,1,0:T(8,128)}, f32[32,8,8,64]{3,2,1,0:T(8,128)}, s32[]{:T(128)}, f32[256,64]{0,1:T(8,128)}, /*index=5*/bf16[8,2,...) while((s32[]{:T(128)}, f32[32,8,8,64]{3,2,1,0:T(8,128)}, ...), condition=%wide.region_89.90_spmd.clone.clone.clone.clone, body=%wide.region_0.89_spmd.sunk.clone.clone.clone.clone.sunk | while | flops 819023872 | bytes 22915536 | solution.py:154
  166.7 3.5 fusion.61
  170.9 3.5 fusion.62
  192.8 3.5 fusion.61
  196.9 3.5 fusion.62
  218.9 3.5 fusion.61
  223.0 3.5 fusion.62
  244.9 3.5 fusion.61
  249.1 3.5 fusion.62
  271.0 3.5 fusion.61
  275.2 3.5 fusion.62
  297.1 3.5 fusion.61
  301.2 3.5 fusion.62
  323.1 3.5 fusion.61
  327.3 3.5 fusion.62
  353.4 3.5 fusion.62
  375.3 3.5 fusion.61
  379.4 3.5 fusion.62
  401.4 3.5 fusion.61
  405.5 3.5 fusion.62
  431.6 3.5 fusion.62
  457.6 3.5 fusion.62
  483.7 3.5 fusion.62
  509.8 3.5 fusion.62
  535.9 3.5 fusion.62
  561.9 3.5 fusion.62
  588.0 3.5 fusion.62
  614.1 3.5 fusion.62
  640.2 3.5 fusion.62
  666.2 3.5 fusion.62
  692.3 3.5 fusion.62
  718.4 3.5 fusion.62
  744.5 3.5 fusion.62
  770.5 3.5 fusion.62
  796.6 3.5 fusion.62
  822.7 3.5 fusion.62
  848.7 3.5 fusion.62
  874.8 3.5 fusion.62
  900.9 3.5 fusion.62
  926.9 3.5 fusion.62
  953.0 3.5 fusion.62
  979.1 3.5 fusion.62
  1001.0 4.1 copy.28
  1008.1 7.9 broadcast_in_dim.266
  1020.8 366.8 %reduce-scatter.2.cloned.1.call-done = f32[32,8,8,8]{0,2,1,3:T(8,128)} async-done(((f32[32,8,8,512]{0,2,1,3:T(8,128)}), f32[32,8,8,8]{0,2,1,3:T(8,128)}) %reduce-scatter.2.cloned.1.call-update) | async-done | bytes 65552 | tf_op jit(solution)/shard_map/reduce_scatter | solution.py:159
  1389.5 11.8 psum.7
  (2264 shorter events, 692.2 us)
Async XLA Ops:
  6.5 158.7 %all-gather.2.cloned.1.call-start = ((), (), s32[]{:S(2)}) async-start(), calls=%async_computation.1 | async-start | bytes 1064960 | tf_op jit(solution)/shard_map/all_gather | solution.py:120
  7.3 1380.4 %reduce-scatter.2.cloned.1.call-start = ((), (), s32[]{:S(2)}) async-start(), calls=%async_computation.2 | async-start | bytes 17039360 | tf_op jit(solution)/shard_map/reduce_scatter | solution.py:159
  7.3 8.6 copy-start.7
  7.3 8.7 copy-start.8
  7.4 8.7 copy-start.6
  7.4 159.1 %copy-start.4 = (s32[256]{0:T(256)S(1)}, s32[256]{0:T(256)}, u32[]{:S(2)}) copy-start(s32[256]{0:T(256)} %param.18) | copy-start | bytes 3076
  7.4 159.1 %copy-start.5 = (f32[8]{0:T(128)S(1)}, f32[8]{0:T(128)}, u32[]{:S(2)}) copy-start(f32[8]{0:T(128)} %constant.174.clone..sunk.7) | copy-start | bytes 100
  178.8 1.9 copy-start.1
  178.8 1.9 copy-start.2
  178.8 1.9 copy-start.3
  230.9 1.9 copy-start.1
  230.9 1.9 copy-start.2
  230.9 1.9 copy-start.3
  257.0 1.9 copy-start.1
  257.0 1.9 copy-start.2
  257.0 1.9 copy-start.3
  335.2 1.9 copy-start.1
  335.2 1.9 copy-start.2
  335.2 1.9 copy-start.3
  387.3 1.9 copy-start.1
  387.3 1.9 copy-start.2
  387.3 1.9 copy-start.3
  439.5 1.9 copy-start.1
  439.5 1.9 copy-start.2
  439.5 1.9 copy-start.3
  465.5 1.9 copy-start.1
  465.6 1.9 copy-start.2
  465.6 1.9 copy-start.3
  491.6 1.9 copy-start.1
  491.6 1.9 copy-start.2
  491.6 1.9 copy-start.3
  569.8 1.9 copy-start.1
  569.8 1.9 copy-start.2
  569.9 1.9 copy-start.3
  595.9 1.9 copy-start.1
  595.9 1.9 copy-start.2
  595.9 1.9 copy-start.3
  674.1 1.9 copy-start.1
  674.1 1.9 copy-start.2
  674.2 1.9 copy-start.3
  752.4 1.9 copy-start.1
  752.4 1.9 copy-start.2
  752.4 1.9 copy-start.3
  778.4 1.9 copy-start.1
  934.8 1.9 copy-start.1
  934.9 1.9 copy-start.2
  934.9 1.9 copy-start.3
  1008.1 7.9 copy-start
  (56 other events, 106.6 us)
Sparse Core Ops, SparseCore 0:
  9.0 156.1 all-gather.1
  1020.9 366.6 reduce-scatter.1
where the time goes:
time: 1410 us
  waiting for transfers between devices  517 us (37%)
  matrix products  364 us (26%)
  other arithmetic  341 us (24%)
  local copies, waits for them, and re-layouts  149 us (11%)
    reduce_scatter x1, waiting for transfers between devices, per_device(): lax.psum_scatter(partial_value, ('row', 'col'), scatter_dimension=3, tile...  367 us
    dot_general x64, matrix products, jones_matrix(): jnp.einsum('b,pkbe->ekp', basis_row, coef_block, precision=lax.Precision....  222 us
    all_gather x1, waiting for transfers between devices, per_device(): coef_whole = lax.all_gather(coeffs, ('row', 'col'), axis=0, tiled=True)  149 us
    reduce_sum x64, other arithmetic, channel_cost(): prod_im = prod_im + left_im * right_re - left_re * right_im  127 us
    dot_general x32, matrix products, coherency(): jnp.einsum('tkps,tqs->tkpq', jnp.concatenate([left_cos, -left_sin], axis=...  80.6 us
    dot_general x32, matrix products, coherency(): jnp.einsum('tkps,tqs->tkpq', jnp.concatenate([left_cos, left_sin], axis=3...  59.8 us
    sub x32, other arithmetic, channel_cost(): prod_im = prod_im + left_im * right_re - left_re * right_im  50.1 us
    dot_general x64, local copies, waits for them, and re-layouts, jones_matrix(): jnp.einsum('b,pkbe->ekp', basis_row, coef_block, precision=lax.Precision....  43.3 us
  transfers between devices with their start and end apart: 2, of which 2 were waited for; matrix products, arithmetic and copies ran while one was open for 1% of the time, Pallas kernels for 0%

commit v1 on v0

v1 whole, which is shorter than its diff:
```python
import math

import jax
import jax.numpy as jnp
from jax import lax
from jax.experimental import pallas as pl
from jax.experimental.pallas import tpu as pltpu
from jax.sharding import PartitionSpec as P

S = 512
K = 8
F = 64
NB = 8
NSRC = 256
T_SMP = 2
RB = 64

f32 = jnp.float32
bf16 = jnp.bfloat16

SIN_TERMS = [(-1) ** n * math.pi ** (2 * n + 1) / math.factorial(2 * n + 1) for n in range(8)]
COS_TERMS = [(-1) ** n * math.pi ** (2 * n) / math.factorial(2 * n) for n in range(8)]


def bernstein(channel_index, nbasis):
    position = (channel_index.astype(f32) + 0.5) / F
    power = jnp.arange(nbasis).astype(f32)
    binomial = jnp.array([math.comb(nbasis - 1, degree) for degree in range(nbasis)], f32)
    return (
        binomial[None, :]
        * position[:, None] ** power[None, :]
        * (1.0 - position)[:, None] ** (nbasis - 1.0 - power)[None, :]
    )


def frequency(channel_index):
    return 1.0 + 0.5 * (channel_index.astype(f32) + 0.5) / F


def horner(terms, y):
    total = terms[-1]
    for term in terms[-2::-1]:
        total = total * y + term
    return total


def phasors(turns):
    r = turns - jnp.round(turns)
    y = r * r
    half_sin = r * horner(SIN_TERMS, y)
    half_cos = horner(COS_TERMS, y)
    return 1.0 - 2.0 * half_sin * half_sin, -2.0 * half_sin * half_cos


def split(x):
    high = x.astype(bf16)
    return high, (x - high.astype(f32)).astype(bf16)


def dot_nn(a, b):
    return lax.dot_general(a, b, (((1,), (0,)), ((), ())), preferred_element_type=f32)


def dot_nt(a, b):
    return lax.dot_general(a, b, (((1,), (1,)), ((), ())), preferred_element_type=f32)


def kernel(basis_ref, ids_ref, hot_ref, coef_ref, ec_ref, es_ref, vis_ref, flag_ref, out_ref,
           ct_ref, jg_ref, xh_ref, xl_ref, bh_ref, bl_ref, d_ref, acc_ref, turn_ref, pair_ref):
    step = pl.program_id(0)
    chans = pl.num_programs(0)
    odd = lax.broadcasted_iota(jnp.int32, (32, 128), 1) >= 64

    @pl.when(step == 0)
    def _():
        acc_ref[...] = jnp.zeros_like(acc_ref)
        for part in range(4):
            lanes = slice(part * 128, (part + 1) * 128)
            pair_ref[part] = coef_ref[0, :, lanes]
            ct_ref[lanes, :] = jnp.concatenate(
                [
                    pair_ref[part, pl.ds(0, 32, stride=2), :],
                    pair_ref[part, pl.ds(1, 32, stride=2), :],
                    coef_ref[1, :, lanes],
                ],
                axis=0,
            ).T

    element = lax.broadcasted_iota(jnp.int32, (8, 128), 0)
    identity = jnp.where((element == 0) | (element == 6), 1.0, 0.0).astype(f32)
    rows = []
    for k in range(K):
        total = identity
        for b in range(NB):
            total = total + basis_ref[step, b] * ct_ref[k * 64 + b * 8:k * 64 + b * 8 + 8, :]
        rows.append(total)
    jones = jnp.concatenate(rows + rows, axis=0).T
    halves = [jnp.broadcast_to(ids_ref[0:1, h * 128:(h + 1) * 128], (RB, 128)) for h in range(2)]
    for side in range(2):
        for e in range(8):
            for h in range(2):
                jg_ref[side, e, :, h * 128:(h + 1) * 128] = jnp.take_along_axis(
                    jones[side * RB:(side + 1) * RB], halves[h] + e, axis=1, mode="promise_in_bounds"
                )

    lane_row = step % 8
    for t in range(T_SMP):
        for side in range(2):
            er = ec_ref[0, t, side]
            ei = es_ref[0, t, side]
            high_ref, low_ref = (xh_ref, xl_ref) if side == 0 else (bh_ref, bl_ref)
            for i in range(2):
                for j in range(2):
                    jr = jg_ref[side, 2 * (2 * i + j)]
                    ji = jg_ref[side, 2 * (2 * i + j) + 1]
                    re = split(jr * er - ji * ei)
                    im = split(jr * ei + ji * er)
                    first = slice(i * RB, (i + 1) * RB)
                    second = slice(128 + i * RB, 128 + (i + 1) * RB)
                    left = slice(j * 256, (j + 1) * 256)
                    right = slice(512 + j * 256, 512 + (j + 1) * 256)
                    for ref, a, b in zip((high_ref, low_ref), re, im):
                        ref[t, first, left] = a
                        ref[t, first, right] = b
                        if side == 0:
                            ref[t, second, left] = b
                            ref[t, second, right] = -a
                        else:
                            ref[t, second, left] = -b
                            ref[t, second, right] = a
        x_high, x_low = xh_ref[t, 0:128], xl_ref[t, 0:128]
        b_high, b_low = bh_ref[t], bl_ref[t]
        model = dot_nt(x_high, b_high) + dot_nt(x_low, b_high) + dot_nt(x_high, b_low)
        observed = []
        for i in range(2):
            columns = []
            for c in range(2):
                one = vis_ref[4 * i + c, t, 0, pl.ds(lane_row, 32, stride=8), :]
                two = vis_ref[4 * i + 2 + c, t, 0, pl.ds(lane_row, 32, stride=8), :]
                columns.append((
                    jnp.where(odd, pltpu.roll(two, 64, 1), one),
                    jnp.where(odd, two, pltpu.roll(one, 64, 1)),
                ))
            observed.append(jnp.concatenate(
                [jnp.concatenate([columns[0][h], columns[1][h]], axis=1) for h in range(2)], axis=0
            ))
        resid = model - jnp.concatenate(observed, axis=0)
        square = resid * resid
        square = square[0:64] + square[64:128]
        square = square[:, 0:128] + square[:, 128:256]
        square = square + pltpu.roll(square, 64, 1)
        flag = flag_ref[t, 0].astype(f32)
        other = pltpu.roll(flag, 64, 1)
        flag = jnp.concatenate([jnp.where(odd, other, flag), jnp.where(odd, flag, other)], axis=0)
        weight = flag / (2.0 + square)
        weight = jnp.concatenate([weight, weight], axis=0)
        g_re = resid[:, 0:128] * weight
        g_im = resid[:, 128:256] * weight
        for side in range(2):
            if side == 0:
                g_high, g_low = split(jnp.concatenate([g_re, g_im], axis=1))
                m_high, m_low = bh_ref, bl_ref
            else:
                g_high, g_low = split(jnp.concatenate([g_re.T, g_im.T], axis=1))
                m_high, m_low = xh_ref, xl_ref
            er = ec_ref[0, t, side]
            ei = es_ref[0, t, side]
            for j in range(2):
                parts = []
                for c in range(2):
                    cols = slice(c * 512 + j * 256, c * 512 + (j + 1) * 256)
                    w_high = m_high[t, :, cols]
                    w_low = m_low[t, :, cols]
                    parts.append(dot_nn(g_high, w_high) + dot_nn(g_low, w_high) + dot_nn(g_high, w_low))
                for i in range(2):
                    dr = parts[0][i * RB:(i + 1) * RB]
                    di = parts[1][i * RB:(i + 1) * RB]
                    e = 2 * (2 * i + j)
                    jr = dr * er + di * ei
                    ji = di * er - dr * ei
                    if t == 0:
                        d_ref[side, e * RB:(e + 1) * RB] = jr
                        d_ref[side, (e + 1) * RB:(e + 2) * RB] = ji
                    else:
                        d_ref[side, e * RB:(e + 1) * RB] += jr
                        d_ref[side, (e + 1) * RB:(e + 2) * RB] += ji

    for side in range(2):
        d_high, d_low = split(d_ref[side])
        summed = (dot_nt(hot_ref[...], d_high) + dot_nt(hot_ref[...], d_low))[0:8]
        for b in range(NB):
            acc_ref[b, side] += basis_ref[step, b] * summed

    @pl.when(step == chans - 1)
    def _():
        for b in range(NB):
            for e in range(8):
                turn_ref[pl.ds(b * 8 + e, 8, stride=64), :] = jnp.concatenate(
                    [acc_ref[b, side, :, e * RB:(e + 1) * RB] for side in range(2)], axis=1
                )
        turned = turn_ref[...].T
        out_ref[1] = turned[64:128]
        for part in range(4):
            lanes = slice(part * 128, (part + 1) * 128)
            pair_ref[part, pl.ds(0, 32, stride=2), :] = turned[0:32, lanes]
            pair_ref[part, pl.ds(1, 32, stride=2), :] = turned[32:64, lanes]
            out_ref[0, :, lanes] = pair_ref[part]


def gradient_call(basis, ids, hot, coef, ec, es, vis, flag):
    chans = ec.shape[0]
    const = lambda shape: pl.BlockSpec(shape, lambda f: (0,) * len(shape))
    return pl.pallas_call(
        kernel,
        grid=(chans,),
        in_specs=[
            pl.BlockSpec(memory_space=pltpu.SMEM),
            const((8, NSRC)),
            const((16, NSRC)),
            const((2, RB, 512)),
            pl.BlockSpec((1, T_SMP, 2, RB, NSRC), lambda f: (f, 0, 0, 0, 0)),
            pl.BlockSpec((1, T_SMP, 2, RB, NSRC), lambda f: (f, 0, 0, 0, 0)),
            pl.BlockSpec((8, T_SMP, 1, 256, 128), lambda f: (0, 0, f // 8, 0, 0)),
            pl.BlockSpec((T_SMP, 1, 32, 128), lambda f: (0, f, 0, 0)),
        ],
        out_specs=const((2, RB, 512)),
        out_shape=jax.ShapeDtypeStruct((2, RB, 512), f32),
        scratch_shapes=[
            pltpu.VMEM((512, 128), f32),
            pltpu.VMEM((2, 8, RB, NSRC), f32),
            pltpu.VMEM((T_SMP, 256, 1024), bf16),
            pltpu.VMEM((T_SMP, 256, 1024), bf16),
            pltpu.VMEM((T_SMP, 256, 1024), bf16),
            pltpu.VMEM((T_SMP, 256, 1024), bf16),
            pltpu.VMEM((2, 512, NSRC), f32),
            pltpu.VMEM((NB, 2, K, 512), f32),
            pltpu.VMEM((512, 128), f32),
            pltpu.VMEM((4, RB, 128), f32),
        ],
        compiler_params=pltpu.CompilerParams(
            dimension_semantics=("arbitrary",), vmem_limit_bytes=40 * 1024 * 1024
        ),
        cost_estimate=pl.CostEstimate(
            flops=2 * 3 * 6 * 128 * 1024 * 256 * T_SMP * chans, bytes_accessed=24 * 1024 * 1024, transcendentals=0
        ),
        name="robust_gradient",
    )(basis, ids, hot, coef, ec, es, vis, flag)


CROSS = [(r * 8 + c, c * 8 + r) for r in range(8) for c in range(8)]


def gather_block(own):
    col = lax.axis_index("col")
    held = own
    for bit in (1, 2, 4):
        other = lax.ppermute(held, "col", [(c, c ^ bit) for c in range(8)])
        upper = (col & bit) != 0
        held = jnp.concatenate([jnp.where(upper, other, held), jnp.where(upper, held, other)], axis=0)
    return held


def per_device(visibility, flags, coeffs, station_uv, source_lm, source_flux, cluster_ids):
    scale = 1.0 / math.sqrt(S * F * T_SMP)
    chans = visibility.shape[2]
    row = lax.axis_index("row")
    col = lax.axis_index("col")
    chan_start = lax.axis_index("chan") * chans
    channels = chan_start + jnp.arange(chans)

    row_coef = gather_block(coeffs)
    col_coef = lax.ppermute(row_coef, ("row", "col"), CROSS)
    coef = jnp.stack([row_coef, col_coef])

    basis = bernstein(channels, NB)
    row_uv = lax.dynamic_slice_in_dim(station_uv, row * RB, RB, 2)
    row_uv = row_uv.reshape(2, T_SMP, 32, 2).transpose(0, 1, 3, 2).reshape(2, T_SMP, RB)
    col_uv = lax.dynamic_slice_in_dim(station_uv, col * RB, RB, 2)
    uv = jnp.stack([row_uv, col_uv], axis=2)
    geo = uv[0][..., None] * source_lm[0] + uv[1][..., None] * source_lm[1]
    turns = frequency(channels)[:, None, None, None, None] * geo[None]
    flux = lax.dynamic_slice_in_dim(source_flux, chan_start, chans, 1).T
    amplitude = jnp.stack([flux, jnp.ones_like(flux)], axis=1)[:, None, :, None, :]
    cosine, sine = phasors(turns)
    ids = jnp.broadcast_to(cluster_ids[None] * 8, (8, NSRC))
    hot = (cluster_ids[None] == jnp.arange(16)[:, None]).astype(bf16)

    vis = visibility.astype(f32).reshape(8, T_SMP, chans // 8, 8, 32, 128)
    vis = vis.transpose(0, 1, 2, 4, 3, 5).reshape(8, T_SMP, chans // 8, 256, 128)
    flag = flags.reshape(T_SMP, chans, 32, 128)

    grad = gradient_call(basis, ids, hot, coef, cosine * amplitude, sine * amplitude, vis, flag)
    row_part = grad[0].reshape(8, 8, 512)
    col_part = lax.ppermute(grad[1], ("row", "col"), CROSS).reshape(8, 8, 512)
    both = jnp.concatenate([row_part, col_part], axis=1)
    both = lax.all_to_all(both, "col", 0, 0, tiled=True)
    total = both.reshape(16, 8, 512).sum(0) * (10.0 * scale)
    return total + lax.ppermute(total, "chan", [(0, 1), (1, 0)])


def solution(mesh):
    return jax.shard_map(
        per_device,
        mesh=mesh,
        in_specs=(
            P(None, None, "chan", "row", "col", None),
            P(None, "chan", "row", "col", None),
            P(("row", "col"), None),
            P(),
            P(),
            P(),
            P(),
        ),
        out_specs=P(("row", "col"), None),
        check_vma=False,
    )
```

time: 1410 us -> 207 us (0.15)
  waiting for transfers between devices: 517 us -> 6.61 us
  matrix products: 364 us -> 0 us
  other arithmetic: 341 us -> 20.7 us
  local copies, waits for them, and re-layouts: 149 us -> 5.38 us
  Pallas kernels: 0 us -> 126 us
  blocking collectives: 11.8 us -> 35.9 us
    reduce_scatter x1 -> x0, waiting for transfers between devices: 367 us -> none  [per_device(): lax.psum_scatter(partial_value, ('row', 'col'), scatter_dimension=3, tile...]
    dot_general x129 -> x0, matrix products: 364 us -> none  [the longest x64 222 us: jones_matrix(): jnp.einsum('b,pkbe->ekp', basis_row, coef_block, precision=lax.Precision....]
    reduce_sum x96 -> x1, other arithmetic: 159 us -> 0.02 us  [per_device(): total = both.reshape(16, 8, 512).sum(0) * (10.0 * scale)]
    all_gather x1 -> x0, waiting for transfers between devices: 149 us -> none  [per_device(): coef_whole = lax.all_gather(coeffs, ('row', 'col'), axis=0, tiled=True)]
    pallas_call x0 -> x1, Pallas kernels: none -> 126 us  [gradient_call(): pl.pallas_call(kernel, grid=(chans,), in_specs=[pl.BlockSpec(memory_space...]
    sub x32 -> x0, other arithmetic: 50.1 us -> none  [channel_cost(): prod_im = prod_im + left_im * right_re - left_re * right_im]
    dynamic_slice x67 -> x1, local copies, waits for them, and re-layouts: 48.2 us -> 0.84 us  [per_device(): row_uv = lax.dynamic_slice_in_dim(station_uv, row * RB, RB, 2)]
    dot_general x64 -> x0, local copies, waits for them, and re-layouts: 43.3 us -> none  [jones_matrix(): jnp.einsum('b,pkbe->ekp', basis_row, coef_block, precision=lax.Precision....]
  transfers between devices with their start and end apart: 2 -> 6, of which waited for: 2 -> 3; matrix products, arithmetic and copies ran while one was open for 1% -> 11% of each run, Pallas kernels for 0% -> 0%
where the time goes in v1:
time: 207 us
  Pallas kernels  126 us (61%)
  blocking collectives  35.9 us (17%)
  other arithmetic  20.7 us (10%)
  starting transfers between devices  12.4 us (6%)
  waiting for transfers between devices  6.61 us (3%)
  local copies, waits for them, and re-layouts  5.38 us (3%)
    pallas_call x1, Pallas kernels, gradient_call(): pl.pallas_call(kernel, grid=(chans,), in_specs=[pl.BlockSpec(memory_space...  126 us
    all_to_all x1, blocking collectives, per_device(): both = lax.all_to_all(both, 'col', 0, 0, tiled=True)  35.9 us
    mul x1, other arithmetic, per_device(): sine * amplitude  13.2 us
    ppermute x3, starting transfers between devices, gather_block(): other = lax.ppermute(held, 'col', [(c, c ^ bit) for c in range(8)])  6.81 us
    reshape x1, other arithmetic, per_device(): vis.transpose(0, 1, 2, 4, 3, 5).reshape(8, T_SMP, chans // 8, 256, 128)  6.51 us
    ppermute x3, waiting for transfers between devices, gather_block(): other = lax.ppermute(held, 'col', [(c, c ^ bit) for c in range(8)])  4.89 us
    ppermute x1, starting transfers between devices, per_device(): return total + lax.ppermute(total, 'chan', [(0, 1), (1, 0)])  4.25 us
  transfers between devices with their start and end apart: 6, of which 3 were waited for; matrix products, arithmetic and copies ran while one was open for 11% of the time, Pallas kernels for 0%

profile of v1, /device:TPU:0, one launch (start us, length us, event | category | flops | bytes accessed | tf_op | source)
XLA Modules:
  0.0 207.1 jit_solution(6041572683258012661)
XLA Ops:
  0.0 0.0 copy-start
  0.0 2.0 collective-permute-start
  2.0 0.8 constant_dynamic-slice_fusion
  2.9 0.1 reshape.58
  3.0 0.1 copy.16
  3.1 0.1 stack_reshape.3
  3.2 0.8 fusion.12
  3.9 0.0 copy-done
  4.0 6.5 %convert_bitcast_fusion.vis_ref = f32[8,2,4,256,128]{4,3,2,1,0:T(8,128)} fusion(bf16[8,2,32,1,1,4096]{5,2,4,3,1,0:T(8,128)(2,1)} %param.8), kind=kLoop, calls=%fused_computation.4 | loop fusion | flops 2097152 | bytes 12582912 | tf_op jit(solution)/shard_map/reshape | solution.py:289
  10.5 0.1 multiply_add_fusion
  10.7 0.0 copy-start.3
  10.7 0.0 copy-start.5
  10.7 0.0 copy-start.4
  10.7 0.0 copy-start.2
  10.7 13.2 %multiply_multiply_fusion.1 = (f32[32,2,2,64,256]{4,3,2,1,0:T(8,128)}, f32[32,2,2,64,256]{4,3,2,1,0:T(8,128)}) fusion(f32[32,2,256]{2,1,0:T(2,128)S(1)} %stack.27.clone, f32[2,2,64,256]{3,2,1,0:T(8,128)S(1)} %multiply_add_fusion, f32[32]{0:T(128)S(1)} %multiply_add_fusion.1), kind=kLoop, calls=%fused_computation.5 | loop fusion | flops 83886080 | bytes 17105024 | tf_op jit(solution)/shard_map/mul | solution.py:292
  23.9 0.0 collective-permute-done
  23.9 0.0 copy-done.3
  23.9 1.6 collective-permute-start.1
  25.5 0.0 copy-done.5
  25.5 0.1 power_multiply_fusion.basis_ref
  25.6 2.3 %collective-permute-done.1 = f32[16,512]{1,0:T(8,128)S(1)} collective-permute-done((f32[16,512]{1,0:T(8,128)S(1)}, f32[16,512]{1,0:T(8,128)S(1)}, u32[]{:S(2)}, u32[]{:S(2)}) %collective-permute-start.1) | collective-permute-done | bytes 32800 | tf_op jit(solution)/shard_map/ppermute | solution.py:257
  27.9 3.2 %collective-permute-start.2 = (f32[32,512]{1,0:T(8,128)S(1)}, f32[32,512]{1,0:T(8,128)S(1)}, u32[]{:S(2)}, u32[]{:S(2)}) collective-permute-start(f32[32,512]{1,0:T(8,128)S(1)} %pad_maximum_fusion.3), channel_id=1, source_target_pairs={{0,8},{2,10},{4,12},{6,14},{8,0},{10,2},{12,4},{14,6},{1,9},{3,11}... | collective-permute-start | bytes 196616 | tf_op jit(solution)/shard_map/ppermute | solution.py:257
  31.2 0.0 copy-done.4
  31.2 2.6 %collective-permute-done.2 = f32[32,512]{1,0:T(8,128)S(1)} collective-permute-done((f32[32,512]{1,0:T(8,128)S(1)}, f32[32,512]{1,0:T(8,128)S(1)}, u32[]{:S(2)}, u32[]{:S(2)}) %collective-permute-start.2) | collective-permute-done | bytes 65568 | tf_op jit(solution)/shard_map/ppermute | solution.py:257
  33.8 0.7 collective-permute-start.3
  34.5 0.0 collective-permute-done.3
  34.6 0.0 copy-done.2
  34.6 0.0 copy-start.1
  34.6 3.4 %copy-done.1 = f32[32,2,2,64,256]{4,3,2,1,0:T(8,128)S(1)} copy-done((f32[32,2,2,64,256]{4,3,2,1,0:T(8,128)S(1)}, f32[32,2,2,64,256]{4,3,2,1,0:T(8,128)}, u32[]{:S(2)}) %copy-start.1) | copy-done | bytes 8388632
  38.0 125.9 %robust_gradient.1 = f32[2,64,512]{2,1,0:T(8,128)S(1)} custom-call(f32[32,8]{1,0:T(8,128)S(1)} %power_multiply_fusion.basis_ref, s32[8,256]{1,0:T(8,128)S(1)} %broadcast_in_dim.2.ids_ref, bf16[16,256]{1,0:T(8,128)(2,1)S(1)} %fusion.7.hot_ref, f32[2,64,512]{2,1,0:T(8,128)S(1)} %pad_maximum_fusion.coef_ref, f32[32,2,2,64,256]{4,3,2,1,0:T(8,128)S(1)} %copy-done.1, ...), custom_call_target="tpu_custom_call" | custom-call | flops 77309411328 | bytes 25165824 | tf_op jit(solution)/shard_map/robust_gradient/pallas_call | solution.py:213
  163.9 0.7 collective-permute-start.4
  164.6 0.0 collective-permute-done.4
  164.6 35.9 %all_to_all.5 = f32[8,16,512]{2,1,0:T(8,128)S(1)} all-to-all(f32[8,16,512]{2,1,0:T(8,128)S(1)} %pad_maximum_fusion.1), channel_id=1, replica_groups=mesh['row'=8,'col'=8,'chan'=2] {'col'}, dimensions={0} | all-to-all | bytes 524288 | tf_op jit(solution)/shard_map/all_to_all | solution.py:296
  200.5 4.2 %collective-permute-start.5 = (f32[8,512]{1,0:T(8,128)S(1)}, f32[8,512]{1,0:T(8,128)S(1)}, u32[]{:S(2)}, u32[]{:S(2)}) collective-permute-start(f32[8,512]{1,0:T(8,128)S(1)} %broadcast_multiply_fusion), channel_id=1, source_target_pairs={{0,1},{1,0},{2,3},{3,2},{4,5},{5,4},{6,7},{7,6},{8,9},{9,8},{10,11... | collective-permute-start | bytes 49160 | tf_op jit(solution)/shard_map/ppermute | solution.py:298
  204.8 1.7 collective-permute-done.5
  206.5 0.6 fusion.10
  (23 shorter events, 0.3 us)
Async XLA Ops:
  0.0 3.9 %copy-start = (f32[256,64]{0,1:T(8,128)S(1)}, f32[256,64]{0,1:T(8,128)}, u32[]{:S(2)}) copy-start(f32[256,64]{0,1:T(8,128)} %param.13) | copy-start | bytes 196612
  0.0 23.9 %collective-permute-start = (f32[8,512]{1,0:T(8,128)}, f32[8,512]{1,0:T(8,128)S(1)}, u32[]{:S(2)}, u32[]{:S(2)}) collective-permute-start(f32[8,512]{1,0:T(8,128)} %param.10), channel_id=1, source_target_pairs={{0,2},{2,0},{4,6},{6,4},{8,10},{10,8},{12,14},{14,12},{1,3},{3,1},... | collective-permute-start | bytes 49160 | tf_op jit(solution)/shard_map/ppermute | solution.py:257
  10.7 13.2 %copy-start.3 = (f32[8,512]{1,0:T(8,128)S(1)}, f32[8,512]{1,0:T(8,128)}, u32[]{:S(2)}) copy-start(f32[8,512]{1,0:T(8,128)} %param.10) | copy-start | bytes 49156
  10.7 14.8 %copy-start.5 = (f32[8]{0:T(128)S(1)}, f32[8]{0:T(128)}, u32[]{:S(2)}) copy-start(f32[8]{0:T(128)} %constant.82.clone) | copy-start | bytes 100
  10.7 20.5 %copy-start.4 = (s32[256]{0:T(256)S(1)}, s32[256]{0:T(256)}, u32[]{:S(2)}) copy-start(s32[256]{0:T(256)} %param.14) | copy-start | bytes 3076
  10.7 23.9 %copy-start.2 = (s32[2,32,1,1,4096]{4,3,2,1,0:T(1,128)S(1)}, s32[2,32,1,1,4096]{4,3,2,1,0:T(1,128)}, u32[]{:S(2)}) copy-start(s32[2,32,1,1,4096]{4,3,2,1,0:T(1,128)} %param.9) | copy-start | bytes 3145732
  23.9 4.0 %collective-permute-start.1 = (f32[16,512]{1,0:T(8,128)S(1)}, f32[16,512]{1,0:T(8,128)S(1)}, u32[]{:S(2)}, u32[]{:S(2)}) collective-permute-start(f32[16,512]{1,0:T(8,128)S(1)} %pad_maximum_fusion.4), channel_id=1, source_target_pairs={{0,4},{2,6},{4,0},{6,2},{8,12},{10,14},{12,8},{14,10},{1,5},{3,7},... | collective-permute-start | bytes 98312 | tf_op jit(solution)/shard_map/ppermute | solution.py:257
  27.9 5.8 %collective-permute-start.2 = (f32[32,512]{1,0:T(8,128)S(1)}, f32[32,512]{1,0:T(8,128)S(1)}, u32[]{:S(2)}, u32[]{:S(2)}) collective-permute-start(f32[32,512]{1,0:T(8,128)S(1)} %pad_maximum_fusion.3), channel_id=1, source_target_pairs={{0,8},{2,10},{4,12},{6,14},{8,0},{10,2},{12,4},{14,6},{1,9},{3,11}... | collective-permute-start | bytes 196616 | tf_op jit(solution)/shard_map/ppermute | solution.py:257
  33.8 0.7 collective-permute-start.3
  34.6 3.4 %copy-start.1 = (f32[32,2,2,64,256]{4,3,2,1,0:T(8,128)S(1)}, f32[32,2,2,64,256]{4,3,2,1,0:T(8,128)}, u32[]{:S(2)}) copy-start(f32[32,2,2,64,256]{4,3,2,1,0:T(8,128)} %get-tuple-element.6.ec_ref) | copy-start | bytes 25165828
  163.9 0.7 collective-permute-start.4
  200.5 6.0 %collective-permute-start.5 = (f32[8,512]{1,0:T(8,128)S(1)}, f32[8,512]{1,0:T(8,128)S(1)}, u32[]{:S(2)}, u32[]{:S(2)}) collective-permute-start(f32[8,512]{1,0:T(8,128)S(1)} %broadcast_multiply_fusion), channel_id=1, source_target_pairs={{0,1},{1,0},{2,3},{3,2},{4,5},{5,4},{6,7},{7,6},{8,9},{9,8},{10,11... | collective-permute-start | bytes 49160 | tf_op jit(solution)/shard_map/ppermute | solution.py:298

commit v2 on v1

v2 whole, which is shorter than its diff:
```python
import math

import jax
import jax.numpy as jnp
from jax import lax
from jax.experimental import pallas as pl
from jax.experimental.pallas import tpu as pltpu
from jax.sharding import PartitionSpec as P

S = 512
K = 8
F = 64
NB = 8
NSRC = 256
T_SMP = 2
RB = 64
SCALE = 10.0 / math.sqrt(S * F * T_SMP)

f32 = jnp.float32
bf16 = jnp.bfloat16

SIN_TERMS = [(-1) ** n * math.pi ** (2 * n + 1) / math.factorial(2 * n + 1) for n in range(8)]
COS_TERMS = [(-1) ** n * math.pi ** (2 * n) / math.factorial(2 * n) for n in range(8)]


def bernstein(channel_index, nbasis):
    position = (channel_index.astype(f32) + 0.5) / F
    power = jnp.arange(nbasis).astype(f32)
    binomial = jnp.array([math.comb(nbasis - 1, degree) for degree in range(nbasis)], f32)
    return (
        binomial[None, :]
        * position[:, None] ** power[None, :]
        * (1.0 - position)[:, None] ** (nbasis - 1.0 - power)[None, :]
    )


def frequency(channel_index):
    return 1.0 + 0.5 * (channel_index.astype(f32) + 0.5) / F


def horner(terms, y):
    total = terms[-1]
    for term in terms[-2::-1]:
        total = total * y + term
    return total


def phasors(turns):
    r = turns - jnp.round(turns)
    y = r * r
    half_sin = r * horner(SIN_TERMS, y)
    half_cos = horner(COS_TERMS, y)
    return 1.0 - 2.0 * half_sin * half_sin, -2.0 * half_sin * half_cos


def split(x):
    high = x.astype(bf16)
    return high, (x - high.astype(f32)).astype(bf16)


def dot_nn(a, b):
    return lax.dot_general(a, b, (((1,), (0,)), ((), ())), preferred_element_type=f32)


def dot_nt(a, b):
    return lax.dot_general(a, b, (((1,), (1,)), ((), ())), preferred_element_type=f32)


def product(a, b):
    return dot_nn(a[0], b[0]) + dot_nn(a[1], b[0]) + dot_nn(a[0], b[1])


def kernel(basis_ref, ids_ref, hot_ref, hott_ref, coef_ref, c0_ref, c1_ref, s0_ref, s1_ref, c0n_ref, c1n_ref, s0n_ref,
           s1n_ref, vis_ref, flag_ref, row_ref, col_ref, ct_ref, cq_ref, jn0_ref, jn1_ref, jt0_ref, jt1_ref, x0h, x0l, x1h, x1l,
           w0h, w0l, w1h, w1l, dp0_ref, dp1_ref, dq0_ref, dq1_ref, acc_ref, pair_ref):
    step = pl.program_id(0)
    now = ((c0_ref, c1_ref), (s0_ref, s1_ref))
    ahead = ((c0n_ref, c1n_ref), (s0n_ref, s1n_ref))
    steps = pl.num_programs(0)
    odd = lax.broadcasted_iota(jnp.int32, (32, 128), 1) >= 64
    x_refs = ((x0h, x0l), (x1h, x1l))
    w_refs = ((w0h, w0l), (w1h, w1l))
    jn_refs, jt_refs = (jn0_ref, jn1_ref), (jt0_ref, jt1_ref)
    dp_refs, dq_refs = (dp0_ref, dp1_ref), (dq0_ref, dq1_ref)

    def prepare(slot, chan, table, at):
        jn_ref, jt_ref = jn_refs[slot], jt_refs[slot]
        element = lax.broadcasted_iota(jnp.int32, (8, 128), 0)
        identity = jnp.where((element == 0) | (element == 6), 1.0, 0.0).astype(f32)
        rows = []
        for k in range(K):
            total = identity
            for b in range(NB):
                total = total + basis_ref[chan, b] * ct_ref[k * 64 + b * 8:k * 64 + b * 8 + 8, :]
            rows.append(total)
        jones = jnp.concatenate(rows + rows, axis=0).T[0:RB]
        halves = [jnp.broadcast_to(ids_ref[0:1, h * 128:(h + 1) * 128], (RB, 128)) for h in range(2)]
        for e in range(8):
            for h in range(2):
                jn_ref[e, :, h * 128:(h + 1) * 128] = jnp.take_along_axis(
                    jones, halves[h] + e, axis=1, mode="promise_in_bounds"
                )
        place = lax.broadcasted_iota(jnp.int32, (K, 512), 1)
        total = jnp.where((place < 64) | ((place >= 320) & (place < 384)), 1.0, 0.0).astype(f32)
        for b in range(NB):
            total = total + basis_ref[chan, b] * cq_ref[b]
        high, low = split(total)
        total = dot_nn(hott_ref[...], jnp.concatenate([high.astype(f32), low.astype(f32)], axis=0).astype(bf16))
        for part in range(4):
            jt_ref[part] = total[:, part * 128:(part + 1) * 128]
        for t in range(T_SMP):
            er, ei = table[0][t][at, 0], table[1][t][at, 0]
            for j in range(2):
                for i in range(2):
                    jr = jn_ref[4 * i + 2 * j]
                    ji = jn_ref[4 * i + 2 * j + 1]
                    for c, value in enumerate((jr * er - ji * ei, jr * ei + ji * er)):
                        spot = slice(c * 128 + i * RB, c * 128 + (i + 1) * RB)
                        for ref, part in zip(x_refs[slot], split(value)):
                            ref[t, spot, j * 256:(j + 1) * 256] = part
            er, ei = table[0][t][at, 1], table[1][t][at, 1]
            er = jnp.concatenate([er, er], axis=0).T
            ei = jnp.concatenate([ei, ei], axis=0).T
            for j in range(2):
                jr = jt_ref[2 * j]
                ji = jt_ref[2 * j + 1]
                for c, value in enumerate((jr * er - ji * ei, jr * ei + ji * er)):
                    for ref, part in zip(w_refs[slot], split(value)):
                        ref[t, j * 256:(j + 1) * 256, c * 128:(c + 1) * 128] = part

    def forward(slot, t, row):
        result = product([ref[t] for ref in x_refs[slot]], [ref[t] for ref in w_refs[slot]])
        model = (
            result[0:128, 0:128] + result[128:256, 128:256],
            result[128:256, 0:128] - result[0:128, 128:256],
        )
        resid = []
        for c in range(2):
            observed = []
            for i in range(2):
                one = vis_ref[4 * i + c, t, 0, pl.ds(row, 32, stride=8), :]
                two = vis_ref[4 * i + 2 + c, t, 0, pl.ds(row, 32, stride=8), :]
                observed.append(jnp.where(odd, pltpu.roll(two, 64, 1), one))
                observed.append(jnp.where(odd, two, pltpu.roll(one, 64, 1)))
            resid.append(model[c] - jnp.concatenate(observed, axis=0))
        square = resid[0] * resid[0] + resid[1] * resid[1]
        square = square[0:64] + square[64:128]
        square = square + pltpu.roll(square, 64, 1)
        flag = flag_ref[t, slot].astype(f32) * SCALE
        other = pltpu.roll(flag, 64, 1)
        flag = jnp.concatenate([jnp.where(odd, other, flag), jnp.where(odd, flag, other)], axis=0)
        weight = flag / (2.0 + square)
        weight = jnp.concatenate([weight, weight], axis=0)
        re = (resid[0] * weight).T
        im = (resid[1] * weight).T
        return split(
            jnp.concatenate([jnp.concatenate([re, im], axis=1), jnp.concatenate([-im, re], axis=1)], axis=0)
        )

    def backward(slot, t, g):
        dp_ref, dq_ref = dp_refs[slot], dq_refs[slot]
        er, ei = now[0][t][slot, 0], now[1][t][slot, 0]
        er = jnp.concatenate([er, er], axis=0).T
        ei = jnp.concatenate([ei, ei], axis=0).T
        for j in range(2):
            part = product([ref[t, j * 256:(j + 1) * 256] for ref in w_refs[slot]], g)
            dr, di = part[:, 0:128], part[:, 128:256]
            jr = dr * er + di * ei
            ji = di * er - dr * ei
            if t > 0:
                jr = jr + dp_ref[:, (2 * j) * 128:(2 * j + 1) * 128]
                ji = ji + dp_ref[:, (2 * j + 1) * 128:(2 * j + 2) * 128]
            dp_ref[:, (2 * j) * 128:(2 * j + 1) * 128] = jr
            dp_ref[:, (2 * j + 1) * 128:(2 * j + 2) * 128] = ji
        er, ei = now[0][t][slot, 1], now[1][t][slot, 1]
        for j in range(2):
            part = product(g, [ref[t, :, j * 256:(j + 1) * 256] for ref in x_refs[slot]])
            for i in range(2):
                dr, di = part[i * RB:(i + 1) * RB], part[128 + i * RB:128 + (i + 1) * RB]
                jr = dr * er + di * ei
                ji = di * er - dr * ei
                e = 4 * i + 2 * j
                if t > 0:
                    jr = jr + dq_ref[e * RB:(e + 1) * RB]
                    ji = ji + dq_ref[(e + 1) * RB:(e + 2) * RB]
                dq_ref[e * RB:(e + 1) * RB] = jr
                dq_ref[(e + 1) * RB:(e + 2) * RB] = ji

    def collect(slot, chan):
        hot = hot_ref[...]
        high, low = split(dp_refs[slot][...])
        sums = [(dot_nn(hot, high) + dot_nn(hot, low))[0:8]]
        high, low = split(dq_refs[slot][...])
        sums.append((dot_nt(hot, high) + dot_nt(hot, low))[0:8])
        for side in range(2):
            for b in range(NB):
                acc_ref[b, side] += basis_ref[chan, b] * sums[side]

    @pl.when(step == 0)
    def _():
        acc_ref[...] = jnp.zeros_like(acc_ref)
        for part in range(4):
            lanes = slice(part * 128, (part + 1) * 128)
            pair_ref[part] = coef_ref[0, :, lanes]
            ct_ref[lanes, :] = jnp.concatenate(
                [
                    pair_ref[part, pl.ds(0, 32, stride=2), :],
                    pair_ref[part, pl.ds(1, 32, stride=2), :],
                    coef_ref[1, :, lanes],
                ],
                axis=0,
            ).T
        for b in range(NB):
            for j in range(2):
                for c in range(2):
                    both = [ct_ref[pl.ds(b * 8 + 4 * i + 2 * j + c, 8, stride=64), :][:, 64:128] for i in range(2)]
                    cq_ref[b, :, (2 * j + c) * 128:(2 * j + c + 1) * 128] = jnp.concatenate(both, axis=1)
        prepare(0, 0, now, 0)

    first = 2 * step
    row = first % 8
    g = [forward(0, t, row) for t in range(T_SMP)]
    prepare(1, first + 1, now, 1)
    for t in range(T_SMP):
        backward(0, t, g[t])
    g = [forward(1, t, row + 1) for t in range(T_SMP)]
    prepare(0, jnp.minimum(first + 2, 2 * steps - 1), ahead, 0)
    collect(0, first)
    for t in range(T_SMP):
        backward(1, t, g[t])
    collect(1, first + 1)

    @pl.when(step == steps - 1)
    def _():
        for b in range(NB):
            for e in range(8):
                i, j, c = e // 4, e // 2 % 2, e % 2
                first = (4 * j + 2 * c + i) * RB
                ct_ref[pl.ds(b * 8 + e, 8, stride=64), :] = jnp.concatenate(
                    [acc_ref[b, 0, :, first:first + RB], acc_ref[b, 1, :, e * RB:(e + 1) * RB]], axis=1
                )
        turned = ct_ref[...].T
        col_ref[...] = turned[64:128]
        for part in range(4):
            lanes = slice(part * 128, (part + 1) * 128)
            pair_ref[part, pl.ds(0, 32, stride=2), :] = turned[0:32, lanes]
            pair_ref[part, pl.ds(1, 32, stride=2), :] = turned[32:64, lanes]
            row_ref[:, lanes] = pair_ref[part]


def gradient_call(basis, ids, hot, coef, cosines, sines, vis, flag):
    chans = basis.shape[0]
    const = lambda shape: pl.BlockSpec(shape, lambda f: (0,) * len(shape))
    hott = jnp.concatenate([hot[0:8], hot[0:8]], axis=0).T
    now = pl.BlockSpec((2, 2, RB, NSRC), lambda f: (f, 0, 0, 0))
    ahead = pl.BlockSpec((1, 2, RB, NSRC), lambda f: (jnp.minimum(2 * f + 2, chans - 1), 0, 0, 0))
    factors = []
    for shape in ((T_SMP, 256, 512), (T_SMP, 512, 256)):
        factors += [pltpu.VMEM(shape, bf16)] * 4
    return pl.pallas_call(
        kernel,
        grid=(chans // 2,),
        in_specs=[
            pl.BlockSpec(memory_space=pltpu.SMEM),
            const((8, NSRC)),
            const((16, NSRC)),
            const((NSRC, 16)),
            const((2, RB, 512)),
            *[now] * 4,
            *[ahead] * 4,
            pl.BlockSpec((8, T_SMP, 1, 256, 128), lambda f: (0, 0, f // 4, 0, 0)),
            pl.BlockSpec((T_SMP, 2, 32, 128), lambda f: (0, f, 0, 0)),
        ],
        out_specs=[const((RB, 512))] * 2,
        out_shape=[jax.ShapeDtypeStruct((RB, 512), f32)] * 2,
        scratch_shapes=[
            pltpu.VMEM((512, 128), f32),
            pltpu.VMEM((NB, K, 512), f32),
            pltpu.VMEM((8, RB, NSRC), f32),
            pltpu.VMEM((8, RB, NSRC), f32),
            pltpu.VMEM((4, NSRC, 128), f32),
            pltpu.VMEM((4, NSRC, 128), f32),
            *factors,
            pltpu.VMEM((NSRC, 512), f32),
            pltpu.VMEM((NSRC, 512), f32),
            pltpu.VMEM((512, NSRC), f32),
            pltpu.VMEM((512, NSRC), f32),
            pltpu.VMEM((NB, 2, K, 512), f32),
            pltpu.VMEM((4, RB, 128), f32),
        ],
        compiler_params=pltpu.CompilerParams(
            dimension_semantics=("arbitrary",), vmem_limit_bytes=60 * 1024 * 1024
        ),
        cost_estimate=pl.CostEstimate(
            flops=2 * 3 * 6 * 128 * 1024 * 256 * T_SMP * chans, bytes_accessed=24 * 1024 * 1024, transcendentals=0
        ),
        name="robust_gradient",
    )(basis, ids, hot, hott, coef, *cosines, *sines, *cosines, *sines, vis, flag)


CROSS = [(r * 8 + c, c * 8 + r) for r in range(8) for c in range(8)]


def merge(held, other, axis, bit):
    upper = (lax.axis_index(axis) & bit) != 0
    return jnp.concatenate([jnp.where(upper, other, held), jnp.where(upper, held, other)], axis=0)


def table(uv, source_lm, freq, amplitude):
    geo = uv[0][..., None] * source_lm[0] + uv[1][..., None] * source_lm[1]
    cosine, sine = phasors(freq[:, None, None, None] * geo[None])
    return cosine * amplitude, sine * amplitude


def per_device(visibility, flags, coeffs, station_uv, source_lm, source_flux, cluster_ids):
    chans = visibility.shape[2]
    row = lax.axis_index("row")
    col = lax.axis_index("col")
    chan_start = lax.axis_index("chan") * chans
    channels = chan_start + jnp.arange(chans)

    basis = bernstein(channels, NB)
    row_uv = lax.dynamic_slice_in_dim(station_uv, row * RB, RB, 2)
    row_uv = row_uv.reshape(2, T_SMP, 32, 2).transpose(0, 1, 3, 2).reshape(2, T_SMP, RB)
    col_uv = lax.dynamic_slice_in_dim(station_uv, col * RB, RB, 2)
    uv = jnp.stack([row_uv, col_uv], axis=2)
    freq = frequency(channels)
    flux = lax.dynamic_slice_in_dim(source_flux, chan_start, chans, 1).T
    amplitude = jnp.stack([flux, jnp.ones_like(flux)], axis=1)[:, :, None, :]
    ids = jnp.broadcast_to(cluster_ids[None] * 8, (8, NSRC))
    hot = (cluster_ids[None] == jnp.arange(16)[:, None]).astype(bf16)

    vis = visibility.astype(f32).reshape(8, T_SMP, chans // 8, 8, 32, 128)
    vis = vis.transpose(0, 1, 2, 4, 3, 5).reshape(8, T_SMP, chans // 8, 256, 128)
    flag = flags.reshape(T_SMP, chans, 32, 128)

    row_coef, col_coef = coeffs, None
    tables = []
    for bit, t in ((1, None), (2, 0), (4, 1)):
        if t is not None:
            uv_now = lax.optimization_barrier((uv[:, t], row_coef, col_coef, tables))[0]
        other = lax.ppermute(row_coef, "col", [(c, c ^ bit) for c in range(8)])
        if col_coef is None:
            col_coef = lax.ppermute(coeffs, ("row", "col"), CROSS)
        else:
            passed = lax.ppermute(col_coef, "row", [(r, r ^ (bit // 2)) for r in range(8)])
            col_coef = merge(col_coef, passed, "row", bit // 2)
        row_coef = merge(row_coef, other, "col", bit)
        if t is not None:
            tables.append(table(uv_now, source_lm, freq, amplitude))
    passed = lax.ppermute(col_coef, "row", [(r, r ^ 4) for r in range(8)])
    col_coef = merge(col_coef, passed, "row", 4)
    coef = jnp.stack([row_coef, col_coef])

    row_part, col_part = gradient_call(
        basis, ids, hot, coef, [t[0] for t in tables], [t[1] for t in tables], vis, flag
    )
    col_part = lax.ppermute(col_part, ("row", "col"), CROSS)
    both = jnp.concatenate([row_part.reshape(8, 8, 512), col_part.reshape(8, 8, 512)], axis=1)
    both = lax.all_to_all(both, "col", 0, 0, tiled=True)
    total = both.reshape(16, 8, 512).sum(0)
    return total + lax.ppermute(total, "chan", [(0, 1), (1, 0)])


def solution(mesh):
    return jax.shard_map(
        per_device,
        mesh=mesh,
        in_specs=(
            P(None, None, "chan", "row", "col", None),
            P(None, "chan", "row", "col", None),
            P(("row", "col"), None),
            P(),
            P(),
            P(),
            P(),
        ),
        out_specs=P(("row", "col"), None),
        check_vma=False,
    )
```

time: 207 us -> 153 us (0.74)
  Pallas kernels: 126 us -> 76.6 us
  blocking collectives: 35.9 us -> 20.5 us
  starting transfers between devices: 12.4 us -> 18.7 us
  other arithmetic: 20.7 us -> 26.1 us
  local copies, waits for them, and re-layouts: 5.38 us -> 3.29 us
    pallas_call x1, Pallas kernels: 126 us -> 76.6 us  [gradient_call(): pl.pallas_call(kernel, grid=(chans // 2,), in_specs=[pl.BlockSpec(memory_...]
    all_to_all x1, blocking collectives: 35.9 us -> 20.5 us  [per_device(): both = lax.all_to_all(both, 'col', 0, 0, tiled=True)]
    ppermute x5 -> x8, starting transfers between devices: 8.15 us -> 15 us  [the longest x3 11.3 us: per_device(): other = lax.ppermute(row_coef, 'col', [(c, c ^ bit) for c in range(8)])]
    unnamed x13 -> x9, local copies, waits for them, and re-layouts: 3.44 us -> 0.05 us
    ppermute x5 -> x8, waiting for transfers between devices: 4.89 us -> 5.51 us  [the longest x1 5.5 us: per_device(): passed = lax.ppermute(col_coef, 'row', [(r, r ^ 4) for r in range(8)])]
  transfers between devices with their start and end apart: 6 -> 9, of which waited for: 3 -> 2; matrix products, arithmetic and copies ran while one was open for 11% -> 17% of each run, Pallas kernels for 0% -> 0%
where the time goes in v2:
time: 153 us
  Pallas kernels  76.6 us (50%)
  other arithmetic  26.1 us (17%)
  blocking collectives  20.5 us (13%)
  starting transfers between devices  18.7 us (12%)
  waiting for transfers between devices  7.23 us (5%)
  local copies, waits for them, and re-layouts  3.29 us (2%)
    pallas_call x1, Pallas kernels, gradient_call(): pl.pallas_call(kernel, grid=(chans // 2,), in_specs=[pl.BlockSpec(memory_...  76.6 us
    all_to_all x1, blocking collectives, per_device(): both = lax.all_to_all(both, 'col', 0, 0, tiled=True)  20.5 us
    mul x2, other arithmetic, table(): return (cosine * amplitude, sine * amplitude)  14.8 us
    ppermute x3, starting transfers between devices, per_device(): other = lax.ppermute(row_coef, 'col', [(c, c ^ bit) for c in range(8)])  11.3 us
    reshape x1, other arithmetic, per_device(): vis.transpose(0, 1, 2, 4, 3, 5).reshape(8, T_SMP, chans // 8, 256, 128)  6.58 us
    ppermute x1, waiting for transfers between devices, per_device(): passed = lax.ppermute(col_coef, 'row', [(r, r ^ 4) for r in range(8)])  5.5 us
    ppermute x1, starting transfers between devices, per_device(): return total + lax.ppermute(total, 'chan', [(0, 1), (1, 0)])  3.66 us
  transfers between devices with their start and end apart: 9, of which 2 were waited for; matrix products, arithmetic and copies ran while one was open for 17% of the time, Pallas kernels for 0%

profile of v2, /device:TPU:0, one launch (start us, length us, event | category | flops | bytes accessed | tf_op | source)
XLA Modules:
  0.0 152.6 jit_solution(3060856162609590455)
XLA Ops:
  0.0 0.0 copy-start
  0.0 2.0 %collective-permute-start = (f32[8,512]{1,0:T(8,128)}, f32[8,512]{1,0:T(8,128)S(1)}, u32[]{:S(2)}, u32[]{:S(2)}) collective-permute-start(f32[8,512]{1,0:T(8,128)} %param.10), channel_id=1, source_target_pairs={{0,2},{2,0},{4,6},{6,4},{8,10},{10,8},{12,14},{14,12},{1,3},{3,1},... | collective-permute-start | bytes 49160 | tf_op jit(solution)/shard_map/ppermute | solution.py:342
  2.0 1.4 collective-permute-start.3
  3.4 0.7 broadcast_multiply_fusion
  4.1 0.7 fusion.14.hot_ref
  4.8 0.0 copy-start.1
  4.8 0.8 fusion.19
  5.5 0.8 dynamic-slice_bitcast_fusion.1
  6.4 0.1 reshape.66
  6.5 0.1 copy.21
  6.6 0.1 stack_reshape.3
  6.7 0.0 copy-start.3
  6.7 0.0 copy-start.2
  6.7 6.6 %convert_bitcast_fusion.vis_ref = f32[8,2,4,256,128]{4,3,2,1,0:T(8,128)} fusion(bf16[8,2,32,1,1,4096]{5,2,4,3,1,0:T(8,128)(2,1)} %param.8), kind=kLoop, calls=%fused_computation | loop fusion | flops 2097152 | bytes 12582912 | tf_op jit(solution)/shard_map/reshape | solution.py:334
  13.2 0.0 copy-done.1
  13.3 0.0 copy-done
  13.3 0.0 copy-done.3
  13.3 0.7 power_multiply_fusion.basis_ref
  14.0 0.7 copy.20
  14.8 0.0 collective-permute-done
  14.8 0.0 copy-done.2
  14.9 3.5 %collective-permute-start.1 = (f32[16,512]{1,0:T(8,128)S(1)}, f32[16,512]{1,0:T(8,128)S(1)}, u32[]{:S(2)}, u32[]{:S(2)}) collective-permute-start(f32[16,512]{1,0:T(8,128)S(1)} %pad_maximum_fusion.4), channel_id=1, source_target_pairs={{0,4},{2,6},{4,0},{6,2},{8,12},{10,14},{12,8},{14,10},{1,5},{3,7},... | collective-permute-start | bytes 98312 | tf_op jit(solution)/shard_map/ppermute | solution.py:342
  18.4 0.0 collective-permute-done.3
  18.4 0.1 multiply_add_fusion.1
  18.5 0.1 collective-permute-start.4
  18.6 7.3 %multiply_multiply_fusion.8 = (f32[32,2,64,256]{3,2,1,0:T(8,128)}, f32[32,2,64,256]{3,2,1,0:T(8,128)}) fusion(f32[32,2,256]{2,1,0:T(2,128)S(1)} %stack.27.clone, f32[2,64,256]{2,1,0:T(8,128)S(1)} %multiply_add_fusion.1, f32[32]{0:T(128)S(1)} %get-tuple-element.39), kind=kLoop, calls=%fused_computation.21 | loop fusion | flops 41943040 | bytes 8585344 | tf_op jit(solution)/shard_map/mul | solution.py:312
  25.9 0.0 collective-permute-done.4
  25.9 0.2 collective-permute-start.5
  26.1 0.0 collective-permute-done.1
  26.2 5.8 %collective-permute-start.2 = (f32[32,512]{1,0:T(8,128)S(1)}, f32[32,512]{1,0:T(8,128)S(1)}, u32[]{:S(2)}, u32[]{:S(2)}) collective-permute-start(f32[32,512]{1,0:T(8,128)S(1)} %pad_maximum_fusion.2), channel_id=1, source_target_pairs={{0,8},{2,10},{4,12},{6,14},{8,0},{10,2},{12,4},{14,6},{1,9},{3,11}... | collective-permute-start | bytes 196616 | tf_op jit(solution)/shard_map/ppermute | solution.py:342
  32.0 0.1 multiply_add_fusion
  32.1 7.4 %multiply_multiply_fusion.2 = (f32[32,2,64,256]{3,2,1,0:T(8,128)}, f32[32,2,64,256]{3,2,1,0:T(8,128)}) fusion(f32[2,64,256]{2,1,0:T(8,128)S(1)} %multiply_add_fusion, f32[32,2,256]{2,1,0:T(2,128)S(1)} %stack.27.clone, f32[32]{0:T(128)S(1)} %get-tuple-element.39), kind=kLoop, calls=%fused_computation.9 | loop fusion | flops 41943040 | bytes 8585344 | tf_op jit(solution)/shard_map/mul | solution.py:312
  39.5 0.0 collective-permute-done.5
  39.5 0.5 collective-permute-start.6
  40.0 0.0 collective-permute-done.2
  40.1 5.5 %collective-permute-done.6 = f32[32,512]{1,0:T(8,128)S(1)} collective-permute-done((f32[32,512]{1,0:T(8,128)S(1)}, f32[32,512]{1,0:T(8,128)S(1)}, u32[]{:S(2)}, u32[]{:S(2)}) %collective-permute-start.6) | collective-permute-done | bytes 65568 | tf_op jit(solution)/shard_map/ppermute | solution.py:351
  45.6 0.7 pad_maximum_fusion.coef_ref
  46.3 0.6 broadcast_in_dim.2.ids_ref
  46.9 76.6 %robust_gradient.1 = (f32[64,512]{1,0:T(8,128)}, f32[64,512]{1,0:T(8,128)}) custom-call(f32[32,8]{1,0:T(8,128)} %power_multiply_fusion.basis_ref, s32[8,256]{1,0:T(8,128)} %broadcast_in_dim.2.ids_ref, bf16[16,256]{1,0:T(8,128)(2,1)} %copy-done.1, bf16[256,16]{1,0:T(8,128)(2,1)} %bitcast.35, f32[2,64,512]{2,1,0:T(8,128)} %pad_maximum_fusion.coef_ref, ...), custom_call_target="tpu_custom_call" | custom-call | flops 77309411328 | bytes 25165824 | tf_op jit(solution)/shard_map/robust_gradient/pallas_call | solution.py:260
  123.5 1.6 %collective-permute-start.7 = (f32[64,512]{1,0:T(8,128)}, f32[64,512]{1,0:T(8,128)S(1)}, u32[]{:S(2)}, u32[]{:S(2)}) collective-permute-start(f32[64,512]{1,0:T(8,128)} %get-tuple-element.12), channel_id=1, source_target_pairs={{0,0},{2,16},{4,32},{6,48},{8,64},{10,80},{12,96},{14,112},{16,2},... | collective-permute-start | bytes 393224 | tf_op jit(solution)/shard_map/ppermute | solution.py:358
  125.1 0.0 collective-permute-done.7
  125.1 0.9 pad_maximum_fusion.1
  126.0 20.5 %all_to_all.5 = f32[8,16,512]{2,1,0:T(8,128)S(1)} all-to-all(f32[8,16,512]{2,1,0:T(8,128)S(1)} %pad_maximum_fusion.1), channel_id=1, replica_groups=mesh['row'=8,'col'=8,'chan'=2] {'col'}, dimensions={0} | all-to-all | bytes 524288 | tf_op jit(solution)/shard_map/all_to_all | solution.py:360
  146.6 3.7 %collective-permute-start.8 = (f32[8,512]{1,0:T(8,128)S(1)}, f32[8,512]{1,0:T(8,128)S(1)}, u32[]{:S(2)}, u32[]{:S(2)}) collective-permute-start(f32[8,512]{1,0:T(8,128)S(1)} %reduce_sum.9), channel_id=1, source_target_pairs={{0,1},{1,0},{2,3},{3,2},{4,5},{5,4},{6,7},{7,6},{8,9},{9,8},{10,11... | collective-permute-start | bytes 49160 | tf_op jit(solution)/shard_map/ppermute | solution.py:362
  150.3 1.7 %collective-permute-done.8 = f32[8,512]{1,0:T(8,128)S(1)} collective-permute-done((f32[8,512]{1,0:T(8,128)S(1)}, f32[8,512]{1,0:T(8,128)S(1)}, u32[]{:S(2)}, u32[]{:S(2)}) %collective-permute-start.8) | collective-permute-done | bytes 16416 | tf_op jit(solution)/shard_map/ppermute | solution.py:362
  152.0 0.6 add.188
  (24 shorter events, 0.2 us)
Async XLA Ops:
  0.0 13.3 %copy-start = (f32[256,64]{0,1:T(8,128)S(1)}, f32[256,64]{0,1:T(8,128)}, u32[]{:S(2)}) copy-start(f32[256,64]{0,1:T(8,128)} %param.13) | copy-start | bytes 196612
  0.0 14.8 %collective-permute-start = (f32[8,512]{1,0:T(8,128)}, f32[8,512]{1,0:T(8,128)S(1)}, u32[]{:S(2)}, u32[]{:S(2)}) collective-permute-start(f32[8,512]{1,0:T(8,128)} %param.10), channel_id=1, source_target_pairs={{0,2},{2,0},{4,6},{6,4},{8,10},{10,8},{12,14},{14,12},{1,3},{3,1},... | collective-permute-start | bytes 49160 | tf_op jit(solution)/shard_map/ppermute | solution.py:342
  2.0 16.4 %collective-permute-start.3 = (f32[8,512]{1,0:T(8,128)}, f32[8,512]{1,0:T(8,128)S(1)}, u32[]{:S(2)}, u32[]{:S(2)}) collective-permute-start(f32[8,512]{1,0:T(8,128)} %param.10), channel_id=1, source_target_pairs={{0,0},{2,16},{4,32},{6,48},{8,64},{10,80},{12,96},{14,112},{16,2},... | collective-permute-start | bytes 49160 | tf_op jit(solution)/shard_map/ppermute | solution.py:344
  4.8 8.5 %copy-start.1 = (bf16[16,256]{1,0:T(8,128)(2,1)}, bf16[16,256]{1,0:T(8,128)(2,1)S(1)}, u32[]{:S(2)}) copy-start(bf16[16,256]{1,0:T(8,128)(2,1)S(1)} %fusion.14.hot_ref) | copy-start | bytes 24580
  6.7 6.6 %copy-start.3 = (f32[8]{0:T(128)S(1)}, f32[8]{0:T(128)}, u32[]{:S(2)}) copy-start(f32[8]{0:T(128)} %constant.80.clone) | copy-start | bytes 100
  6.7 8.1 %copy-start.2 = (f32[8,512]{1,0:T(8,128)S(1)}, f32[8,512]{1,0:T(8,128)}, u32[]{:S(2)}) copy-start(f32[8,512]{1,0:T(8,128)} %param.10) | copy-start | bytes 49156
  14.9 11.3 %collective-permute-start.1 = (f32[16,512]{1,0:T(8,128)S(1)}, f32[16,512]{1,0:T(8,128)S(1)}, u32[]{:S(2)}, u32[]{:S(2)}) collective-permute-start(f32[16,512]{1,0:T(8,128)S(1)} %pad_maximum_fusion.4), channel_id=1, source_target_pairs={{0,4},{2,6},{4,0},{6,2},{8,12},{10,14},{12,8},{14,10},{1,5},{3,7},... | collective-permute-start | bytes 98312 | tf_op jit(solution)/shard_map/ppermute | solution.py:342
  18.5 7.4 %collective-permute-start.4 = (f32[8,512]{1,0:T(8,128)S(1)}, f32[8,512]{1,0:T(8,128)S(1)}, u32[]{:S(2)}, u32[]{:S(2)}) collective-permute-start(f32[8,512]{1,0:T(8,128)S(1)} %collective-permute-done.3), channel_id=1, source_target_pairs={{0,16},{16,0},{32,48},{48,32},{64,80},{80,64},{96,112},{112,96},{1... | collective-permute-start | bytes 49160 | tf_op jit(solution)/shard_map/ppermute | solution.py:346
  25.9 13.6 %collective-permute-start.5 = (f32[16,512]{1,0:T(8,128)S(1)}, f32[16,512]{1,0:T(8,128)S(1)}, u32[]{:S(2)}, u32[]{:S(2)}) collective-permute-start(f32[16,512]{1,0:T(8,128)S(1)} %pad_maximum_fusion.5), channel_id=1, source_target_pairs={{0,32},{16,48},{32,0},{48,16},{64,96},{80,112},{96,64},{112,80},{1... | collective-permute-start | bytes 98312 | tf_op jit(solution)/shard_map/ppermute | solution.py:346
  26.2 13.9 %collective-permute-start.2 = (f32[32,512]{1,0:T(8,128)S(1)}, f32[32,512]{1,0:T(8,128)S(1)}, u32[]{:S(2)}, u32[]{:S(2)}) collective-permute-start(f32[32,512]{1,0:T(8,128)S(1)} %pad_maximum_fusion.2), channel_id=1, source_target_pairs={{0,8},{2,10},{4,12},{6,14},{8,0},{10,2},{12,4},{14,6},{1,9},{3,11}... | collective-permute-start | bytes 196616 | tf_op jit(solution)/shard_map/ppermute | solution.py:342
  39.5 6.0 %collective-permute-start.6 = (f32[32,512]{1,0:T(8,128)S(1)}, f32[32,512]{1,0:T(8,128)S(1)}, u32[]{:S(2)}, u32[]{:S(2)}) collective-permute-start(f32[32,512]{1,0:T(8,128)S(1)} %pad_maximum_fusion.3), channel_id=1, source_target_pairs={{0,64},{16,80},{32,96},{48,112},{64,0},{80,16},{96,32},{112,48},{1... | collective-permute-start | bytes 196616 | tf_op jit(solution)/shard_map/ppermute | solution.py:351
  123.5 1.6 %collective-permute-start.7 = (f32[64,512]{1,0:T(8,128)}, f32[64,512]{1,0:T(8,128)S(1)}, u32[]{:S(2)}, u32[]{:S(2)}) collective-permute-start(f32[64,512]{1,0:T(8,128)} %get-tuple-element.12), channel_id=1, source_target_pairs={{0,0},{2,16},{4,32},{6,48},{8,64},{10,80},{12,96},{14,112},{16,2},... | collective-permute-start | bytes 393224 | tf_op jit(solution)/shard_map/ppermute | solution.py:358
  146.6 5.4 %collective-permute-start.8 = (f32[8,512]{1,0:T(8,128)S(1)}, f32[8,512]{1,0:T(8,128)S(1)}, u32[]{:S(2)}, u32[]{:S(2)}) collective-permute-start(f32[8,512]{1,0:T(8,128)S(1)} %reduce_sum.9), channel_id=1, source_target_pairs={{0,1},{1,0},{2,3},{3,2},{4,5},{5,4},{6,7},{7,6},{8,9},{9,8},{10,11... | collective-permute-start | bytes 49160 | tf_op jit(solution)/shard_map/ppermute | solution.py:362

commit v3 on v2

--- a/solution.py
+++ b/solution.py
@@ -70,12 +70,11 @@
     return dot_nn(a[0], b[0]) + dot_nn(a[1], b[0]) + dot_nn(a[0], b[1])
 
 
-def kernel(basis_ref, ids_ref, hot_ref, hott_ref, coef_ref, c0_ref, c1_ref, s0_ref, s1_ref, c0n_ref, c1n_ref, s0n_ref,
-           s1n_ref, vis_ref, flag_ref, row_ref, col_ref, ct_ref, cq_ref, jn0_ref, jn1_ref, jt0_ref, jt1_ref, x0h, x0l, x1h, x1l,
-           w0h, w0l, w1h, w1l, dp0_ref, dp1_ref, dq0_ref, dq1_ref, acc_ref, pair_ref):
+def kernel(basis_ref, ids_ref, hot_ref, hott_ref, coef_ref, flux_ref, begin_ref, turn_ref, vis_ref, flag_ref, row_ref, col_ref, ct_ref, cq_ref, jn0_ref, jn1_ref, jt0_ref, jt1_ref, x0h, x0l, x1h, x1l,
+           w0h, w0l, w1h, w1l, dp0_ref, dp1_ref, dq0_ref, dq1_ref, acc_ref, pair_ref,
+           e0_ref, e1_ref, f0_ref, f1_ref):
     step = pl.program_id(0)
-    now = ((c0_ref, c1_ref), (s0_ref, s1_ref))
-    ahead = ((c0n_ref, c1n_ref), (s0n_ref, s1n_ref))
+    e_refs, f_refs = (e0_ref, e1_ref), (f0_ref, f1_ref)
     steps = pl.num_programs(0)
     odd = lax.broadcasted_iota(jnp.int32, (32, 128), 1) >= 64
     x_refs = ((x0h, x0l), (x1h, x1l))
@@ -83,7 +82,7 @@
     jn_refs, jt_refs = (jn0_ref, jn1_ref), (jt0_ref, jt1_ref)
     dp_refs, dq_refs = (dp0_ref, dp1_ref), (dq0_ref, dq1_ref)
 
-    def prepare(slot, chan, table, at):
+    def prepare(slot, chan, before):
         jn_ref, jt_ref = jn_refs[slot], jt_refs[slot]
         element = lax.broadcasted_iota(jnp.int32, (8, 128), 0)
         identity = jnp.where((element == 0) | (element == 6), 1.0, 0.0).astype(f32)
@@ -109,7 +108,17 @@
         for part in range(4):
             jt_ref[part] = total[:, part * 128:(part + 1) * 128]
         for t in range(T_SMP):
-            er, ei = table[0][t][at, 0], table[1][t][at, 0]
+            for side in range(2):
+                er, ei = before[0, t, side], before[1, t, side]
+                if before is not begin_ref:
+                    sr, si = turn_ref[0, t, side], turn_ref[1, t, side]
+                    er, ei = er * sr - ei * si, er * si + ei * sr
+                e_refs[slot][0, t, side] = er
+                e_refs[slot][1, t, side] = ei
+            flux = flux_ref[pl.ds(chan, 1), :]
+            er, ei = e_refs[slot][0, t, 0] * flux, e_refs[slot][1, t, 0] * flux
+            f_refs[slot][0, t] = er
+            f_refs[slot][1, t] = ei
             for j in range(2):
                 for i in range(2):
                     jr = jn_ref[4 * i + 2 * j]
@@ -118,7 +127,7 @@
                         spot = slice(c * 128 + i * RB, c * 128 + (i + 1) * RB)
                         for ref, part in zip(x_refs[slot], split(value)):
                             ref[t, spot, j * 256:(j + 1) * 256] = part
-            er, ei = table[0][t][at, 1], table[1][t][at, 1]
+            er, ei = e_refs[slot][0, t, 1], e_refs[slot][1, t, 1]
             er = jnp.concatenate([er, er], axis=0).T
             ei = jnp.concatenate([ei, ei], axis=0).T
             for j in range(2):
@@ -159,7 +168,7 @@
 
     def backward(slot, t, g):
         dp_ref, dq_ref = dp_refs[slot], dq_refs[slot]
-        er, ei = now[0][t][slot, 0], now[1][t][slot, 0]
+        er, ei = f_refs[slot][0, t], f_refs[slot][1, t]
         er = jnp.concatenate([er, er], axis=0).T
         ei = jnp.concatenate([ei, ei], axis=0).T
         for j in range(2):
@@ -172,7 +181,7 @@
                 ji = ji + dp_ref[:, (2 * j + 1) * 128:(2 * j + 2) * 128]
             dp_ref[:, (2 * j) * 128:(2 * j + 1) * 128] = jr
             dp_ref[:, (2 * j + 1) * 128:(2 * j + 2) * 128] = ji
-        er, ei = now[0][t][slot, 1], now[1][t][slot, 1]
+        er, ei = e_refs[slot][0, t, 1], e_refs[slot][1, t, 1]
         for j in range(2):
             part = product(g, [ref[t, :, j * 256:(j + 1) * 256] for ref in x_refs[slot]])
             for i in range(2):
@@ -215,16 +224,16 @@
                 for c in range(2):
                     both = [ct_ref[pl.ds(b * 8 + 4 * i + 2 * j + c, 8, stride=64), :][:, 64:128] for i in range(2)]
                     cq_ref[b, :, (2 * j + c) * 128:(2 * j + c + 1) * 128] = jnp.concatenate(both, axis=1)
-        prepare(0, 0, now, 0)
+        prepare(0, 0, begin_ref)
 
     first = 2 * step
     row = first % 8
     g = [forward(0, t, row) for t in range(T_SMP)]
-    prepare(1, first + 1, now, 1)
+    prepare(1, first + 1, e0_ref)
     for t in range(T_SMP):
         backward(0, t, g[t])
     g = [forward(1, t, row + 1) for t in range(T_SMP)]
-    prepare(0, jnp.minimum(first + 2, 2 * steps - 1), ahead, 0)
+    prepare(0, jnp.minimum(first + 2, 2 * steps - 1), e1_ref)
     collect(0, first)
     for t in range(T_SMP):
         backward(1, t, g[t])
@@ -248,12 +257,10 @@
             row_ref[:, lanes] = pair_ref[part]
 
 
-def gradient_call(basis, ids, hot, coef, cosines, sines, vis, flag):
+def gradient_call(basis, ids, hot, coef, flux, begin, turn, vis, flag):
     chans = basis.shape[0]
     const = lambda shape: pl.BlockSpec(shape, lambda f: (0,) * len(shape))
     hott = jnp.concatenate([hot[0:8], hot[0:8]], axis=0).T
-    now = pl.BlockSpec((2, 2, RB, NSRC), lambda f: (f, 0, 0, 0))
-    ahead = pl.BlockSpec((1, 2, RB, NSRC), lambda f: (jnp.minimum(2 * f + 2, chans - 1), 0, 0, 0))
     factors = []
     for shape in ((T_SMP, 256, 512), (T_SMP, 512, 256)):
         factors += [pltpu.VMEM(shape, bf16)] * 4
@@ -266,8 +273,9 @@
             const((16, NSRC)),
             const((NSRC, 16)),
             const((2, RB, 512)),
-            *[now] * 4,
-            *[ahead] * 4,
+            const(flux.shape),
+            const(begin.shape),
+            const(turn.shape),
             pl.BlockSpec((8, T_SMP, 1, 256, 128), lambda f: (0, 0, f // 4, 0, 0)),
             pl.BlockSpec((T_SMP, 2, 32, 128), lambda f: (0, f, 0, 0)),
         ],
@@ -287,6 +295,8 @@
             pltpu.VMEM((512, NSRC), f32),
             pltpu.VMEM((NB, 2, K, 512), f32),
             pltpu.VMEM((4, RB, 128), f32),
+            *[pltpu.VMEM((2, T_SMP, 2, RB, NSRC), f32)] * 2,
+            *[pltpu.VMEM((2, T_SMP, RB, NSRC), f32)] * 2,
         ],
         compiler_params=pltpu.CompilerParams(
             dimension_semantics=("arbitrary",), vmem_limit_bytes=60 * 1024 * 1024
@@ -295,7 +305,7 @@
             flops=2 * 3 * 6 * 128 * 1024 * 256 * T_SMP * chans, bytes_accessed=24 * 1024 * 1024, transcendentals=0
         ),
         name="robust_gradient",
-    )(basis, ids, hot, hott, coef, *cosines, *sines, *cosines, *sines, vis, flag)
+    )(basis, ids, hot, hott, coef, flux, begin, turn, vis, flag)
 
 
 CROSS = [(r * 8 + c, c * 8 + r) for r in range(8) for c in range(8)]
@@ -306,10 +316,15 @@
     return jnp.concatenate([jnp.where(upper, other, held), jnp.where(upper, held, other)], axis=0)
 
 
-def table(uv, source_lm, freq, amplitude):
-    geo = uv[0][..., None] * source_lm[0] + uv[1][..., None] * source_lm[1]
-    cosine, sine = phasors(freq[:, None, None, None] * geo[None])
-    return cosine * amplitude, sine * amplitude
+def scatter(held, axis):
+    size = lax.axis_size(axis)
+    for bit in (4, 2, 1):
+        half = held.shape[0] // 2
+        upper = (lax.axis_index(axis) & bit) != 0
+        low, high = held[:half], held[half:]
+        passed = lax.ppermute(jnp.where(upper, low, high), axis, [(r, r ^ bit) for r in range(size)])
+        held = jnp.where(upper, high, low) + passed
+    return held
 
 
 def per_device(visibility, flags, coeffs, station_uv, source_lm, source_flux, cluster_ids):
@@ -324,9 +339,10 @@
     row_uv = row_uv.reshape(2, T_SMP, 32, 2).transpose(0, 1, 3, 2).reshape(2, T_SMP, RB)
     col_uv = lax.dynamic_slice_in_dim(station_uv, col * RB, RB, 2)
     uv = jnp.stack([row_uv, col_uv], axis=2)
-    freq = frequency(channels)
+    geo = uv[0][..., None] * source_lm[0] + uv[1][..., None] * source_lm[1]
+    begin = jnp.stack(phasors(frequency(chan_start) * geo))
+    turn = jnp.stack(phasors((0.5 / F) * geo))
     flux = lax.dynamic_slice_in_dim(source_flux, chan_start, chans, 1).T
-    amplitude = jnp.stack([flux, jnp.ones_like(flux)], axis=1)[:, :, None, :]
     ids = jnp.broadcast_to(cluster_ids[None] * 8, (8, NSRC))
     hot = (cluster_ids[None] == jnp.arange(16)[:, None]).astype(bf16)
 
@@ -334,32 +350,21 @@
     vis = vis.transpose(0, 1, 2, 4, 3, 5).reshape(8, T_SMP, chans // 8, 256, 128)
     flag = flags.reshape(T_SMP, chans, 32, 128)
 
-    row_coef, col_coef = coeffs, None
-    tables = []
-    for bit, t in ((1, None), (2, 0), (4, 1)):
-        if t is not None:
-            uv_now = lax.optimization_barrier((uv[:, t], row_coef, col_coef, tables))[0]
-        other = lax.ppermute(row_coef, "col", [(c, c ^ bit) for c in range(8)])
-        if col_coef is None:
-            col_coef = lax.ppermute(coeffs, ("row", "col"), CROSS)
-        else:
-            passed = lax.ppermute(col_coef, "row", [(r, r ^ (bit // 2)) for r in range(8)])
-            col_coef = merge(col_coef, passed, "row", bit // 2)
-        row_coef = merge(row_coef, other, "col", bit)
-        if t is not None:
-            tables.append(table(uv_now, source_lm, freq, amplitude))
-    passed = lax.ppermute(col_coef, "row", [(r, r ^ 4) for r in range(8)])
-    col_coef = merge(col_coef, passed, "row", 4)
+    row_coef = coeffs
+    col_coef = lax.ppermute(coeffs, ("row", "col"), CROSS)
+    for bit in (1, 2, 4):
+        row_coef = merge(row_coef, lax.ppermute(row_coef, "col", [(c, c ^ bit) for c in range(8)]), "col", bit)
+        col_coef = merge(col_coef, lax.ppermute(col_coef, "row", [(r, r ^ bit) for r in range(8)]), "row", bit)
     coef = jnp.stack([row_coef, col_coef])
 
-    row_part, col_part = gradient_call(
-        basis, ids, hot, coef, [t[0] for t in tables], [t[1] for t in tables], vis, flag
-    )
-    col_part = lax.ppermute(col_part, ("row", "col"), CROSS)
-    both = jnp.concatenate([row_part.reshape(8, 8, 512), col_part.reshape(8, 8, 512)], axis=1)
-    both = lax.all_to_all(both, "col", 0, 0, tiled=True)
-    total = both.reshape(16, 8, 512).sum(0)
-    return total + lax.ppermute(total, "chan", [(0, 1), (1, 0)])
+    row_part, col_part = gradient_call(basis, ids, hot, coef, flux, begin, turn, vis, flag)
+    row_sum, col_sum = scatter(row_part, "col"), scatter(col_part, "row")
+    axes = ("row", "col", "chan")
+    swapped = [((r * 8 + c) * 2 + h, (r * 8 + c) * 2 + 1 - h) for r in range(8) for c in range(8) for h in range(2)]
+    crossed = [((r * 8 + c) * 2 + h, (c * 8 + r) * 2 + h) for r in range(8) for c in range(8) for h in range(2)]
+    both = [((r * 8 + c) * 2 + h, (c * 8 + r) * 2 + 1 - h) for r in range(8) for c in range(8) for h in range(2)]
+    rows = row_sum + lax.ppermute(row_sum, axes, swapped)
+    return rows + (lax.ppermute(col_sum, axes, crossed) + lax.ppermute(col_sum, axes, both))
 
 
 def solution(mesh):

time: 153 us -> 144 us (0.941)
  the two profiles are of different devices: /device:TPU:0 before, /device:TPU:5 now
where the time goes in v3:
time: 144 us; the launch traced here: 143 us
  Pallas kernels  77.2 us (54%)
  starting transfers between devices  32.7 us (23%)
  other arithmetic  15.6 us (11%)
  waiting for transfers between devices  13.5 us (9%)
  local copies, waits for them, and re-layouts  3.76 us (3%)
    pallas_call x1, Pallas kernels, gradient_call(): pl.pallas_call(kernel, grid=(chans // 2,), in_specs=[pl.BlockSpec(memory_...  77.2 us
    ppermute x1, starting transfers between devices, per_device(): lax.ppermute(col_sum, axes, both)  8.86 us
    ppermute x6, starting transfers between devices, scatter(): lax.ppermute(jnp.where(upper, low, high), axis, [(r, r ^ bit) for r in ra...  8.38 us
    ppermute x1, waiting for transfers between devices, per_device(): lax.ppermute(col_sum, axes, crossed) + lax.ppermute(col_sum, axes, both)  6.63 us
    reshape x1, other arithmetic, per_device(): vis.transpose(0, 1, 2, 4, 3, 5).reshape(8, T_SMP, chans // 8, 256, 128)  6.55 us
    ppermute x1, starting transfers between devices, per_device(): col_coef = lax.ppermute(coeffs, ('row', 'col'), CROSS)  5.14 us
    ppermute x3, starting transfers between devices, per_device(): lax.ppermute(col_coef, 'row', [(r, r ^ bit) for r in range(8)])  4.16 us
    ppermute x3, starting transfers between devices, per_device(): lax.ppermute(row_coef, 'col', [(c, c ^ bit) for c in range(8)])  3.02 us
  transfers between devices with their start and end apart: 16, of which 9 were waited for; matrix products, arithmetic and copies ran while one was open for 12% of the time, Pallas kernels for 0%

profile of v3, /device:TPU:5, one launch (start us, length us, event | category | flops | bytes accessed | tf_op | source)
XLA Modules:
  0.0 143.0 jit_solution(17776725396554220000)
XLA Ops:
  0.0 1.7 %collective-permute-start = (f32[8,512]{1,0:T(8,128)}, f32[8,512]{1,0:T(8,128)S(1)}, u32[]{:S(2)}, u32[]{:S(2)}) collective-permute-start(f32[8,512]{1,0:T(8,128)} %param.10), channel_id=1, source_target_pairs={{0,2},{2,0},{4,6},{6,4},{8,10},{10,8},{12,14},{14,12},{1,3},{3,1},... | collective-permute-start | bytes 49160 | tf_op jit(solution)/shard_map/ppermute | solution.py:356
  1.7 5.1 %collective-permute-start.3 = (f32[8,512]{1,0:T(8,128)}, f32[8,512]{1,0:T(8,128)S(1)}, u32[]{:S(2)}, u32[]{:S(2)}) collective-permute-start(f32[8,512]{1,0:T(8,128)} %param.10), channel_id=1, source_target_pairs={{0,0},{2,16},{4,32},{6,48},{8,64},{10,80},{12,96},{14,112},{16,2},... | collective-permute-start | bytes 49160 | tf_op jit(solution)/shard_map/ppermute | solution.py:354
  6.9 0.7 broadcast_multiply_fusion
  7.6 0.7 fusion.12.hot_ref
  8.3 0.8 fusion.16
  9.1 0.8 constant_dynamic-slice_fusion
  9.8 0.1 reshape.277
  9.9 0.1 copy.21
  10.0 0.1 stack_reshape.3
  10.1 6.6 %convert_bitcast_fusion.vis_ref = f32[8,2,4,256,128]{4,3,2,1,0:T(8,128)} fusion(bf16[8,2,32,1,1,4096]{5,2,4,3,1,0:T(8,128)(2,1)} %param.8), kind=kLoop, calls=%fused_computation | loop fusion | flops 2097152 | bytes 12582912 | tf_op jit(solution)/shard_map/reshape | solution.py:350
  16.7 0.6 dynamic-slice_bitcast_fusion.flux_ref
  17.3 0.7 fusion.1
  18.1 1.1 pad_maximum_fusion
  19.2 0.7 power_multiply_fusion.basis_ref
  19.9 0.7 copy.20
  20.6 0.0 collective-permute-done.3
  20.6 0.8 collective-permute-start.4
  21.5 0.1 collective-permute-start.1
  21.6 0.7 collective-permute-done.4
  22.3 1.6 %collective-permute-start.5 = (f32[16,512]{1,0:T(8,128)S(1)}, f32[16,512]{1,0:T(8,128)S(1)}, u32[]{:S(2)}, u32[]{:S(2)}) collective-permute-start(f32[16,512]{1,0:T(8,128)S(1)} %pad_maximum_fusion.6), channel_id=1, source_target_pairs={{0,32},{16,48},{32,0},{48,16},{64,96},{80,112},{96,64},{112,80},{1... | collective-permute-start | bytes 98312 | tf_op jit(solution)/shard_map/ppermute | solution.py:357
  23.9 0.4 collective-permute-done.1
  24.4 1.2 collective-permute-start.2
  25.6 1.7 %collective-permute-start.6 = (f32[32,512]{1,0:T(8,128)S(1)}, f32[32,512]{1,0:T(8,128)S(1)}, u32[]{:S(2)}, u32[]{:S(2)}) collective-permute-start(f32[32,512]{1,0:T(8,128)S(1)} %pad_maximum_fusion.4), channel_id=1, source_target_pairs={{0,64},{16,80},{32,96},{48,112},{64,0},{80,16},{96,32},{112,48},{1... | collective-permute-start | bytes 196616 | tf_op jit(solution)/shard_map/ppermute | solution.py:357
  27.4 1.7 %collective-permute-done.2 = f32[32,512]{1,0:T(8,128)S(1)} collective-permute-done((f32[32,512]{1,0:T(8,128)S(1)}, f32[32,512]{1,0:T(8,128)S(1)}, u32[]{:S(2)}, u32[]{:S(2)}) %collective-permute-start.2) | collective-permute-done | bytes 65568 | tf_op jit(solution)/shard_map/ppermute | solution.py:356
  29.1 1.5 %collective-permute-done.6 = f32[32,512]{1,0:T(8,128)S(1)} collective-permute-done((f32[32,512]{1,0:T(8,128)S(1)}, f32[32,512]{1,0:T(8,128)S(1)}, u32[]{:S(2)}, u32[]{:S(2)}) %collective-permute-start.6) | collective-permute-done | bytes 65568 | tf_op jit(solution)/shard_map/ppermute | solution.py:357
  30.7 0.7 pad_maximum_fusion.2.coef_ref
  31.4 0.6 broadcast_in_dim.2.ids_ref
  32.0 77.2 %robust_gradient.1 = (f32[64,512]{1,0:T(8,128)}, f32[64,512]{1,0:T(8,128)}) custom-call(f32[32,8]{1,0:T(8,128)} %power_multiply_fusion.basis_ref, s32[8,256]{1,0:T(8,128)} %broadcast_in_dim.2.ids_ref, bf16[16,256]{1,0:T(8,128)(2,1)} %copy-done.1, bf16[256,16]{1,0:T(8,128)(2,1)} %bitcast.25, f32[2,64,512]{2,1,0:T(8,128)} %pad_maximum_fusion.2.coef_ref, ...), custom_call_target="tpu_custom_call" | custom-call | flops 77309411328 | bytes 25165824 | tf_op jit(solution)/shard_map/robust_gradient/pallas_call | solution.py:267
  109.2 0.9 slice_select_fusion
  110.1 1.4 %collective-permute-start.11 = (f32[32,512]{1,0:T(8,128)S(1)}, f32[32,512]{1,0:T(8,128)S(1)}, u32[]{:S(2)}, u32[]{:S(2)}) collective-permute-start(f32[32,512]{1,0:T(8,128)S(1)} %slice_select_fusion), channel_id=1, source_target_pairs={{0,64},{16,80},{32,96},{48,112},{64,0},{80,16},{96,32},{112,48},{1... | collective-permute-start | bytes 196616 | tf_op jit(solution)/shard_map/ppermute | solution.py:325
  111.5 0.9 slice_select_fusion.1
  112.4 0.8 collective-permute-start.7
  113.2 1.5 %collective-permute-done.11 = f32[32,512]{1,0:T(8,128)S(1)} collective-permute-done((f32[32,512]{1,0:T(8,128)S(1)}, f32[32,512]{1,0:T(8,128)S(1)}, u32[]{:S(2)}, u32[]{:S(2)}) %collective-permute-start.11) | collective-permute-done | bytes 65568 | tf_op jit(solution)/shard_map/ppermute | solution.py:325
  114.8 0.9 select_add_fusion
  115.7 1.2 collective-permute-start.12
  116.8 0.3 collective-permute-done.7
  117.1 0.9 select_add_fusion.1
  118.0 0.2 collective-permute-start.8
  118.2 0.3 collective-permute-done.12
  118.5 4.3 %collective-permute-start.13 = (f32[8,512]{1,0:T(8,128)S(1)}, f32[8,512]{1,0:T(8,128)S(1)}, u32[]{:S(2)}, u32[]{:S(2)}) collective-permute-start(f32[8,512]{1,0:T(8,128)S(1)} %slice_select_fusion.4), channel_id=1, source_target_pairs={{0,16},{16,0},{32,48},{48,32},{64,80},{80,64},{96,112},{112,96},{1... | collective-permute-start | bytes 49160 | tf_op jit(solution)/shard_map/ppermute | solution.py:325
  122.9 0.4 collective-permute-start.9
  123.3 0.4 collective-permute-done.13
  123.7 8.9 %collective-permute-start.15 = (f32[8,512]{1,0:T(8,128)S(1)}, f32[8,512]{1,0:T(8,128)S(1)}, u32[]{:S(2)}, u32[]{:S(2)}) collective-permute-start(f32[8,512]{1,0:T(8,128)S(1)} %select_add_fusion.4), channel_id=1, source_target_pairs={{0,1},{1,0},{2,17},{3,16},{4,33},{5,32},{6,49},{7,48},{8,65},{9,64... | collective-permute-start | bytes 49160 | tf_op jit(solution)/shard_map/ppermute | solution.py:367
  132.5 1.9 %collective-permute-start.14 = (f32[8,512]{1,0:T(8,128)S(1)}, f32[8,512]{1,0:T(8,128)S(1)}, u32[]{:S(2)}, u32[]{:S(2)}) collective-permute-start(f32[8,512]{1,0:T(8,128)S(1)} %select_add_fusion.4), channel_id=1, source_target_pairs={{0,0},{1,1},{2,16},{3,17},{4,32},{5,33},{6,48},{7,49},{8,64},{9,65... | collective-permute-start | bytes 49160 | tf_op jit(solution)/shard_map/ppermute | solution.py:367
  134.5 0.0 collective-permute-done.9
  134.5 1.3 collective-permute-start.10
  135.8 6.6 %collective-permute-done.14 = f32[8,512]{1,0:T(8,128)S(1)} collective-permute-done((f32[8,512]{1,0:T(8,128)S(1)}, f32[8,512]{1,0:T(8,128)S(1)}, u32[]{:S(2)}, u32[]{:S(2)}) %collective-permute-start.14) | collective-permute-done | bytes 16416 | tf_op jit(solution)/shard_map/ppermute | solution.py:367
  142.4 0.6 add_add_fusion
  (40 shorter events, 0.2 us)
Async XLA Ops:
  0.0 16.7 %copy-start = (f32[256,64]{0,1:T(8,128)S(1)}, f32[256,64]{0,1:T(8,128)}, u32[]{:S(2)}) copy-start(f32[256,64]{0,1:T(8,128)} %param.13) | copy-start | bytes 196612
  0.0 19.2 %copy-start.3 = (f32[8]{0:T(128)S(1)}, f32[8]{0:T(128)}, u32[]{:S(2)}) copy-start(f32[8]{0:T(128)} %constant.81.clone) | copy-start | bytes 100
  0.0 21.5 %copy-start.2 = (f32[8,512]{1,0:T(8,128)S(1)}, f32[8,512]{1,0:T(8,128)}, u32[]{:S(2)}) copy-start(f32[8,512]{1,0:T(8,128)} %param.10) | copy-start | bytes 49156
  0.0 21.5 %collective-permute-start = (f32[8,512]{1,0:T(8,128)}, f32[8,512]{1,0:T(8,128)S(1)}, u32[]{:S(2)}, u32[]{:S(2)}) collective-permute-start(f32[8,512]{1,0:T(8,128)} %param.10), channel_id=1, source_target_pairs={{0,2},{2,0},{4,6},{6,4},{8,10},{10,8},{12,14},{14,12},{1,3},{3,1},... | collective-permute-start | bytes 49160 | tf_op jit(solution)/shard_map/ppermute | solution.py:356
  1.7 18.9 %collective-permute-start.3 = (f32[8,512]{1,0:T(8,128)}, f32[8,512]{1,0:T(8,128)S(1)}, u32[]{:S(2)}, u32[]{:S(2)}) collective-permute-start(f32[8,512]{1,0:T(8,128)} %param.10), channel_id=1, source_target_pairs={{0,0},{2,16},{4,32},{6,48},{8,64},{10,80},{12,96},{14,112},{16,2},... | collective-permute-start | bytes 49160 | tf_op jit(solution)/shard_map/ppermute | solution.py:354
  8.3 17.3 %copy-start.1 = (bf16[16,256]{1,0:T(8,128)(2,1)}, bf16[16,256]{1,0:T(8,128)(2,1)S(1)}, u32[]{:S(2)}) copy-start(bf16[16,256]{1,0:T(8,128)(2,1)S(1)} %fusion.12.hot_ref) | copy-start | bytes 24580
  20.6 1.7 %collective-permute-start.4 = (f32[8,512]{1,0:T(8,128)S(1)}, f32[8,512]{1,0:T(8,128)S(1)}, u32[]{:S(2)}, u32[]{:S(2)}) collective-permute-start(f32[8,512]{1,0:T(8,128)S(1)} %collective-permute-done.3), channel_id=1, source_target_pairs={{0,16},{16,0},{32,48},{48,32},{64,80},{80,64},{96,112},{112,96},{1... | collective-permute-start | bytes 49160 | tf_op jit(solution)/shard_map/ppermute | solution.py:357
  21.5 2.8 %collective-permute-start.1 = (f32[16,512]{1,0:T(8,128)S(1)}, f32[16,512]{1,0:T(8,128)S(1)}, u32[]{:S(2)}, u32[]{:S(2)}) collective-permute-start(f32[16,512]{1,0:T(8,128)S(1)} %pad_maximum_fusion.5), channel_id=1, source_target_pairs={{0,4},{2,6},{4,0},{6,2},{8,12},{10,14},{12,8},{14,10},{1,5},{3,7},... | collective-permute-start | bytes 98312 | tf_op jit(solution)/shard_map/ppermute | solution.py:356
  22.3 3.3 %collective-permute-start.5 = (f32[16,512]{1,0:T(8,128)S(1)}, f32[16,512]{1,0:T(8,128)S(1)}, u32[]{:S(2)}, u32[]{:S(2)}) collective-permute-start(f32[16,512]{1,0:T(8,128)S(1)} %pad_maximum_fusion.6), channel_id=1, source_target_pairs={{0,32},{16,48},{32,0},{48,16},{64,96},{80,112},{96,64},{112,80},{1... | collective-permute-start | bytes 98312 | tf_op jit(solution)/shard_map/ppermute | solution.py:357
  24.4 4.7 %collective-permute-start.2 = (f32[32,512]{1,0:T(8,128)S(1)}, f32[32,512]{1,0:T(8,128)S(1)}, u32[]{:S(2)}, u32[]{:S(2)}) collective-permute-start(f32[32,512]{1,0:T(8,128)S(1)} %pad_maximum_fusion.3), channel_id=1, source_target_pairs={{0,8},{2,10},{4,12},{6,14},{8,0},{10,2},{12,4},{14,6},{1,9},{3,11}... | collective-permute-start | bytes 196616 | tf_op jit(solution)/shard_map/ppermute | solution.py:356
  25.6 5.0 %collective-permute-start.6 = (f32[32,512]{1,0:T(8,128)S(1)}, f32[32,512]{1,0:T(8,128)S(1)}, u32[]{:S(2)}, u32[]{:S(2)}) collective-permute-start(f32[32,512]{1,0:T(8,128)S(1)} %pad_maximum_fusion.4), channel_id=1, source_target_pairs={{0,64},{16,80},{32,96},{48,112},{64,0},{80,16},{96,32},{112,48},{1... | collective-permute-start | bytes 196616 | tf_op jit(solution)/shard_map/ppermute | solution.py:357
  110.1 4.7 %collective-permute-start.11 = (f32[32,512]{1,0:T(8,128)S(1)}, f32[32,512]{1,0:T(8,128)S(1)}, u32[]{:S(2)}, u32[]{:S(2)}) collective-permute-start(f32[32,512]{1,0:T(8,128)S(1)} %slice_select_fusion), channel_id=1, source_target_pairs={{0,64},{16,80},{32,96},{48,112},{64,0},{80,16},{96,32},{112,48},{1... | collective-permute-start | bytes 196616 | tf_op jit(solution)/shard_map/ppermute | solution.py:325
  112.4 4.7 %collective-permute-start.7 = (f32[32,512]{1,0:T(8,128)S(1)}, f32[32,512]{1,0:T(8,128)S(1)}, u32[]{:S(2)}, u32[]{:S(2)}) collective-permute-start(f32[32,512]{1,0:T(8,128)S(1)} %slice_select_fusion.1), channel_id=1, source_target_pairs={{0,8},{2,10},{4,12},{6,14},{8,0},{10,2},{12,4},{14,6},{1,9},{3,11}... | collective-permute-start | bytes 196616 | tf_op jit(solution)/shard_map/ppermute | solution.py:325
  115.7 2.8 %collective-permute-start.12 = (f32[16,512]{1,0:T(8,128)S(1)}, f32[16,512]{1,0:T(8,128)S(1)}, u32[]{:S(2)}, u32[]{:S(2)}) collective-permute-start(f32[16,512]{1,0:T(8,128)S(1)} %slice_select_fusion.2), channel_id=1, source_target_pairs={{0,32},{16,48},{32,0},{48,16},{64,96},{80,112},{96,64},{112,80},{1... | collective-permute-start | bytes 98312 | tf_op jit(solution)/shard_map/ppermute | solution.py:325
  118.0 4.9 %collective-permute-start.8 = (f32[16,512]{1,0:T(8,128)S(1)}, f32[16,512]{1,0:T(8,128)S(1)}, u32[]{:S(2)}, u32[]{:S(2)}) collective-permute-start(f32[16,512]{1,0:T(8,128)S(1)} %slice_select_fusion.3), channel_id=1, source_target_pairs={{0,4},{2,6},{4,0},{6,2},{8,12},{10,14},{12,8},{14,10},{1,5},{3,7},... | collective-permute-start | bytes 98312 | tf_op jit(solution)/shard_map/ppermute | solution.py:325
  118.5 5.1 %collective-permute-start.13 = (f32[8,512]{1,0:T(8,128)S(1)}, f32[8,512]{1,0:T(8,128)S(1)}, u32[]{:S(2)}, u32[]{:S(2)}) collective-permute-start(f32[8,512]{1,0:T(8,128)S(1)} %slice_select_fusion.4), channel_id=1, source_target_pairs={{0,16},{16,0},{32,48},{48,32},{64,80},{80,64},{96,112},{112,96},{1... | collective-permute-start | bytes 49160 | tf_op jit(solution)/shard_map/ppermute | solution.py:325
  122.9 11.6 %collective-permute-start.9 = (f32[8,512]{1,0:T(8,128)S(1)}, f32[8,512]{1,0:T(8,128)S(1)}, u32[]{:S(2)}, u32[]{:S(2)}) collective-permute-start(f32[8,512]{1,0:T(8,128)S(1)} %slice_select_fusion.5), channel_id=1, source_target_pairs={{0,2},{2,0},{4,6},{6,4},{8,10},{10,8},{12,14},{14,12},{1,3},{3,1},... | collective-permute-start | bytes 49160 | tf_op jit(solution)/shard_map/ppermute | solution.py:325
  123.7 12.1 %collective-permute-start.15 = (f32[8,512]{1,0:T(8,128)S(1)}, f32[8,512]{1,0:T(8,128)S(1)}, u32[]{:S(2)}, u32[]{:S(2)}) collective-permute-start(f32[8,512]{1,0:T(8,128)S(1)} %select_add_fusion.4), channel_id=1, source_target_pairs={{0,1},{1,0},{2,17},{3,16},{4,33},{5,32},{6,49},{7,48},{8,65},{9,64... | collective-permute-start | bytes 49160 | tf_op jit(solution)/shard_map/ppermute | solution.py:367
  132.5 9.9 %collective-permute-start.14 = (f32[8,512]{1,0:T(8,128)S(1)}, f32[8,512]{1,0:T(8,128)S(1)}, u32[]{:S(2)}, u32[]{:S(2)}) collective-permute-start(f32[8,512]{1,0:T(8,128)S(1)} %select_add_fusion.4), channel_id=1, source_target_pairs={{0,0},{1,1},{2,16},{3,17},{4,32},{5,33},{6,48},{7,49},{8,64},{9,65... | collective-permute-start | bytes 49160 | tf_op jit(solution)/shard_map/ppermute | solution.py:367
  134.5 7.9 %collective-permute-start.10 = (f32[8,512]{1,0:T(8,128)S(1)}, f32[8,512]{1,0:T(8,128)S(1)}, u32[]{:S(2)}, u32[]{:S(2)}) collective-permute-start(f32[8,512]{1,0:T(8,128)S(1)} %select_add_fusion.5), channel_id=1, source_target_pairs={{0,1},{1,0},{2,3},{3,2},{4,5},{5,4},{6,7},{7,6},{8,9},{9,8},{10,11... | collective-permute-start | bytes 49160 | tf_op jit(solution)/shard_map/ppermute | solution.py:366

commit v4 on v3

--- a/solution.py
+++ b/solution.py
@@ -14,6 +14,7 @@
 NSRC = 256
 T_SMP = 2
 RB = 64
+BLK = 4096
 SCALE = 10.0 / math.sqrt(S * F * T_SMP)
 
 f32 = jnp.float32
@@ -70,9 +71,9 @@
     return dot_nn(a[0], b[0]) + dot_nn(a[1], b[0]) + dot_nn(a[0], b[1])
 
 
-def kernel(basis_ref, ids_ref, hot_ref, hott_ref, coef_ref, flux_ref, begin_ref, turn_ref, vis_ref, flag_ref, row_ref, col_ref, ct_ref, cq_ref, jn0_ref, jn1_ref, jt0_ref, jt1_ref, x0h, x0l, x1h, x1l,
+def kernel(chan_ref, basis_ref, ids_ref, hot_ref, hott_ref, coef_ref, flux_ref, begin_ref, turn_ref, vis_ref, flag_ref, kept_ref, sent_ref, ct_ref, cq_ref, jn0_ref, jn1_ref, jt0_ref, jt1_ref, x0h, x0l, x1h, x1l,
            w0h, w0l, w1h, w1l, dp0_ref, dp1_ref, dq0_ref, dq1_ref, acc_ref, pair_ref,
-           e0_ref, e1_ref, f0_ref, f1_ref):
+           e0_ref, e1_ref, f0_ref, f1_ref, wide_ref):
     step = pl.program_id(0)
     e_refs, f_refs = (e0_ref, e1_ref), (f0_ref, f1_ref)
     steps = pl.num_programs(0)
@@ -147,8 +148,8 @@
         for c in range(2):
             observed = []
             for i in range(2):
-                one = vis_ref[4 * i + c, t, 0, pl.ds(row, 32, stride=8), :]
-                two = vis_ref[4 * i + 2 + c, t, 0, pl.ds(row, 32, stride=8), :]
+                one = wide_ref[4 * i + c, t, pl.ds(row, 32, stride=8), :]
+                two = wide_ref[4 * i + 2 + c, t, pl.ds(row, 32, stride=8), :]
                 observed.append(jnp.where(odd, pltpu.roll(two, 64, 1), one))
                 observed.append(jnp.where(odd, two, pltpu.roll(one, 64, 1)))
             resid.append(model[c] - jnp.concatenate(observed, axis=0))
@@ -166,34 +167,33 @@
             jnp.concatenate([jnp.concatenate([re, im], axis=1), jnp.concatenate([-im, re], axis=1)], axis=0)
         )
 
-    def backward(slot, t, g):
+    def backward(slot, g):
         dp_ref, dq_ref = dp_refs[slot], dq_refs[slot]
-        er, ei = f_refs[slot][0, t], f_refs[slot][1, t]
-        er = jnp.concatenate([er, er], axis=0).T
-        ei = jnp.concatenate([ei, ei], axis=0).T
+        phasors_t = []
+        for t in range(T_SMP):
+            er, ei = f_refs[slot][0, t], f_refs[slot][1, t]
+            phasors_t.append((jnp.concatenate([er, er], axis=0).T, jnp.concatenate([ei, ei], axis=0).T))
         for j in range(2):
-            part = product([ref[t, j * 256:(j + 1) * 256] for ref in w_refs[slot]], g)
-            dr, di = part[:, 0:128], part[:, 128:256]
-            jr = dr * er + di * ei
-            ji = di * er - dr * ei
-            if t > 0:
-                jr = jr + dp_ref[:, (2 * j) * 128:(2 * j + 1) * 128]
-                ji = ji + dp_ref[:, (2 * j + 1) * 128:(2 * j + 2) * 128]
-            dp_ref[:, (2 * j) * 128:(2 * j + 1) * 128] = jr
-            dp_ref[:, (2 * j + 1) * 128:(2 * j + 2) * 128] = ji
-        er, ei = e_refs[slot][0, t, 1], e_refs[slot][1, t, 1]
+            sums = [0.0, 0.0]
+            for t in range(T_SMP):
+                er, ei = phasors_t[t]
+                part = product([ref[t, j * 256:(j + 1) * 256] for ref in w_refs[slot]], g[t])
+                dr, di = part[:, 0:128], part[:, 128:256]
+                sums = [sums[0] + dr * er + di * ei, sums[1] + di * er - dr * ei]
+            for c in range(2):
+                dp_ref[:, (2 * j + c) * 128:(2 * j + c + 1) * 128] = sums[c]
         for j in range(2):
-            part = product(g, [ref[t, :, j * 256:(j + 1) * 256] for ref in x_refs[slot]])
+            sums = [[0.0, 0.0], [0.0, 0.0]]
+            for t in range(T_SMP):
+                er, ei = e_refs[slot][0, t, 1], e_refs[slot][1, t, 1]
+                part = product(g[t], [ref[t, :, j * 256:(j + 1) * 256] for ref in x_refs[slot]])
+                for i in range(2):
+                    dr, di = part[i * RB:(i + 1) * RB], part[128 + i * RB:128 + (i + 1) * RB]
+                    sums[i] = [sums[i][0] + dr * er + di * ei, sums[i][1] + di * er - dr * ei]
             for i in range(2):
-                dr, di = part[i * RB:(i + 1) * RB], part[128 + i * RB:128 + (i + 1) * RB]
-                jr = dr * er + di * ei
-                ji = di * er - dr * ei
-                e = 4 * i + 2 * j
-                if t > 0:
-                    jr = jr + dq_ref[e * RB:(e + 1) * RB]
-                    ji = ji + dq_ref[(e + 1) * RB:(e + 2) * RB]
-                dq_ref[e * RB:(e + 1) * RB] = jr
-                dq_ref[(e + 1) * RB:(e + 2) * RB] = ji
+                for c in range(2):
+                    e = 4 * i + 2 * j + c
+                    dq_ref[e * RB:(e + 1) * RB] = sums[i][c]
 
     def collect(slot, chan):
         hot = hot_ref[...]
@@ -227,16 +227,28 @@
         prepare(0, 0, begin_ref)
 
     first = 2 * step
-    row = first % 8
+    row = first // 8 % 2 * 256 + first % 8
+
+    @pl.when(step % 8 == 0)
+    def _():
+        def widen(index, carry):
+            e, t = index // T_SMP, index % T_SMP
+            wide = vis_ref[e, t].astype(f32)
+            for g in range(2):
+                for p in range(32):
+                    spot = g * 256 + p * 8
+                    wide_ref[e, t, spot:spot + 8, :] = wide[g * 8:(g + 1) * 8, p * 128:(p + 1) * 128]
+            return carry
+
+        lax.fori_loop(0, 8 * T_SMP, widen, 0)
+
     g = [forward(0, t, row) for t in range(T_SMP)]
     prepare(1, first + 1, e0_ref)
-    for t in range(T_SMP):
-        backward(0, t, g[t])
+    backward(0, g)
     g = [forward(1, t, row + 1) for t in range(T_SMP)]
     prepare(0, jnp.minimum(first + 2, 2 * steps - 1), e1_ref)
     collect(0, first)
-    for t in range(T_SMP):
-        backward(1, t, g[t])
+    backward(1, g)
     collect(1, first + 1)
 
     @pl.when(step == steps - 1)
@@ -249,15 +261,17 @@
                     [acc_ref[b, 0, :, first:first + RB], acc_ref[b, 1, :, e * RB:(e + 1) * RB]], axis=1
                 )
         turned = ct_ref[...].T
-        col_ref[...] = turned[64:128]
+        first_chan = chan_ref[0] == 0
         for part in range(4):
             lanes = slice(part * 128, (part + 1) * 128)
             pair_ref[part, pl.ds(0, 32, stride=2), :] = turned[0:32, lanes]
             pair_ref[part, pl.ds(1, 32, stride=2), :] = turned[32:64, lanes]
-            row_ref[:, lanes] = pair_ref[part]
-
-
-def gradient_call(basis, ids, hot, coef, flux, begin, turn, vis, flag):
+            row_part, col_part = pair_ref[part], turned[64:128, lanes]
+            kept_ref[:, lanes] = jnp.where(first_chan, row_part, col_part)
+            sent_ref[:, lanes] = jnp.where(first_chan, col_part, row_part)
+
+
+def gradient_call(chan, basis, ids, hot, coef, flux, begin, turn, vis, flag):
     chans = basis.shape[0]
     const = lambda shape: pl.BlockSpec(shape, lambda f: (0,) * len(shape))
     hott = jnp.concatenate([hot[0:8], hot[0:8]], axis=0).T
@@ -269,6 +283,7 @@
         grid=(chans // 2,),
         in_specs=[
             pl.BlockSpec(memory_space=pltpu.SMEM),
+            pl.BlockSpec(memory_space=pltpu.SMEM),
             const((8, NSRC)),
             const((16, NSRC)),
             const((NSRC, 16)),
@@ -276,7 +291,7 @@
             const(flux.shape),
             const(begin.shape),
             const(turn.shape),
-            pl.BlockSpec((8, T_SMP, 1, 256, 128), lambda f: (0, 0, f // 4, 0, 0)),
+            pl.BlockSpec((8, T_SMP, 16, BLK), lambda f: (0, 0, f // 8, 0)),
             pl.BlockSpec((T_SMP, 2, 32, 128), lambda f: (0, f, 0, 0)),
         ],
         out_specs=[const((RB, 512))] * 2,
@@ -297,6 +312,7 @@
             pltpu.VMEM((4, RB, 128), f32),
             *[pltpu.VMEM((2, T_SMP, 2, RB, NSRC), f32)] * 2,
             *[pltpu.VMEM((2, T_SMP, RB, NSRC), f32)] * 2,
+            pltpu.VMEM((8, T_SMP, 512, 128), f32),
         ],
         compiler_params=pltpu.CompilerParams(
             dimension_semantics=("arbitrary",), vmem_limit_bytes=60 * 1024 * 1024
@@ -305,7 +321,7 @@
             flops=2 * 3 * 6 * 128 * 1024 * 256 * T_SMP * chans, bytes_accessed=24 * 1024 * 1024, transcendentals=0
         ),
         name="robust_gradient",
-    )(basis, ids, hot, hott, coef, flux, begin, turn, vis, flag)
+    )(chan, basis, ids, hot, hott, coef, flux, begin, turn, vis, flag)
 
 
 CROSS = [(r * 8 + c, c * 8 + r) for r in range(8) for c in range(8)]
@@ -316,15 +332,9 @@
     return jnp.concatenate([jnp.where(upper, other, held), jnp.where(upper, held, other)], axis=0)
 
 
-def scatter(held, axis):
-    size = lax.axis_size(axis)
-    for bit in (4, 2, 1):
-        half = held.shape[0] // 2
-        upper = (lax.axis_index(axis) & bit) != 0
-        low, high = held[:half], held[half:]
-        passed = lax.ppermute(jnp.where(upper, low, high), axis, [(r, r ^ bit) for r in range(size)])
-        held = jnp.where(upper, high, low) + passed
-    return held
+def pairs(target):
+    index = lambda r, c, h: (r * 8 + c) * 2 + h
+    return [(index(r, c, h), index(*target(r, c, h))) for r in range(8) for c in range(8) for h in range(2)]
 
 
 def per_device(visibility, flags, coeffs, station_uv, source_lm, source_flux, cluster_ids):
@@ -346,8 +356,7 @@
     ids = jnp.broadcast_to(cluster_ids[None] * 8, (8, NSRC))
     hot = (cluster_ids[None] == jnp.arange(16)[:, None]).astype(bf16)
 
-    vis = visibility.astype(f32).reshape(8, T_SMP, chans // 8, 8, 32, 128)
-    vis = vis.transpose(0, 1, 2, 4, 3, 5).reshape(8, T_SMP, chans // 8, 256, 128)
+    vis = visibility.reshape(8, T_SMP, chans, BLK)
     flag = flags.reshape(T_SMP, chans, 32, 128)
 
     row_coef = coeffs
@@ -357,14 +366,20 @@
         col_coef = merge(col_coef, lax.ppermute(col_coef, "row", [(r, r ^ bit) for r in range(8)]), "row", bit)
     coef = jnp.stack([row_coef, col_coef])
 
-    row_part, col_part = gradient_call(basis, ids, hot, coef, flux, begin, turn, vis, flag)
-    row_sum, col_sum = scatter(row_part, "col"), scatter(col_part, "row")
+    chan = lax.axis_index("chan")
+    kept, sent = gradient_call(chan.reshape(1), basis, ids, hot, coef, flux, begin, turn, vis, flag)
     axes = ("row", "col", "chan")
-    swapped = [((r * 8 + c) * 2 + h, (r * 8 + c) * 2 + 1 - h) for r in range(8) for c in range(8) for h in range(2)]
-    crossed = [((r * 8 + c) * 2 + h, (c * 8 + r) * 2 + h) for r in range(8) for c in range(8) for h in range(2)]
-    both = [((r * 8 + c) * 2 + h, (c * 8 + r) * 2 + 1 - h) for r in range(8) for c in range(8) for h in range(2)]
-    rows = row_sum + lax.ppermute(row_sum, axes, swapped)
-    return rows + (lax.ppermute(col_sum, axes, crossed) + lax.ppermute(col_sum, axes, both))
+    held = kept + lax.ppermute(sent, axes, pairs(lambda r, c, h: (r, c, 1 - h)))
+    place = jnp.where(chan == 0, col, row)
+    for bit in (4, 2, 1):
+        half = held.shape[0] // 2
+        upper = (place & bit) != 0
+        low, high = held[:half], held[half:]
+        partner = pairs(lambda r, c, h: (r, c ^ bit, h) if h == 0 else (r ^ bit, c, h))
+        held = jnp.where(upper, high, low) + lax.ppermute(jnp.where(upper, low, high), axes, partner)
+    other = lax.ppermute(held, axes, pairs(lambda r, c, h: (r, c, 1) if h == 0 else (c, r, 0)))
+    crossed = lax.ppermute(held, axes, pairs(lambda r, c, h: (c, r, h)))
+    return jnp.where(chan == 0, held + other, other + crossed)
 
 
 def solution(mesh):

time: 144 us -> 137 us (0.951)
  the two profiles are of different devices: /device:TPU:5 before, /device:TPU:81 now
where the time goes in v4:
time: 137 us; the launch traced here: 136 us
  Pallas kernels  74.4 us (54%)
  starting transfers between devices  28.3 us (21%)
  waiting for transfers between devices  21.9 us (16%)
  other arithmetic  7.75 us (6%)
  local copies, waits for them, and re-layouts  3.77 us (3%)
    pallas_call x1, Pallas kernels, gradient_call(): pl.pallas_call(kernel, grid=(chans // 2,), in_specs=[pl.BlockSpec(memory_...  74.4 us
    ppermute x3, starting transfers between devices, per_device(): lax.ppermute(jnp.where(upper, low, high), axes, partner)  10.1 us
    ppermute x1, waiting for transfers between devices, per_device(): crossed = lax.ppermute(held, axes, pairs(lambda r, c, h: (c, r, h)))  7.94 us
    ppermute x1, starting transfers between devices, per_device(): col_coef = lax.ppermute(coeffs, ('row', 'col'), CROSS)  6.17 us
    ppermute x1, waiting for transfers between devices, per_device(): held = kept + lax.ppermute(sent, axes, pairs(lambda r, c, h: (r, c, 1 - h)))  5.51 us
    ppermute x1, starting transfers between devices, per_device(): lax.ppermute(held, axes, pairs(lambda r, c, h: (r, c, 1) if h == 0 else (...  5.19 us
    ppermute x3, waiting for transfers between devices, per_device(): lax.ppermute(jnp.where(upper, low, high), axes, partner)  4.58 us
    ppermute x3, starting transfers between devices, per_device(): lax.ppermute(col_coef, 'row', [(r, r ^ bit) for r in range(8)])  4.13 us
  transfers between devices with their start and end apart: 13, of which 9 were waited for; matrix products, arithmetic and copies ran while one was open for 6% of the time, Pallas kernels for 0%

profile of v4, /device:TPU:81, one launch (start us, length us, event | category | flops | bytes accessed | tf_op | source)
XLA Modules:
  0.0 136.3 jit_solution(5273961682942767696)
XLA Ops:
  0.0 0.0 copy-start
  0.0 6.2 %collective-permute-start.3 = (f32[8,512]{1,0:T(8,128)}, f32[8,512]{1,0:T(8,128)S(1)}, u32[]{:S(2)}, u32[]{:S(2)}) collective-permute-start(f32[8,512]{1,0:T(8,128)} %param.10), channel_id=1, source_target_pairs={{0,0},{2,16},{4,32},{6,48},{8,64},{10,80},{12,96},{14,112},{16,2},... | collective-permute-start | bytes 49160 | tf_op jit(solution)/shard_map/ppermute | solution.py:363
  6.2 0.1 collective-permute-start
  6.3 0.7 fusion.12.hot_ref
  7.0 0.0 copy-start.1
  7.0 0.7 broadcast_multiply_fusion
  7.7 0.8 constant_dynamic-slice_fusion
  8.5 0.1 reshape.275
  8.6 0.1 copy.21
  8.7 0.1 stack_reshape.3
  8.8 0.8 fusion.16
  9.5 0.0 copy-done
  9.5 0.6 dynamic-slice_bitcast_fusion.flux_ref
  10.2 0.7 fusion.1
  10.9 1.1 pad_maximum_fusion
  12.0 1.4 %power_multiply_fusion.basis_ref = f32[32,8]{1,0:T(8,128)} fusion(f32[8]{0:T(128)} %constant.81.clone, f32[8]{0:T(128)S(1)} %broadcast_subtract_fusion, f32[32]{0:T(128)S(1)} %get-tuple-element.32, f32[8]{0:T(128)S(1)} %iota_convert_fusion, f32[32]{0:T(128)S(1)} %get-tuple-element.31), kind=kLoop, calls=%fused_computation.52 | loop fusion | flops 512 | bytes 1376 | tf_op jit(solution)/shard_map/mul | solution.py:32
  13.4 0.7 copy.20
  14.1 0.0 collective-permute-done.3
  14.1 0.2 collective-permute-start.4
  14.3 0.0 collective-permute-done
  14.3 0.7 broadcast_select_fusion.11
  15.1 0.6 collective-permute-start.1
  15.7 0.0 collective-permute-done.4
  15.7 1.7 %collective-permute-start.5 = (f32[16,512]{1,0:T(8,128)S(1)}, f32[16,512]{1,0:T(8,128)S(1)}, u32[]{:S(2)}, u32[]{:S(2)}) collective-permute-start(f32[16,512]{1,0:T(8,128)S(1)} %pad_maximum_fusion.6), channel_id=1, source_target_pairs={{0,32},{16,48},{32,0},{48,16},{64,96},{80,112},{96,64},{112,80},{1... | collective-permute-start | bytes 98312 | tf_op jit(solution)/shard_map/ppermute | solution.py:366
  17.4 0.4 collective-permute-done.1
  17.9 0.1 collective-permute-start.2
  18.0 0.9 collective-permute-done.5
  18.9 2.3 %collective-permute-start.6 = (f32[32,512]{1,0:T(8,128)S(1)}, f32[32,512]{1,0:T(8,128)S(1)}, u32[]{:S(2)}, u32[]{:S(2)}) collective-permute-start(f32[32,512]{1,0:T(8,128)S(1)} %pad_maximum_fusion.4), channel_id=1, source_target_pairs={{0,64},{16,80},{32,96},{48,112},{64,0},{80,16},{96,32},{112,48},{1... | collective-permute-start | bytes 196616 | tf_op jit(solution)/shard_map/ppermute | solution.py:366
  21.2 1.4 %collective-permute-done.2 = f32[32,512]{1,0:T(8,128)S(1)} collective-permute-done((f32[32,512]{1,0:T(8,128)S(1)}, f32[32,512]{1,0:T(8,128)S(1)}, u32[]{:S(2)}, u32[]{:S(2)}) %collective-permute-start.2) | collective-permute-done | bytes 65568 | tf_op jit(solution)/shard_map/ppermute | solution.py:365
  22.6 1.1 collective-permute-done.6
  23.7 0.7 pad_maximum_fusion.2.coef_ref
  24.4 0.6 broadcast_in_dim.2.ids_ref
  25.0 0.0 copy-done.1
  25.0 74.4 %robust_gradient.1 = (f32[64,512]{1,0:T(8,128)}, f32[64,512]{1,0:T(8,128)}) custom-call(s32[1]{0:T(128)} %bitcast.chan_ref, f32[32,8]{1,0:T(8,128)} %power_multiply_fusion.basis_ref, s32[8,256]{1,0:T(8,128)} %broadcast_in_dim.2.ids_ref, bf16[16,256]{1,0:T(8,128)(2,1)} %copy-done.1, bf16[256,16]{1,0:T(8,128)(2,1)} %bitcast.20, ...), custom_call_target="tpu_custom_call" | custom-call | flops 77309411328 | bytes 25165824 | tf_op jit(solution)/shard_map/robust_gradient/pallas_call | solution.py:281
  99.4 0.0 collective-permute-start.7
  99.4 5.5 %collective-permute-done.7 = f32[64,512]{1,0:T(8,128)S(1)} collective-permute-done((f32[64,512]{1,0:T(8,128)}, f32[64,512]{1,0:T(8,128)S(1)}, u32[]{:S(2)}, u32[]{:S(2)}) %collective-permute-start.7) | collective-permute-done | bytes 131104 | tf_op jit(solution)/shard_map/ppermute | solution.py:372
  104.9 0.9 add.455
  105.8 2.3 %collective-permute-start.8 = (f32[32,512]{1,0:T(8,128)S(1)}, f32[32,512]{1,0:T(8,128)S(1)}, u32[]{:S(2)}, u32[]{:S(2)}) collective-permute-start(f32[32,512]{1,0:T(8,128)S(1)} %slice_select_fusion), channel_id=1, source_target_pairs={{0,8},{1,65},{2,10},{3,67},{4,12},{5,69},{6,14},{7,71},{8,0},{9,73... | collective-permute-start | bytes 196616 | tf_op jit(solution)/shard_map/ppermute | solution.py:379
  108.1 2.4 %collective-permute-done.8 = f32[32,512]{1,0:T(8,128)S(1)} collective-permute-done((f32[32,512]{1,0:T(8,128)S(1)}, f32[32,512]{1,0:T(8,128)S(1)}, u32[]{:S(2)}, u32[]{:S(2)}) %collective-permute-start.8) | collective-permute-done | bytes 65568 | tf_op jit(solution)/shard_map/ppermute | solution.py:379
  110.6 1.6 %collective-permute-start.9 = (f32[16,512]{1,0:T(8,128)S(1)}, f32[16,512]{1,0:T(8,128)S(1)}, u32[]{:S(2)}, u32[]{:S(2)}) collective-permute-start(f32[16,512]{1,0:T(8,128)S(1)} %slice_select_fusion.1), channel_id=1, source_target_pairs={{0,4},{1,33},{2,6},{3,35},{4,0},{5,37},{6,2},{7,39},{8,12},{9,41},... | collective-permute-start | bytes 98312 | tf_op jit(solution)/shard_map/ppermute | solution.py:379
  112.2 1.3 collective-permute-done.9
  113.5 6.2 %collective-permute-start.10 = (f32[8,512]{1,0:T(8,128)S(1)}, f32[8,512]{1,0:T(8,128)S(1)}, u32[]{:S(2)}, u32[]{:S(2)}) collective-permute-start(f32[8,512]{1,0:T(8,128)S(1)} %slice_select_fusion.2), channel_id=1, source_target_pairs={{0,2},{1,17},{2,0},{3,19},{4,6},{5,21},{6,4},{7,23},{8,10},{9,25},... | collective-permute-start | bytes 49160 | tf_op jit(solution)/shard_map/ppermute | solution.py:379
  119.8 0.8 collective-permute-done.10
  120.6 5.2 %collective-permute-start.11 = (f32[8,512]{1,0:T(8,128)S(1)}, f32[8,512]{1,0:T(8,128)S(1)}, u32[]{:S(2)}, u32[]{:S(2)}) collective-permute-start(f32[8,512]{1,0:T(8,128)S(1)} %select_add_fusion.2), channel_id=1, source_target_pairs={{0,1},{1,0},{2,3},{3,16},{4,5},{5,32},{6,7},{7,48},{8,9},{9,64},{1... | collective-permute-start | bytes 49160 | tf_op jit(solution)/shard_map/ppermute | solution.py:380
  125.8 1.9 %collective-permute-start.12 = (f32[8,512]{1,0:T(8,128)S(1)}, f32[8,512]{1,0:T(8,128)S(1)}, u32[]{:S(2)}, u32[]{:S(2)}) collective-permute-start(f32[8,512]{1,0:T(8,128)S(1)} %select_add_fusion.2), channel_id=1, source_target_pairs={{0,0},{1,1},{2,16},{3,17},{4,32},{5,33},{6,48},{7,49},{8,64},{9,65... | collective-permute-start | bytes 49160 | tf_op jit(solution)/shard_map/ppermute | solution.py:381
  127.7 0.0 collective-permute-done.11
  127.7 7.9 %collective-permute-done.12 = f32[8,512]{1,0:T(8,128)S(1)} collective-permute-done((f32[8,512]{1,0:T(8,128)S(1)}, f32[8,512]{1,0:T(8,128)S(1)}, u32[]{:S(2)}, u32[]{:S(2)}) %collective-permute-start.12) | collective-permute-done | bytes 16416 | tf_op jit(solution)/shard_map/ppermute | solution.py:381
  135.7 0.6 add_select_fusion
  (24 shorter events, 0.2 us)
Async XLA Ops:
  0.0 9.5 %copy-start = (f32[256,64]{0,1:T(8,128)S(1)}, f32[256,64]{0,1:T(8,128)}, u32[]{:S(2)}) copy-start(f32[256,64]{0,1:T(8,128)} %param.13) | copy-start | bytes 196612
  0.0 14.1 %collective-permute-start.3 = (f32[8,512]{1,0:T(8,128)}, f32[8,512]{1,0:T(8,128)S(1)}, u32[]{:S(2)}, u32[]{:S(2)}) collective-permute-start(f32[8,512]{1,0:T(8,128)} %param.10), channel_id=1, source_target_pairs={{0,0},{2,16},{4,32},{6,48},{8,64},{10,80},{12,96},{14,112},{16,2},... | collective-permute-start | bytes 49160 | tf_op jit(solution)/shard_map/ppermute | solution.py:363
  6.2 8.2 %collective-permute-start = (f32[8,512]{1,0:T(8,128)}, f32[8,512]{1,0:T(8,128)S(1)}, u32[]{:S(2)}, u32[]{:S(2)}) collective-permute-start(f32[8,512]{1,0:T(8,128)} %param.10), channel_id=1, source_target_pairs={{0,2},{2,0},{4,6},{6,4},{8,10},{10,8},{12,14},{14,12},{1,3},{3,1},... | collective-permute-start | bytes 49160 | tf_op jit(solution)/shard_map/ppermute | solution.py:365
  7.0 18.0 %copy-start.1 = (bf16[16,256]{1,0:T(8,128)(2,1)}, bf16[16,256]{1,0:T(8,128)(2,1)S(1)}, u32[]{:S(2)}) copy-start(bf16[16,256]{1,0:T(8,128)(2,1)S(1)} %fusion.12.hot_ref) | copy-start | bytes 24580
  14.1 1.6 %collective-permute-start.4 = (f32[8,512]{1,0:T(8,128)S(1)}, f32[8,512]{1,0:T(8,128)S(1)}, u32[]{:S(2)}, u32[]{:S(2)}) collective-permute-start(f32[8,512]{1,0:T(8,128)S(1)} %collective-permute-done.3), channel_id=1, source_target_pairs={{0,16},{16,0},{32,48},{48,32},{64,80},{80,64},{96,112},{112,96},{1... | collective-permute-start | bytes 49160 | tf_op jit(solution)/shard_map/ppermute | solution.py:366
  15.1 2.8 %collective-permute-start.1 = (f32[16,512]{1,0:T(8,128)S(1)}, f32[16,512]{1,0:T(8,128)S(1)}, u32[]{:S(2)}, u32[]{:S(2)}) collective-permute-start(f32[16,512]{1,0:T(8,128)S(1)} %pad_maximum_fusion.5), channel_id=1, source_target_pairs={{0,4},{2,6},{4,0},{6,2},{8,12},{10,14},{12,8},{14,10},{1,5},{3,7},... | collective-permute-start | bytes 98312 | tf_op jit(solution)/shard_map/ppermute | solution.py:365
  15.7 3.2 %collective-permute-start.5 = (f32[16,512]{1,0:T(8,128)S(1)}, f32[16,512]{1,0:T(8,128)S(1)}, u32[]{:S(2)}, u32[]{:S(2)}) collective-permute-start(f32[16,512]{1,0:T(8,128)S(1)} %pad_maximum_fusion.6), channel_id=1, source_target_pairs={{0,32},{16,48},{32,0},{48,16},{64,96},{80,112},{96,64},{112,80},{1... | collective-permute-start | bytes 98312 | tf_op jit(solution)/shard_map/ppermute | solution.py:366
  17.9 4.7 %collective-permute-start.2 = (f32[32,512]{1,0:T(8,128)S(1)}, f32[32,512]{1,0:T(8,128)S(1)}, u32[]{:S(2)}, u32[]{:S(2)}) collective-permute-start(f32[32,512]{1,0:T(8,128)S(1)} %pad_maximum_fusion.3), channel_id=1, source_target_pairs={{0,8},{2,10},{4,12},{6,14},{8,0},{10,2},{12,4},{14,6},{1,9},{3,11}... | collective-permute-start | bytes 196616 | tf_op jit(solution)/shard_map/ppermute | solution.py:365
  18.9 4.7 %collective-permute-start.6 = (f32[32,512]{1,0:T(8,128)S(1)}, f32[32,512]{1,0:T(8,128)S(1)}, u32[]{:S(2)}, u32[]{:S(2)}) collective-permute-start(f32[32,512]{1,0:T(8,128)S(1)} %pad_maximum_fusion.4), channel_id=1, source_target_pairs={{0,64},{16,80},{32,96},{48,112},{64,0},{80,16},{96,32},{112,48},{1... | collective-permute-start | bytes 196616 | tf_op jit(solution)/shard_map/ppermute | solution.py:366
  99.4 5.5 %collective-permute-start.7 = (f32[64,512]{1,0:T(8,128)}, f32[64,512]{1,0:T(8,128)S(1)}, u32[]{:S(2)}, u32[]{:S(2)}) collective-permute-start(f32[64,512]{1,0:T(8,128)} %get-tuple-element.8), channel_id=1, source_target_pairs={{0,1},{1,0},{2,3},{3,2},{4,5},{5,4},{6,7},{7,6},{8,9},{9,8},{10,11... | collective-permute-start | bytes 393224 | tf_op jit(solution)/shard_map/ppermute | solution.py:372
  105.8 4.7 %collective-permute-start.8 = (f32[32,512]{1,0:T(8,128)S(1)}, f32[32,512]{1,0:T(8,128)S(1)}, u32[]{:S(2)}, u32[]{:S(2)}) collective-permute-start(f32[32,512]{1,0:T(8,128)S(1)} %slice_select_fusion), channel_id=1, source_target_pairs={{0,8},{1,65},{2,10},{3,67},{4,12},{5,69},{6,14},{7,71},{8,0},{9,73... | collective-permute-start | bytes 196616 | tf_op jit(solution)/shard_map/ppermute | solution.py:379
  110.6 2.9 %collective-permute-start.9 = (f32[16,512]{1,0:T(8,128)S(1)}, f32[16,512]{1,0:T(8,128)S(1)}, u32[]{:S(2)}, u32[]{:S(2)}) collective-permute-start(f32[16,512]{1,0:T(8,128)S(1)} %slice_select_fusion.1), channel_id=1, source_target_pairs={{0,4},{1,33},{2,6},{3,35},{4,0},{5,37},{6,2},{7,39},{8,12},{9,41},... | collective-permute-start | bytes 98312 | tf_op jit(solution)/shard_map/ppermute | solution.py:379
  113.5 7.1 %collective-permute-start.10 = (f32[8,512]{1,0:T(8,128)S(1)}, f32[8,512]{1,0:T(8,128)S(1)}, u32[]{:S(2)}, u32[]{:S(2)}) collective-permute-start(f32[8,512]{1,0:T(8,128)S(1)} %slice_select_fusion.2), channel_id=1, source_target_pairs={{0,2},{1,17},{2,0},{3,19},{4,6},{5,21},{6,4},{7,23},{8,10},{9,25},... | collective-permute-start | bytes 49160 | tf_op jit(solution)/shard_map/ppermute | solution.py:379
  120.6 7.1 %collective-permute-start.11 = (f32[8,512]{1,0:T(8,128)S(1)}, f32[8,512]{1,0:T(8,128)S(1)}, u32[]{:S(2)}, u32[]{:S(2)}) collective-permute-start(f32[8,512]{1,0:T(8,128)S(1)} %select_add_fusion.2), channel_id=1, source_target_pairs={{0,1},{1,0},{2,3},{3,16},{4,5},{5,32},{6,7},{7,48},{8,9},{9,64},{1... | collective-permute-start | bytes 49160 | tf_op jit(solution)/shard_map/ppermute | solution.py:380
  125.8 9.9 %collective-permute-start.12 = (f32[8,512]{1,0:T(8,128)S(1)}, f32[8,512]{1,0:T(8,128)S(1)}, u32[]{:S(2)}, u32[]{:S(2)}) collective-permute-start(f32[8,512]{1,0:T(8,128)S(1)} %select_add_fusion.2), channel_id=1, source_target_pairs={{0,0},{1,1},{2,16},{3,17},{4,32},{5,33},{6,48},{7,49},{8,64},{9,65... | collective-permute-start | bytes 49160 | tf_op jit(solution)/shard_map/ppermute | solution.py:381

commit v5 on v4

--- a/solution.py
+++ b/solution.py
@@ -71,7 +71,7 @@
     return dot_nn(a[0], b[0]) + dot_nn(a[1], b[0]) + dot_nn(a[0], b[1])
 
 
-def kernel(chan_ref, basis_ref, ids_ref, hot_ref, hott_ref, coef_ref, flux_ref, begin_ref, turn_ref, vis_ref, flag_ref, kept_ref, sent_ref, ct_ref, cq_ref, jn0_ref, jn1_ref, jt0_ref, jt1_ref, x0h, x0l, x1h, x1l,
+def kernel(basis_ref, ids_ref, hot_ref, hott_ref, coef_ref, flux_ref, begin_ref, turn_ref, vis_ref, flag_ref, row_ref, col_ref, ct_ref, cq_ref, jn0_ref, jn1_ref, jt0_ref, jt1_ref, x0h, x0l, x1h, x1l,
            w0h, w0l, w1h, w1l, dp0_ref, dp1_ref, dq0_ref, dq1_ref, acc_ref, pair_ref,
            e0_ref, e1_ref, f0_ref, f1_ref, wide_ref):
     step = pl.program_id(0)
@@ -261,17 +261,15 @@
                     [acc_ref[b, 0, :, first:first + RB], acc_ref[b, 1, :, e * RB:(e + 1) * RB]], axis=1
                 )
         turned = ct_ref[...].T
-        first_chan = chan_ref[0] == 0
+        col_ref[...] = turned[64:128]
         for part in range(4):
             lanes = slice(part * 128, (part + 1) * 128)
             pair_ref[part, pl.ds(0, 32, stride=2), :] = turned[0:32, lanes]
             pair_ref[part, pl.ds(1, 32, stride=2), :] = turned[32:64, lanes]
-            row_part, col_part = pair_ref[part], turned[64:128, lanes]
-            kept_ref[:, lanes] = jnp.where(first_chan, row_part, col_part)
-            sent_ref[:, lanes] = jnp.where(first_chan, col_part, row_part)
-
-
-def gradient_call(chan, basis, ids, hot, coef, flux, begin, turn, vis, flag):
+            row_ref[:, lanes] = pair_ref[part]
+
+
+def gradient_call(basis, ids, hot, coef, flux, begin, turn, vis, flag):
     chans = basis.shape[0]
     const = lambda shape: pl.BlockSpec(shape, lambda f: (0,) * len(shape))
     hott = jnp.concatenate([hot[0:8], hot[0:8]], axis=0).T
@@ -282,7 +280,6 @@
         kernel,
         grid=(chans // 2,),
         in_specs=[
-            pl.BlockSpec(memory_space=pltpu.SMEM),
             pl.BlockSpec(memory_space=pltpu.SMEM),
             const((8, NSRC)),
             const((16, NSRC)),
@@ -321,7 +318,7 @@
             flops=2 * 3 * 6 * 128 * 1024 * 256 * T_SMP * chans, bytes_accessed=24 * 1024 * 1024, transcendentals=0
         ),
         name="robust_gradient",
-    )(chan, basis, ids, hot, hott, coef, flux, begin, turn, vis, flag)
+    )(basis, ids, hot, hott, coef, flux, begin, turn, vis, flag)
 
 
 CROSS = [(r * 8 + c, c * 8 + r) for r in range(8) for c in range(8)]
@@ -330,11 +327,6 @@
 def merge(held, other, axis, bit):
     upper = (lax.axis_index(axis) & bit) != 0
     return jnp.concatenate([jnp.where(upper, other, held), jnp.where(upper, held, other)], axis=0)
-
-
-def pairs(target):
-    index = lambda r, c, h: (r * 8 + c) * 2 + h
-    return [(index(r, c, h), index(*target(r, c, h))) for r in range(8) for c in range(8) for h in range(2)]
 
 
 def per_device(visibility, flags, coeffs, station_uv, source_lm, source_flux, cluster_ids):
@@ -344,6 +336,17 @@
     chan_start = lax.axis_index("chan") * chans
     channels = chan_start + jnp.arange(chans)
 
+    flux = lax.dynamic_slice_in_dim(source_flux, chan_start, chans, 1).T
+    ids = jnp.broadcast_to(cluster_ids[None] * 8, (8, NSRC))
+    hot = (cluster_ids[None] == jnp.arange(16)[:, None]).astype(bf16)
+
+    vis = visibility.reshape(8, T_SMP, chans, BLK)
+    flag = flags.reshape(T_SMP, chans, 32, 128)
+
+    row_coef = coeffs
+    col_coef = lax.ppermute(coeffs, ("row", "col"), CROSS)
+    station_uv, chan_start = lax.optimization_barrier((station_uv, chan_start, col_coef))[:2]
+    channels = chan_start + jnp.arange(chans)
     basis = bernstein(channels, NB)
     row_uv = lax.dynamic_slice_in_dim(station_uv, row * RB, RB, 2)
     row_uv = row_uv.reshape(2, T_SMP, 32, 2).transpose(0, 1, 3, 2).reshape(2, T_SMP, RB)
@@ -352,34 +355,15 @@
     geo = uv[0][..., None] * source_lm[0] + uv[1][..., None] * source_lm[1]
     begin = jnp.stack(phasors(frequency(chan_start) * geo))
     turn = jnp.stack(phasors((0.5 / F) * geo))
-    flux = lax.dynamic_slice_in_dim(source_flux, chan_start, chans, 1).T
-    ids = jnp.broadcast_to(cluster_ids[None] * 8, (8, NSRC))
-    hot = (cluster_ids[None] == jnp.arange(16)[:, None]).astype(bf16)
-
-    vis = visibility.reshape(8, T_SMP, chans, BLK)
-    flag = flags.reshape(T_SMP, chans, 32, 128)
-
-    row_coef = coeffs
-    col_coef = lax.ppermute(coeffs, ("row", "col"), CROSS)
     for bit in (1, 2, 4):
         row_coef = merge(row_coef, lax.ppermute(row_coef, "col", [(c, c ^ bit) for c in range(8)]), "col", bit)
         col_coef = merge(col_coef, lax.ppermute(col_coef, "row", [(r, r ^ bit) for r in range(8)]), "row", bit)
     coef = jnp.stack([row_coef, col_coef])
 
-    chan = lax.axis_index("chan")
-    kept, sent = gradient_call(chan.reshape(1), basis, ids, hot, coef, flux, begin, turn, vis, flag)
-    axes = ("row", "col", "chan")
-    held = kept + lax.ppermute(sent, axes, pairs(lambda r, c, h: (r, c, 1 - h)))
-    place = jnp.where(chan == 0, col, row)
-    for bit in (4, 2, 1):
-        half = held.shape[0] // 2
-        upper = (place & bit) != 0
-        low, high = held[:half], held[half:]
-        partner = pairs(lambda r, c, h: (r, c ^ bit, h) if h == 0 else (r ^ bit, c, h))
-        held = jnp.where(upper, high, low) + lax.ppermute(jnp.where(upper, low, high), axes, partner)
-    other = lax.ppermute(held, axes, pairs(lambda r, c, h: (r, c, 1) if h == 0 else (c, r, 0)))
-    crossed = lax.ppermute(held, axes, pairs(lambda r, c, h: (c, r, h)))
-    return jnp.where(chan == 0, held + other, other + crossed)
+    row_part, col_part = gradient_call(basis, ids, hot, coef, flux, begin, turn, vis, flag)
+    part = row_part + lax.ppermute(col_part, ("row", "col"), CROSS)
+    part = jnp.broadcast_to(part.reshape(8, 1, 8, 512), (8, 2, 8, 512)).reshape(16, 8, 512)
+    return lax.all_to_all(part, ("col", "chan"), 0, 0, tiled=True).sum(0)
 
 
 def solution(mesh):

time: 137 us -> 134 us (0.978)
  the two profiles are of different devices: /device:TPU:81 before, /device:TPU:0 now
where the time goes in v5:
time: 134 us
  Pallas kernels  74.4 us (56%)
  blocking collectives  28 us (21%)
  starting transfers between devices  16 us (12%)
  other arithmetic  7.69 us (6%)
  waiting for transfers between devices  4.07 us (3%)
  local copies, waits for them, and re-layouts  3.83 us (3%)
    pallas_call x1, Pallas kernels, gradient_call(): pl.pallas_call(kernel, grid=(chans // 2,), in_specs=[pl.BlockSpec(memory_...  74.4 us
    all_to_all x1, blocking collectives, per_device(): return lax.all_to_all(part, ('col', 'chan'), 0, 0, tiled=True).sum(0)  28 us
    ppermute x3, starting transfers between devices, per_device(): lax.ppermute(row_coef, 'col', [(c, c ^ bit) for c in range(8)])  9.76 us
    ppermute x3, waiting for transfers between devices, per_device(): lax.ppermute(col_coef, 'row', [(r, r ^ bit) for r in range(8)])  3.46 us
    ppermute x3, starting transfers between devices, per_device(): lax.ppermute(col_coef, 'row', [(r, r ^ bit) for r in range(8)])  3.16 us
  transfers between devices with their start and end apart: 8, of which 2 were waited for; matrix products, arithmetic and copies ran while one was open for 6% of the time, Pallas kernels for 0%

profile of v5, /device:TPU:0, one launch (start us, length us, event | category | flops | bytes accessed | tf_op | source)
XLA Modules:
  0.0 134.0 jit_solution(6165015486859289725)
XLA Ops:
  0.0 0.0 copy-start
  0.0 1.5 %collective-permute-start = (f32[8,512]{1,0:T(8,128)}, f32[8,512]{1,0:T(8,128)S(1)}, u32[]{:S(2)}, u32[]{:S(2)}) collective-permute-start(f32[8,512]{1,0:T(8,128)} %param.10), channel_id=1, source_target_pairs={{0,0},{2,16},{4,32},{6,48},{8,64},{10,80},{12,96},{14,112},{16,2},... | collective-permute-start | bytes 49160 | tf_op jit(solution)/shard_map/ppermute | solution.py:347
  1.5 2.6 %collective-permute-start.1 = (f32[8,512]{1,0:T(8,128)}, f32[8,512]{1,0:T(8,128)S(1)}, u32[]{:S(2)}, u32[]{:S(2)}) collective-permute-start(f32[8,512]{1,0:T(8,128)} %param.10), channel_id=1, source_target_pairs={{0,2},{2,0},{4,6},{6,4},{8,10},{10,8},{12,14},{14,12},{1,3},{3,1},... | collective-permute-start | bytes 49160 | tf_op jit(solution)/shard_map/ppermute | solution.py:359
  4.1 0.7 fusion.12.hot_ref
  4.8 0.0 copy-start.1
  4.8 0.7 broadcast_multiply_fusion
  5.5 0.8 fusion.16
  6.3 0.0 copy-done
  6.3 0.6 dynamic-slice_bitcast_fusion.flux_ref
  6.9 0.7 copy.24
  7.6 0.0 collective-permute-done
  7.6 0.8 constant_dynamic-slice_fusion
  8.4 0.1 reshape.276
  8.6 0.1 copy.25
  8.7 0.1 stack_reshape.3
  8.8 0.0 collective-permute-done.1
  8.8 0.7 broadcast_select_fusion.11
  9.5 1.9 %collective-permute-start.2 = (f32[16,512]{1,0:T(8,128)S(1)}, f32[16,512]{1,0:T(8,128)S(1)}, u32[]{:S(2)}, u32[]{:S(2)}) collective-permute-start(f32[16,512]{1,0:T(8,128)S(1)} %pad_maximum_fusion.5), channel_id=1, source_target_pairs={{0,4},{2,6},{4,0},{6,2},{8,12},{10,14},{12,8},{14,10},{1,5},{3,7},... | collective-permute-start | bytes 98312 | tf_op jit(solution)/shard_map/ppermute | solution.py:359
  11.4 0.7 fusion.1
  12.1 1.4 %power_multiply_fusion.basis_ref = f32[32,8]{1,0:T(8,128)} fusion(f32[8]{0:T(128)} %constant.83.clone, f32[8]{0:T(128)S(1)} %broadcast_subtract_fusion, f32[32]{0:T(128)S(1)} %get-tuple-element.36, f32[8]{0:T(128)S(1)} %iota_convert_fusion, f32[32]{0:T(128)S(1)} %get-tuple-element.35), kind=kLoop, calls=%fused_computation.47 | loop fusion | flops 512 | bytes 1376 | tf_op jit(solution)/shard_map/mul | solution.py:32
  13.5 0.3 collective-permute-start.4
  13.8 1.1 pad_maximum_fusion
  14.9 0.0 collective-permute-done.4
  14.9 1.1 collective-permute-start.5
  16.0 0.0 collective-permute-done.2
  16.0 5.3 %collective-permute-start.3 = (f32[32,512]{1,0:T(8,128)S(1)}, f32[32,512]{1,0:T(8,128)S(1)}, u32[]{:S(2)}, u32[]{:S(2)}) collective-permute-start(f32[32,512]{1,0:T(8,128)S(1)} %pad_maximum_fusion.3), channel_id=1, source_target_pairs={{0,8},{2,10},{4,12},{6,14},{8,0},{10,2},{12,4},{14,6},{1,9},{3,11}... | collective-permute-start | bytes 196616 | tf_op jit(solution)/shard_map/ppermute | solution.py:359
  21.3 0.0 collective-permute-done.5
  21.3 1.8 %collective-permute-start.6 = (f32[32,512]{1,0:T(8,128)S(1)}, f32[32,512]{1,0:T(8,128)S(1)}, u32[]{:S(2)}, u32[]{:S(2)}) collective-permute-start(f32[32,512]{1,0:T(8,128)S(1)} %pad_maximum_fusion.4), channel_id=1, source_target_pairs={{0,64},{16,80},{32,96},{48,112},{64,0},{80,16},{96,32},{112,48},{1... | collective-permute-start | bytes 196616 | tf_op jit(solution)/shard_map/ppermute | solution.py:360
  23.1 0.6 collective-permute-done.3
  23.7 3.5 %collective-permute-done.6 = f32[32,512]{1,0:T(8,128)S(1)} collective-permute-done((f32[32,512]{1,0:T(8,128)S(1)}, f32[32,512]{1,0:T(8,128)S(1)}, u32[]{:S(2)}, u32[]{:S(2)}) %collective-permute-start.6) | collective-permute-done | bytes 65568 | tf_op jit(solution)/shard_map/ppermute | solution.py:360
  27.2 0.7 pad_maximum_fusion.2.coef_ref
  27.9 0.6 broadcast_in_dim.6.ids_ref
  28.5 0.0 copy-done.1
  28.5 74.4 %robust_gradient.1 = (f32[64,512]{1,0:T(8,128)}, f32[64,512]{1,0:T(8,128)}) custom-call(f32[32,8]{1,0:T(8,128)} %power_multiply_fusion.basis_ref, s32[8,256]{1,0:T(8,128)} %broadcast_in_dim.6.ids_ref, bf16[16,256]{1,0:T(8,128)(2,1)} %copy-done.1, bf16[256,16]{1,0:T(8,128)(2,1)} %bitcast.23, f32[2,64,512]{2,1,0:T(8,128)} %pad_maximum_fusion.2.coef_ref, ...), custom_call_target="tpu_custom_call" | custom-call | flops 77309411328 | bytes 25165824 | tf_op jit(solution)/shard_map/robust_gradient/pallas_call | solution.py:279
  102.9 1.6 %collective-permute-start.7 = (f32[64,512]{1,0:T(8,128)}, f32[64,512]{1,0:T(8,128)S(1)}, u32[]{:S(2)}, u32[]{:S(2)}) collective-permute-start(f32[64,512]{1,0:T(8,128)} %get-tuple-element.12), channel_id=1, source_target_pairs={{0,0},{2,16},{4,32},{6,48},{8,64},{10,80},{12,96},{14,112},{16,2},... | collective-permute-start | bytes 393224 | tf_op jit(solution)/shard_map/ppermute | solution.py:364
  104.4 0.0 collective-permute-done.7
  104.4 0.9 add_bitcast_fusion
  105.4 28.0 %all_to_all.5 = f32[16,8,512]{2,1,0:T(8,128)S(1)} all-to-all(f32[16,8,512]{2,1,0:T(8,128)S(1)} %bitcast.21), channel_id=1, replica_groups=mesh['row'=8,'col'=8,'chan'=2] {'col','chan'}, dimensions={0} | all-to-all | bytes 524288 | tf_op jit(solution)/shard_map/all_to_all | solution.py:366
  133.4 0.6 reduce_sum.9
  (19 shorter events, 0.1 us)
Async XLA Ops:
  0.0 6.3 %copy-start = (f32[256,64]{0,1:T(8,128)S(1)}, f32[256,64]{0,1:T(8,128)}, u32[]{:S(2)}) copy-start(f32[256,64]{0,1:T(8,128)} %param.13) | copy-start | bytes 196612
  0.0 7.6 %collective-permute-start = (f32[8,512]{1,0:T(8,128)}, f32[8,512]{1,0:T(8,128)S(1)}, u32[]{:S(2)}, u32[]{:S(2)}) collective-permute-start(f32[8,512]{1,0:T(8,128)} %param.10), channel_id=1, source_target_pairs={{0,0},{2,16},{4,32},{6,48},{8,64},{10,80},{12,96},{14,112},{16,2},... | collective-permute-start | bytes 49160 | tf_op jit(solution)/shard_map/ppermute | solution.py:347
  1.5 7.3 %collective-permute-start.1 = (f32[8,512]{1,0:T(8,128)}, f32[8,512]{1,0:T(8,128)S(1)}, u32[]{:S(2)}, u32[]{:S(2)}) collective-permute-start(f32[8,512]{1,0:T(8,128)} %param.10), channel_id=1, source_target_pairs={{0,2},{2,0},{4,6},{6,4},{8,10},{10,8},{12,14},{14,12},{1,3},{3,1},... | collective-permute-start | bytes 49160 | tf_op jit(solution)/shard_map/ppermute | solution.py:359
  4.8 23.7 %copy-start.1 = (bf16[16,256]{1,0:T(8,128)(2,1)}, bf16[16,256]{1,0:T(8,128)(2,1)S(1)}, u32[]{:S(2)}) copy-start(bf16[16,256]{1,0:T(8,128)(2,1)S(1)} %fusion.12.hot_ref) | copy-start | bytes 24580
  9.5 6.5 %collective-permute-start.2 = (f32[16,512]{1,0:T(8,128)S(1)}, f32[16,512]{1,0:T(8,128)S(1)}, u32[]{:S(2)}, u32[]{:S(2)}) collective-permute-start(f32[16,512]{1,0:T(8,128)S(1)} %pad_maximum_fusion.5), channel_id=1, source_target_pairs={{0,4},{2,6},{4,0},{6,2},{8,12},{10,14},{12,8},{14,10},{1,5},{3,7},... | collective-permute-start | bytes 98312 | tf_op jit(solution)/shard_map/ppermute | solution.py:359
  13.5 1.4 %collective-permute-start.4 = (f32[8,512]{1,0:T(8,128)S(1)}, f32[8,512]{1,0:T(8,128)S(1)}, u32[]{:S(2)}, u32[]{:S(2)}) collective-permute-start(f32[8,512]{1,0:T(8,128)S(1)} %collective-permute-done), channel_id=1, source_target_pairs={{0,16},{16,0},{32,48},{48,32},{64,80},{80,64},{96,112},{112,96},{1... | collective-permute-start | bytes 49160 | tf_op jit(solution)/shard_map/ppermute | solution.py:360
  14.9 6.3 %collective-permute-start.5 = (f32[16,512]{1,0:T(8,128)S(1)}, f32[16,512]{1,0:T(8,128)S(1)}, u32[]{:S(2)}, u32[]{:S(2)}) collective-permute-start(f32[16,512]{1,0:T(8,128)S(1)} %pad_maximum_fusion.6), channel_id=1, source_target_pairs={{0,32},{16,48},{32,0},{48,16},{64,96},{80,112},{96,64},{112,80},{1... | collective-permute-start | bytes 98312 | tf_op jit(solution)/shard_map/ppermute | solution.py:360
  16.0 7.7 %collective-permute-start.3 = (f32[32,512]{1,0:T(8,128)S(1)}, f32[32,512]{1,0:T(8,128)S(1)}, u32[]{:S(2)}, u32[]{:S(2)}) collective-permute-start(f32[32,512]{1,0:T(8,128)S(1)} %pad_maximum_fusion.3), channel_id=1, source_target_pairs={{0,8},{2,10},{4,12},{6,14},{8,0},{10,2},{12,4},{14,6},{1,9},{3,11}... | collective-permute-start | bytes 196616 | tf_op jit(solution)/shard_map/ppermute | solution.py:359
  21.3 5.8 %collective-permute-start.6 = (f32[32,512]{1,0:T(8,128)S(1)}, f32[32,512]{1,0:T(8,128)S(1)}, u32[]{:S(2)}, u32[]{:S(2)}) collective-permute-start(f32[32,512]{1,0:T(8,128)S(1)} %pad_maximum_fusion.4), channel_id=1, source_target_pairs={{0,64},{16,80},{32,96},{48,112},{64,0},{80,16},{96,32},{112,48},{1... | collective-permute-start | bytes 196616 | tf_op jit(solution)/shard_map/ppermute | solution.py:360
  102.9 1.6 %collective-permute-start.7 = (f32[64,512]{1,0:T(8,128)}, f32[64,512]{1,0:T(8,128)S(1)}, u32[]{:S(2)}, u32[]{:S(2)}) collective-permute-start(f32[64,512]{1,0:T(8,128)} %get-tuple-element.12), channel_id=1, source_target_pairs={{0,0},{2,16},{4,32},{6,48},{8,64},{10,80},{12,96},{14,112},{16,2},... | collective-permute-start | bytes 393224 | tf_op jit(solution)/shard_map/ppermute | solution.py:364

commit v6 on v5

--- a/solution.py
+++ b/solution.py
@@ -343,9 +343,14 @@
     vis = visibility.reshape(8, T_SMP, chans, BLK)
     flag = flags.reshape(T_SMP, chans, 32, 128)
 
-    row_coef = coeffs
-    col_coef = lax.ppermute(coeffs, ("row", "col"), CROSS)
-    station_uv, chan_start = lax.optimization_barrier((station_uv, chan_start, col_coef))[:2]
+    row_four = [coeffs] + [lax.ppermute(coeffs, "col", [(c, c ^ m) for c in range(8)]) for m in range(1, 4)]
+    col_four = [
+        lax.ppermute(coeffs, ("row", "col"), [(a * 8 + b, (b ^ m) * 8 + a) for a in range(8) for b in range(8)])
+        for m in range(4)
+    ]
+    row_coef = merge(merge(*row_four[:2], "col", 1), merge(*row_four[2:], "col", 1), "col", 2)
+    col_coef = merge(merge(*col_four[:2], "row", 1), merge(*col_four[2:], "row", 1), "row", 2)
+    station_uv, chan_start = lax.optimization_barrier((station_uv, chan_start, row_coef))[:2]
     channels = chan_start + jnp.arange(chans)
     basis = bernstein(channels, NB)
     row_uv = lax.dynamic_slice_in_dim(station_uv, row * RB, RB, 2)
@@ -355,9 +360,8 @@
     geo = uv[0][..., None] * source_lm[0] + uv[1][..., None] * source_lm[1]
     begin = jnp.stack(phasors(frequency(chan_start) * geo))
     turn = jnp.stack(phasors((0.5 / F) * geo))
-    for bit in (1, 2, 4):
-        row_coef = merge(row_coef, lax.ppermute(row_coef, "col", [(c, c ^ bit) for c in range(8)]), "col", bit)
-        col_coef = merge(col_coef, lax.ppermute(col_coef, "row", [(r, r ^ bit) for r in range(8)]), "row", bit)
+    row_coef = merge(row_coef, lax.ppermute(row_coef, "col", [(c, c ^ 4) for c in range(8)]), "col", 4)
+    col_coef = merge(col_coef, lax.ppermute(col_coef, "row", [(r, r ^ 4) for r in range(8)]), "row", 4)
     coef = jnp.stack([row_coef, col_coef])
 
     row_part, col_part = gradient_call(basis, ids, hot, coef, flux, begin, turn, vis, flag)

time: 134 us -> 139 us (1.037)
  starting transfers between devices: 16 us -> 26.9 us
  waiting for transfers between devices: 4.07 us -> 0.03 us
  blocking collectives: 28 us -> 26 us
    ppermute x7 -> x9, starting transfers between devices: 14.4 us -> 25.3 us  [the longest x1 12.7 us: per_device(): lax.ppermute(row_coef, 'col', [(c, c ^ 4) for c in range(8)])]
    ppermute x7 -> x9, waiting for transfers between devices: 4.06 us -> 0.02 us  [the longest x4 0.01 us: per_device(): lax.ppermute(coeffs, ('row', 'col'), [(a * 8 + b, (b ^ m) * 8 + a) for a...]
    all_to_all x1, blocking collectives: 28 us -> 26 us  [per_device(): return lax.all_to_all(part, ('col', 'chan'), 0, 0, tiled=True).sum(0)]
  transfers between devices with their start and end apart: 8 -> 10, of which waited for: 2 -> 0; matrix products, arithmetic and copies ran while one was open for 6% -> 6% of each run, Pallas kernels for 0% -> 0%
where the time goes in v6:
time: 139 us
  Pallas kernels  74.4 us (54%)
  starting transfers between devices  26.9 us (19%)
  blocking collectives  26 us (19%)
  other arithmetic  7.73 us (6%)
  local copies, waits for them, and re-layouts  3.84 us (3%)
    pallas_call x1, Pallas kernels, gradient_call(): pl.pallas_call(kernel, grid=(chans // 2,), in_specs=[pl.BlockSpec(memory_...  74.4 us
    all_to_all x1, blocking collectives, per_device(): return lax.all_to_all(part, ('col', 'chan'), 0, 0, tiled=True).sum(0)  26 us
    ppermute x1, starting transfers between devices, per_device(): lax.ppermute(row_coef, 'col', [(c, c ^ 4) for c in range(8)])  12.7 us
    ppermute x4, starting transfers between devices, per_device(): lax.ppermute(coeffs, ('row', 'col'), [(a * 8 + b, (b ^ m) * 8 + a) for a...  5.36 us
    ppermute x3, starting transfers between devices, per_device(): lax.ppermute(coeffs, 'col', [(c, c ^ m) for c in range(8)])  3.66 us
    ppermute x1, starting transfers between devices, per_device(): lax.ppermute(col_coef, 'row', [(r, r ^ 4) for r in range(8)])  3.56 us
  transfers between devices with their start and end apart: 10, of which 0 were waited for; matrix products, arithmetic and copies ran while one was open for 6% of the time, Pallas kernels for 0%

profile of v6, /device:TPU:0, one launch (start us, length us, event | category | flops | bytes accessed | tf_op | source)
XLA Modules:
  0.0 138.9 jit_solution(13131662333930425857)
XLA Ops:
  0.0 0.0 copy-start
  0.0 3.0 %collective-permute-start = (f32[8,512]{1,0:T(8,128)}, f32[8,512]{1,0:T(8,128)S(1)}, u32[]{:S(2)}, u32[]{:S(2)}) collective-permute-start(f32[8,512]{1,0:T(8,128)} %param.10), channel_id=1, source_target_pairs={{0,6},{2,4},{4,2},{6,0},{8,14},{10,12},{12,10},{14,8},{1,7},{3,5},... | collective-permute-start | bytes 49160 | tf_op jit(solution)/shard_map/ppermute | solution.py:346
  3.0 0.5 collective-permute-start.1
  3.5 0.2 collective-permute-start.2
  3.7 0.4 collective-permute-start.4
  4.0 1.4 collective-permute-start.5
  5.4 0.7 fusion.16.hot_ref
  6.1 0.0 copy-start.1
  6.1 0.7 broadcast_multiply_fusion
  6.8 0.8 fusion.20
  7.6 0.0 copy-done
  7.6 0.6 dynamic-slice_bitcast_fusion.flux_ref
  8.2 0.7 copy.24
  8.9 0.0 collective-permute-done.2
  8.9 2.2 %collective-permute-start.6 = (f32[8,512]{1,0:T(8,128)}, f32[8,512]{1,0:T(8,128)S(1)}, u32[]{:S(2)}, u32[]{:S(2)}) collective-permute-start(f32[8,512]{1,0:T(8,128)} %param.10), channel_id=1, source_target_pairs={{0,16},{2,0},{4,48},{6,32},{8,80},{10,64},{12,112},{14,96},{16,18}... | collective-permute-start | bytes 49160 | tf_op jit(solution)/shard_map/ppermute | solution.py:348
  11.2 0.7 broadcast_select_fusion.9
  11.9 0.0 collective-permute-done
  11.9 1.4 collective-permute-start.7
  13.2 0.0 collective-permute-done.1
  13.3 12.7 %collective-permute-start.3 = (f32[32,512]{1,0:T(8,128)S(1)}, f32[32,512]{1,0:T(8,128)S(1)}, u32[]{:S(2)}, u32[]{:S(2)}) collective-permute-start(f32[32,512]{1,0:T(8,128)S(1)} %pad_maximum_fusion.3), channel_id=1, source_target_pairs={{0,8},{2,10},{4,12},{6,14},{8,0},{10,2},{12,4},{14,6},{1,9},{3,11}... | collective-permute-start | bytes 196616 | tf_op jit(solution)/shard_map/ppermute | solution.py:363
  26.0 0.8 constant_dynamic-slice_fusion
  26.8 0.1 reshape.276
  27.0 0.1 copy.25
  27.1 0.1 stack_reshape.3
  27.1 0.0 collective-permute-done.4
  27.2 0.0 collective-permute-done.5
  27.2 0.0 collective-permute-done.6
  27.2 0.0 collective-permute-done.7
  27.3 3.6 %collective-permute-start.8 = (f32[32,512]{1,0:T(8,128)S(1)}, f32[32,512]{1,0:T(8,128)S(1)}, u32[]{:S(2)}, u32[]{:S(2)}) collective-permute-start(f32[32,512]{1,0:T(8,128)S(1)} %pad_maximum_fusion.4), channel_id=1, source_target_pairs={{0,64},{16,80},{32,96},{48,112},{64,0},{80,16},{96,32},{112,48},{1... | collective-permute-start | bytes 196616 | tf_op jit(solution)/shard_map/ppermute | solution.py:364
  30.9 0.7 fusion.1
  31.6 1.4 power_multiply_fusion.basis_ref
  33.0 1.1 pad_maximum_fusion
  34.1 0.0 collective-permute-done.3
  34.1 0.0 collective-permute-done.8
  34.2 0.7 pad_maximum_fusion.2.coef_ref
  34.9 0.6 broadcast_in_dim.6.ids_ref
  35.5 0.0 copy-done.1
  35.5 74.4 %robust_gradient.1 = (f32[64,512]{1,0:T(8,128)}, f32[64,512]{1,0:T(8,128)}) custom-call(f32[32,8]{1,0:T(8,128)} %power_multiply_fusion.basis_ref, s32[8,256]{1,0:T(8,128)} %broadcast_in_dim.6.ids_ref, bf16[16,256]{1,0:T(8,128)(2,1)} %copy-done.1, bf16[256,16]{1,0:T(8,128)(2,1)} %bitcast.23, f32[2,64,512]{2,1,0:T(8,128)} %pad_maximum_fusion.2.coef_ref, ...), custom_call_target="tpu_custom_call" | custom-call | flops 77309411328 | bytes 25165824 | tf_op jit(solution)/shard_map/robust_gradient/pallas_call | solution.py:279
  109.8 1.6 %collective-permute-start.9 = (f32[64,512]{1,0:T(8,128)}, f32[64,512]{1,0:T(8,128)S(1)}, u32[]{:S(2)}, u32[]{:S(2)}) collective-permute-start(f32[64,512]{1,0:T(8,128)} %get-tuple-element.12), channel_id=1, source_target_pairs={{0,0},{2,16},{4,32},{6,48},{8,64},{10,80},{12,96},{14,112},{16,2},... | collective-permute-start | bytes 393224 | tf_op jit(solution)/shard_map/ppermute | solution.py:368
  111.4 0.0 collective-permute-done.9
  111.4 0.9 add_bitcast_fusion
  112.3 26.0 %all_to_all.5 = f32[16,8,512]{2,1,0:T(8,128)S(1)} all-to-all(f32[16,8,512]{2,1,0:T(8,128)S(1)} %bitcast.21), channel_id=1, replica_groups=mesh['row'=8,'col'=8,'chan'=2] {'col','chan'}, dimensions={0} | all-to-all | bytes 524288 | tf_op jit(solution)/shard_map/all_to_all | solution.py:370
  138.3 0.6 reduce_sum.9
  (19 shorter events, 0.2 us)
Async XLA Ops:
  0.0 7.6 %copy-start = (f32[256,64]{0,1:T(8,128)S(1)}, f32[256,64]{0,1:T(8,128)}, u32[]{:S(2)}) copy-start(f32[256,64]{0,1:T(8,128)} %param.13) | copy-start | bytes 196612
  0.0 11.9 %collective-permute-start = (f32[8,512]{1,0:T(8,128)}, f32[8,512]{1,0:T(8,128)S(1)}, u32[]{:S(2)}, u32[]{:S(2)}) collective-permute-start(f32[8,512]{1,0:T(8,128)} %param.10), channel_id=1, source_target_pairs={{0,6},{2,4},{4,2},{6,0},{8,14},{10,12},{12,10},{14,8},{1,7},{3,5},... | collective-permute-start | bytes 49160 | tf_op jit(solution)/shard_map/ppermute | solution.py:346
  3.0 10.2 %collective-permute-start.1 = (f32[8,512]{1,0:T(8,128)}, f32[8,512]{1,0:T(8,128)S(1)}, u32[]{:S(2)}, u32[]{:S(2)}) collective-permute-start(f32[8,512]{1,0:T(8,128)} %param.10), channel_id=1, source_target_pairs={{0,4},{2,6},{4,0},{6,2},{8,12},{10,14},{12,8},{14,10},{1,5},{3,7},... | collective-permute-start | bytes 49160 | tf_op jit(solution)/shard_map/ppermute | solution.py:346
  3.5 5.4 %collective-permute-start.2 = (f32[8,512]{1,0:T(8,128)}, f32[8,512]{1,0:T(8,128)S(1)}, u32[]{:S(2)}, u32[]{:S(2)}) collective-permute-start(f32[8,512]{1,0:T(8,128)} %param.10), channel_id=1, source_target_pairs={{0,2},{2,0},{4,6},{6,4},{8,10},{10,8},{12,14},{14,12},{1,3},{3,1},... | collective-permute-start | bytes 49160 | tf_op jit(solution)/shard_map/ppermute | solution.py:346
  3.7 23.5 %collective-permute-start.4 = (f32[8,512]{1,0:T(8,128)}, f32[8,512]{1,0:T(8,128)S(1)}, u32[]{:S(2)}, u32[]{:S(2)}) collective-permute-start(f32[8,512]{1,0:T(8,128)} %param.10), channel_id=1, source_target_pairs={{0,48},{2,32},{4,16},{6,0},{8,112},{10,96},{12,80},{14,64},{16,50}... | collective-permute-start | bytes 49160 | tf_op jit(solution)/shard_map/ppermute | solution.py:348
  4.0 23.1 %collective-permute-start.5 = (f32[8,512]{1,0:T(8,128)}, f32[8,512]{1,0:T(8,128)S(1)}, u32[]{:S(2)}, u32[]{:S(2)}) collective-permute-start(f32[8,512]{1,0:T(8,128)} %param.10), channel_id=1, source_target_pairs={{0,32},{2,48},{4,0},{6,16},{8,96},{10,112},{12,64},{14,80},{16,34}... | collective-permute-start | bytes 49160 | tf_op jit(solution)/shard_map/ppermute | solution.py:348
  6.1 29.4 %copy-start.1 = (bf16[16,256]{1,0:T(8,128)(2,1)}, bf16[16,256]{1,0:T(8,128)(2,1)S(1)}, u32[]{:S(2)}) copy-start(bf16[16,256]{1,0:T(8,128)(2,1)S(1)} %fusion.16.hot_ref) | copy-start | bytes 24580
  8.9 18.3 %collective-permute-start.6 = (f32[8,512]{1,0:T(8,128)}, f32[8,512]{1,0:T(8,128)S(1)}, u32[]{:S(2)}, u32[]{:S(2)}) collective-permute-start(f32[8,512]{1,0:T(8,128)} %param.10), channel_id=1, source_target_pairs={{0,16},{2,0},{4,48},{6,32},{8,80},{10,64},{12,112},{14,96},{16,18}... | collective-permute-start | bytes 49160 | tf_op jit(solution)/shard_map/ppermute | solution.py:348
  11.9 15.3 %collective-permute-start.7 = (f32[8,512]{1,0:T(8,128)}, f32[8,512]{1,0:T(8,128)S(1)}, u32[]{:S(2)}, u32[]{:S(2)}) collective-permute-start(f32[8,512]{1,0:T(8,128)} %param.10), channel_id=1, source_target_pairs={{0,0},{2,16},{4,32},{6,48},{8,64},{10,80},{12,96},{14,112},{16,2},... | collective-permute-start | bytes 49160 | tf_op jit(solution)/shard_map/ppermute | solution.py:348
  13.3 20.8 %collective-permute-start.3 = (f32[32,512]{1,0:T(8,128)S(1)}, f32[32,512]{1,0:T(8,128)S(1)}, u32[]{:S(2)}, u32[]{:S(2)}) collective-permute-start(f32[32,512]{1,0:T(8,128)S(1)} %pad_maximum_fusion.3), channel_id=1, source_target_pairs={{0,8},{2,10},{4,12},{6,14},{8,0},{10,2},{12,4},{14,6},{1,9},{3,11}... | collective-permute-start | bytes 196616 | tf_op jit(solution)/shard_map/ppermute | solution.py:363
  27.3 6.8 %collective-permute-start.8 = (f32[32,512]{1,0:T(8,128)S(1)}, f32[32,512]{1,0:T(8,128)S(1)}, u32[]{:S(2)}, u32[]{:S(2)}) collective-permute-start(f32[32,512]{1,0:T(8,128)S(1)} %pad_maximum_fusion.4), channel_id=1, source_target_pairs={{0,64},{16,80},{32,96},{48,112},{64,0},{80,16},{96,32},{112,48},{1... | collective-permute-start | bytes 196616 | tf_op jit(solution)/shard_map/ppermute | solution.py:364
  109.8 1.6 %collective-permute-start.9 = (f32[64,512]{1,0:T(8,128)}, f32[64,512]{1,0:T(8,128)S(1)}, u32[]{:S(2)}, u32[]{:S(2)}) collective-permute-start(f32[64,512]{1,0:T(8,128)} %get-tuple-element.12), channel_id=1, source_target_pairs={{0,0},{2,16},{4,32},{6,48},{8,64},{10,80},{12,96},{14,112},{16,2},... | collective-permute-start | bytes 393224 | tf_op jit(solution)/shard_map/ppermute | solution.py:368

commit v7 on v5

--- a/solution.py
+++ b/solution.py
@@ -362,8 +362,8 @@
 
     row_part, col_part = gradient_call(basis, ids, hot, coef, flux, begin, turn, vis, flag)
     part = row_part + lax.ppermute(col_part, ("row", "col"), CROSS)
-    part = jnp.broadcast_to(part.reshape(8, 1, 8, 512), (8, 2, 8, 512)).reshape(16, 8, 512)
-    return lax.all_to_all(part, ("col", "chan"), 0, 0, tiled=True).sum(0)
+    total = lax.all_to_all(part, "col", 0, 0, tiled=True).reshape(8, 8, 512).sum(0)
+    return total + lax.ppermute(total, "chan", [(0, 1), (1, 0)])
 
 
 def solution(mesh):

time: 134 us -> 135 us (level)
  blocking collectives: 28 us -> 23 us
  starting transfers between devices: 16 us -> 19.9 us
  waiting for transfers between devices: 4.07 us -> 5.78 us
    all_to_all x1, blocking collectives: 28 us -> 23 us  [per_device(): lax.all_to_all(part, 'col', 0, 0, tiled=True).reshape(8, 8, 512).sum(0)]
    ppermute x0 -> x1, starting transfers between devices: none -> 3.97 us  [per_device(): return total + lax.ppermute(total, 'chan', [(0, 1), (1, 0)])]
    ppermute x0 -> x1, waiting for transfers between devices: none -> 1.72 us  [per_device(): return total + lax.ppermute(total, 'chan', [(0, 1), (1, 0)])]
  transfers between devices with their start and end apart: 8 -> 9, of which waited for: 2 -> 3; matrix products, arithmetic and copies ran while one was open for 6% -> 6% of each run, Pallas kernels for 0% -> 0%
where the time goes in v7:
time: 135 us
  Pallas kernels  74.4 us (55%)
  blocking collectives  23 us (17%)
  starting transfers between devices  19.9 us (15%)
  other arithmetic  7.69 us (6%)
  waiting for transfers between devices  5.78 us (4%)
  local copies, waits for them, and re-layouts  3.84 us (3%)
    pallas_call x1, Pallas kernels, gradient_call(): pl.pallas_call(kernel, grid=(chans // 2,), in_specs=[pl.BlockSpec(memory_...  74.4 us
    all_to_all x1, blocking collectives, per_device(): lax.all_to_all(part, 'col', 0, 0, tiled=True).reshape(8, 8, 512).sum(0)  23 us
    ppermute x3, starting transfers between devices, per_device(): lax.ppermute(row_coef, 'col', [(c, c ^ bit) for c in range(8)])  9.73 us
    ppermute x1, starting transfers between devices, per_device(): return total + lax.ppermute(total, 'chan', [(0, 1), (1, 0)])  3.97 us
    ppermute x3, waiting for transfers between devices, per_device(): lax.ppermute(col_coef, 'row', [(r, r ^ bit) for r in range(8)])  3.45 us
    ppermute x3, starting transfers between devices, per_device(): lax.ppermute(col_coef, 'row', [(r, r ^ bit) for r in range(8)])  3.14 us
  transfers between devices with their start and end apart: 9, of which 3 were waited for; matrix products, arithmetic and copies ran while one was open for 6% of the time, Pallas kernels for 0%

profile of v7, /device:TPU:0, one launch (start us, length us, event | category | flops | bytes accessed | tf_op | source)
XLA Modules:
  0.0 134.7 jit_solution(8104142118913602696)
XLA Ops:
  0.0 0.0 copy-start
  0.0 1.5 %collective-permute-start = (f32[8,512]{1,0:T(8,128)}, f32[8,512]{1,0:T(8,128)S(1)}, u32[]{:S(2)}, u32[]{:S(2)}) collective-permute-start(f32[8,512]{1,0:T(8,128)} %param.10), channel_id=1, source_target_pairs={{0,0},{2,16},{4,32},{6,48},{8,64},{10,80},{12,96},{14,112},{16,2},... | collective-permute-start | bytes 49160 | tf_op jit(solution)/shard_map/ppermute | solution.py:347
  1.5 2.6 %collective-permute-start.1 = (f32[8,512]{1,0:T(8,128)}, f32[8,512]{1,0:T(8,128)S(1)}, u32[]{:S(2)}, u32[]{:S(2)}) collective-permute-start(f32[8,512]{1,0:T(8,128)} %param.10), channel_id=1, source_target_pairs={{0,2},{2,0},{4,6},{6,4},{8,10},{10,8},{12,14},{14,12},{1,3},{3,1},... | collective-permute-start | bytes 49160 | tf_op jit(solution)/shard_map/ppermute | solution.py:359
  4.1 0.7 fusion.12.hot_ref
  4.8 0.0 copy-start.1
  4.8 0.7 broadcast_multiply_fusion
  5.5 0.8 fusion.16
  6.3 0.0 copy-done
  6.3 0.6 dynamic-slice_bitcast_fusion.flux_ref
  6.9 0.7 copy.20
  7.6 0.0 collective-permute-done
  7.7 0.8 constant_dynamic-slice_fusion
  8.5 0.1 reshape.275
  8.6 0.1 copy.21
  8.7 0.1 stack_reshape.3
  8.8 0.0 collective-permute-done.1
  8.8 0.7 broadcast_select_fusion.11
  9.6 1.9 %collective-permute-start.2 = (f32[16,512]{1,0:T(8,128)S(1)}, f32[16,512]{1,0:T(8,128)S(1)}, u32[]{:S(2)}, u32[]{:S(2)}) collective-permute-start(f32[16,512]{1,0:T(8,128)S(1)} %pad_maximum_fusion.5), channel_id=1, source_target_pairs={{0,4},{2,6},{4,0},{6,2},{8,12},{10,14},{12,8},{14,10},{1,5},{3,7},... | collective-permute-start | bytes 98312 | tf_op jit(solution)/shard_map/ppermute | solution.py:359
  11.4 0.7 fusion.1
  12.2 1.4 %power_multiply_fusion.basis_ref = f32[32,8]{1,0:T(8,128)} fusion(f32[8]{0:T(128)} %constant.83.clone, f32[8]{0:T(128)S(1)} %broadcast_subtract_fusion, f32[32]{0:T(128)S(1)} %get-tuple-element.36, f32[8]{0:T(128)S(1)} %iota_convert_fusion, f32[32]{0:T(128)S(1)} %get-tuple-element.35), kind=kLoop, calls=%fused_computation.47 | loop fusion | flops 512 | bytes 1376 | tf_op jit(solution)/shard_map/mul | solution.py:32
  13.6 0.3 collective-permute-start.4
  13.9 1.1 pad_maximum_fusion
  15.0 0.0 collective-permute-done.4
  15.0 1.0 collective-permute-start.5
  16.0 0.0 collective-permute-done.2
  16.1 5.2 %collective-permute-start.3 = (f32[32,512]{1,0:T(8,128)S(1)}, f32[32,512]{1,0:T(8,128)S(1)}, u32[]{:S(2)}, u32[]{:S(2)}) collective-permute-start(f32[32,512]{1,0:T(8,128)S(1)} %pad_maximum_fusion.3), channel_id=1, source_target_pairs={{0,8},{2,10},{4,12},{6,14},{8,0},{10,2},{12,4},{14,6},{1,9},{3,11}... | collective-permute-start | bytes 196616 | tf_op jit(solution)/shard_map/ppermute | solution.py:359
  21.3 0.0 collective-permute-done.5
  21.3 1.8 %collective-permute-start.6 = (f32[32,512]{1,0:T(8,128)S(1)}, f32[32,512]{1,0:T(8,128)S(1)}, u32[]{:S(2)}, u32[]{:S(2)}) collective-permute-start(f32[32,512]{1,0:T(8,128)S(1)} %pad_maximum_fusion.4), channel_id=1, source_target_pairs={{0,64},{16,80},{32,96},{48,112},{64,0},{80,16},{96,32},{112,48},{1... | collective-permute-start | bytes 196616 | tf_op jit(solution)/shard_map/ppermute | solution.py:360
  23.1 0.6 collective-permute-done.3
  23.7 3.4 %collective-permute-done.6 = f32[32,512]{1,0:T(8,128)S(1)} collective-permute-done((f32[32,512]{1,0:T(8,128)S(1)}, f32[32,512]{1,0:T(8,128)S(1)}, u32[]{:S(2)}, u32[]{:S(2)}) %collective-permute-start.6) | collective-permute-done | bytes 65568 | tf_op jit(solution)/shard_map/ppermute | solution.py:360
  27.2 0.7 pad_maximum_fusion.2.coef_ref
  27.9 0.6 broadcast_in_dim.2.ids_ref
  28.5 0.0 copy-done.1
  28.5 74.4 %robust_gradient.1 = (f32[64,512]{1,0:T(8,128)}, f32[64,512]{1,0:T(8,128)}) custom-call(f32[32,8]{1,0:T(8,128)} %power_multiply_fusion.basis_ref, s32[8,256]{1,0:T(8,128)} %broadcast_in_dim.2.ids_ref, bf16[16,256]{1,0:T(8,128)(2,1)} %copy-done.1, bf16[256,16]{1,0:T(8,128)(2,1)} %bitcast.21, f32[2,64,512]{2,1,0:T(8,128)} %pad_maximum_fusion.2.coef_ref, ...), custom_call_target="tpu_custom_call" | custom-call | flops 77309411328 | bytes 25165824 | tf_op jit(solution)/shard_map/robust_gradient/pallas_call | solution.py:279
  102.9 1.6 %collective-permute-start.7 = (f32[64,512]{1,0:T(8,128)}, f32[64,512]{1,0:T(8,128)S(1)}, u32[]{:S(2)}, u32[]{:S(2)}) collective-permute-start(f32[64,512]{1,0:T(8,128)} %get-tuple-element.12), channel_id=1, source_target_pairs={{0,0},{2,16},{4,32},{6,48},{8,64},{10,80},{12,96},{14,112},{16,2},... | collective-permute-start | bytes 393224 | tf_op jit(solution)/shard_map/ppermute | solution.py:364
  104.4 0.0 collective-permute-done.7
  104.4 0.9 add_bitcast_fusion
  105.4 23.0 %all_to_all.9 = f32[8,8,512]{2,1,0:T(8,128)S(1)} all-to-all(f32[8,8,512]{2,1,0:T(8,128)S(1)} %add_bitcast_fusion), channel_id=1, replica_groups=mesh['row'=8,'col'=8,'chan'=2] {'col'}, dimensions={0} | all-to-all | bytes 262144 | tf_op jit(solution)/shard_map/all_to_all | solution.py:365
  128.4 4.0 %collective-permute-start.8 = (f32[8,512]{1,0:T(8,128)S(1)}, f32[8,512]{1,0:T(8,128)S(1)}, u32[]{:S(2)}, u32[]{:S(2)}) collective-permute-start(f32[8,512]{1,0:T(8,128)S(1)} %reduce_sum.9), channel_id=1, source_target_pairs={{0,1},{1,0},{2,3},{3,2},{4,5},{5,4},{6,7},{7,6},{8,9},{9,8},{10,11... | collective-permute-start | bytes 49160 | tf_op jit(solution)/shard_map/ppermute | solution.py:366
  132.4 1.7 %collective-permute-done.8 = f32[8,512]{1,0:T(8,128)S(1)} collective-permute-done((f32[8,512]{1,0:T(8,128)S(1)}, f32[8,512]{1,0:T(8,128)S(1)}, u32[]{:S(2)}, u32[]{:S(2)}) %collective-permute-start.8) | collective-permute-done | bytes 16416 | tf_op jit(solution)/shard_map/ppermute | solution.py:366
  134.1 0.6 add.444
  (19 shorter events, 0.1 us)
Async XLA Ops:
  0.0 6.3 %copy-start = (f32[256,64]{0,1:T(8,128)S(1)}, f32[256,64]{0,1:T(8,128)}, u32[]{:S(2)}) copy-start(f32[256,64]{0,1:T(8,128)} %param.13) | copy-start | bytes 196612
  0.0 7.6 %collective-permute-start = (f32[8,512]{1,0:T(8,128)}, f32[8,512]{1,0:T(8,128)S(1)}, u32[]{:S(2)}, u32[]{:S(2)}) collective-permute-start(f32[8,512]{1,0:T(8,128)} %param.10), channel_id=1, source_target_pairs={{0,0},{2,16},{4,32},{6,48},{8,64},{10,80},{12,96},{14,112},{16,2},... | collective-permute-start | bytes 49160 | tf_op jit(solution)/shard_map/ppermute | solution.py:347
  1.5 7.3 %collective-permute-start.1 = (f32[8,512]{1,0:T(8,128)}, f32[8,512]{1,0:T(8,128)S(1)}, u32[]{:S(2)}, u32[]{:S(2)}) collective-permute-start(f32[8,512]{1,0:T(8,128)} %param.10), channel_id=1, source_target_pairs={{0,2},{2,0},{4,6},{6,4},{8,10},{10,8},{12,14},{14,12},{1,3},{3,1},... | collective-permute-start | bytes 49160 | tf_op jit(solution)/shard_map/ppermute | solution.py:359
  4.8 23.7 %copy-start.1 = (bf16[16,256]{1,0:T(8,128)(2,1)}, bf16[16,256]{1,0:T(8,128)(2,1)S(1)}, u32[]{:S(2)}) copy-start(bf16[16,256]{1,0:T(8,128)(2,1)S(1)} %fusion.12.hot_ref) | copy-start | bytes 24580
  9.6 6.5 %collective-permute-start.2 = (f32[16,512]{1,0:T(8,128)S(1)}, f32[16,512]{1,0:T(8,128)S(1)}, u32[]{:S(2)}, u32[]{:S(2)}) collective-permute-start(f32[16,512]{1,0:T(8,128)S(1)} %pad_maximum_fusion.5), channel_id=1, source_target_pairs={{0,4},{2,6},{4,0},{6,2},{8,12},{10,14},{12,8},{14,10},{1,5},{3,7},... | collective-permute-start | bytes 98312 | tf_op jit(solution)/shard_map/ppermute | solution.py:359
  13.6 1.4 %collective-permute-start.4 = (f32[8,512]{1,0:T(8,128)S(1)}, f32[8,512]{1,0:T(8,128)S(1)}, u32[]{:S(2)}, u32[]{:S(2)}) collective-permute-start(f32[8,512]{1,0:T(8,128)S(1)} %collective-permute-done), channel_id=1, source_target_pairs={{0,16},{16,0},{32,48},{48,32},{64,80},{80,64},{96,112},{112,96},{1... | collective-permute-start | bytes 49160 | tf_op jit(solution)/shard_map/ppermute | solution.py:360
  15.0 6.3 %collective-permute-start.5 = (f32[16,512]{1,0:T(8,128)S(1)}, f32[16,512]{1,0:T(8,128)S(1)}, u32[]{:S(2)}, u32[]{:S(2)}) collective-permute-start(f32[16,512]{1,0:T(8,128)S(1)} %pad_maximum_fusion.6), channel_id=1, source_target_pairs={{0,32},{16,48},{32,0},{48,16},{64,96},{80,112},{96,64},{112,80},{1... | collective-permute-start | bytes 98312 | tf_op jit(solution)/shard_map/ppermute | solution.py:360
  16.1 7.7 %collective-permute-start.3 = (f32[32,512]{1,0:T(8,128)S(1)}, f32[32,512]{1,0:T(8,128)S(1)}, u32[]{:S(2)}, u32[]{:S(2)}) collective-permute-start(f32[32,512]{1,0:T(8,128)S(1)} %pad_maximum_fusion.3), channel_id=1, source_target_pairs={{0,8},{2,10},{4,12},{6,14},{8,0},{10,2},{12,4},{14,6},{1,9},{3,11}... | collective-permute-start | bytes 196616 | tf_op jit(solution)/shard_map/ppermute | solution.py:359
  21.3 5.8 %collective-permute-start.6 = (f32[32,512]{1,0:T(8,128)S(1)}, f32[32,512]{1,0:T(8,128)S(1)}, u32[]{:S(2)}, u32[]{:S(2)}) collective-permute-start(f32[32,512]{1,0:T(8,128)S(1)} %pad_maximum_fusion.4), channel_id=1, source_target_pairs={{0,64},{16,80},{32,96},{48,112},{64,0},{80,16},{96,32},{112,48},{1... | collective-permute-start | bytes 196616 | tf_op jit(solution)/shard_map/ppermute | solution.py:360
  102.9 1.6 %collective-permute-start.7 = (f32[64,512]{1,0:T(8,128)}, f32[64,512]{1,0:T(8,128)S(1)}, u32[]{:S(2)}, u32[]{:S(2)}) collective-permute-start(f32[64,512]{1,0:T(8,128)} %get-tuple-element.12), channel_id=1, source_target_pairs={{0,0},{2,16},{4,32},{6,48},{8,64},{10,80},{12,96},{14,112},{16,2},... | collective-permute-start | bytes 393224 | tf_op jit(solution)/shard_map/ppermute | solution.py:364
  128.4 5.7 %collective-permute-start.8 = (f32[8,512]{1,0:T(8,128)S(1)}, f32[8,512]{1,0:T(8,128)S(1)}, u32[]{:S(2)}, u32[]{:S(2)}) collective-permute-start(f32[8,512]{1,0:T(8,128)S(1)} %reduce_sum.9), channel_id=1, source_target_pairs={{0,1},{1,0},{2,3},{3,2},{4,5},{5,4},{6,7},{7,6},{8,9},{9,8},{10,11... | collective-permute-start | bytes 49160 | tf_op jit(solution)/shard_map/ppermute | solution.py:366
